TPU v7x, 256 devices: a whole 4x4x8 slice. The times are simulated.
256 devices in a mesh: shot: 8 (over y, x_hi), gx: 4 (over x_lo, core), gy: 8 (over z).
Axes of the slice: x: 4 (x_hi: 2, x_lo: 2; x = x_hi * 2 + x_lo), y: 4, z: 8, core: 2. Of those that a mesh axis runs over, the one named last changes fastest.
Arguments:
- speed_squared: float32 [192, 64, 256], P('gx', 'gy'), may hold values from 0.04 to 0.12
- epsilon_term: float32 [192, 64, 256], P('gx', 'gy'), may hold values from 1 to 1.5
- delta_term: float32 [192, 64, 256], P('gx', 'gy'), may hold values from 0.9 to 1.2
- tilt_term: float32 [192, 64, 256], P('gx', 'gy'), may hold values from -0.1 to 0.1
- perturbation: float32 [3, 192, 64, 256], P(None, 'gx', 'gy', 'shot'), may hold values from -6 to 6
- forward_prev: float32 [8, 192, 64, 256], P('shot', 'gx', 'gy'), may hold values from -1.8 to 1.8
- forward_now: float32 [8, 192, 64, 256], P('shot', 'gx', 'gy'), may hold values from -1.8 to 1.8
- adjoint_prev: float32 [8, 192, 64, 256], P('shot', 'gx', 'gy'), may hold values from -1.8 to 1.8
- adjoint_now: float32 [8, 192, 64, 256], P('shot', 'gx', 'gy'), may hold values from -1.8 to 1.8
- wavelet: float32 [8, 2], P('shot'), may hold values from 0.5 to 2
- source_cell: int32 [8], P('shot'), may hold values from 0 to 255
- receiver_cells: int32 [8, 1536], P('shot'), may hold values from 0 to 3145727
Outputs:
- hessian_product: float32 [3, 192, 64, 256], P(None, 'gx', 'gy', 'shot')
Inputs may be any that keep to these rules, and one draw needn't show every extreme that they name: `source_cell`: the depth index z of the group's horizontal plane source. `receiver_cells`: flattened cell indices x * 64 * 256 + y * 256 + z; several receivers may share a cell.
All inputs are finite; a program needn't handle non-finite values.
Results may differ from a plain program's by a relative error of at most 0.00002.
Values sent between devices are 32-bit elements; how exact they have to be, the bound alone decides.
No kernel may reach another device: no remote copies, remote signals or barrier semaphores. Data moves between devices by JAX's collectives and lax.ppermute only.
A program may use at most 192 MiB of HBM per device.

v0:
```python
import jax
import jax.numpy as jnp
from jax import lax
from jax.sharding import PartitionSpec as P

second_weights = (-1.0 / 12.0, 4.0 / 3.0, -2.5, 4.0 / 3.0, -1.0 / 12.0)
first_weights = (1.0 / 12.0, -2.0 / 3.0, 0.0, 2.0 / 3.0, -1.0 / 12.0)


def with_halo(shard, sides, width):
    for axis, dim in sides:
        size, length = (lax.axis_size(axis), shard.shape[dim])
        up = [(i, (i + 1) % size) for i in range(size - 1)]
        down = [(j, i) for i, j in up]
        last = lax.slice_in_dim(shard, length - width, length, axis=dim)
        first = lax.slice_in_dim(shard, 0, width, axis=dim)
        before = lax.ppermute(last, axis, up)
        after = lax.ppermute(first, axis, down)
        shard = jnp.concatenate([before, shard, after], axis=dim)
    return shard


def derivs(padded):
    size_x = padded.shape[0] - 4
    size_y = padded.shape[1] - 4
    size_z = padded.shape[2]
    padded_z = jnp.pad(padded, ((0, 0), (0, 0), (2, 2)))
    horizontal = 0.0
    vertical = 0.0
    vertical_slope = 0.0
    for offset in range(5):
        horizontal = horizontal + second_weights[offset] * (
            padded_z[offset : offset + size_x, 2 : 2 + size_y, 2 : 2 + size_z]
            + padded_z[2 : 2 + size_x, offset : offset + size_y, 2 : 2 + size_z]
        )
        vertical = (
            vertical
            + second_weights[offset]
            * padded_z[2 : 2 + size_x, 2 : 2 + size_y, offset : offset + size_z]
        )
        vertical_slope = (
            vertical_slope + first_weights[offset] * padded_z[:, :, offset : offset + size_z]
        )
    mixed_term = 0.0
    for offset in range(5):
        mixed_term = mixed_term + first_weights[offset] * (
            vertical_slope[offset : offset + size_x, 2 : 2 + size_y]
            + vertical_slope[2 : 2 + size_x, offset : offset + size_y]
        )
    return (horizontal, vertical, mixed_term)


def operate(parts, speed, epsilon, delta, tilt):
    return speed * (epsilon * parts[0] + delta * parts[1]) + tilt * parts[2]


def born_source(parts, speed, epsilon, delta, change):
    return change[0] * (epsilon * parts[0] + delta * parts[1]) + speed * (
        change[1] * parts[0] + change[2] * parts[1]
    )


def imaging(parts, speed, epsilon, delta):
    return jnp.stack([epsilon * parts[0] + delta * parts[1], speed * parts[0], speed * parts[1]])


def per_device(
    speed_squared,
    epsilon_term,
    delta_term,
    tilt_term,
    perturbation,
    forward_prev,
    forward_now,
    adjoint_prev,
    adjoint_now,
    wavelet,
    source_cell,
    receiver_cells,
):
    own_x, own_y, depth = speed_squared.shape
    levels = wavelet.shape[1]
    change = lax.all_gather(perturbation, "shot", axis=3, tiled=True)
    margin = 0
    fields = (
        speed_squared,
        epsilon_term,
        delta_term,
        tilt_term,
        change[0],
        change[1],
        change[2],
        forward_prev[0],
        forward_now[0],
        adjoint_prev[0],
        adjoint_now[0],
    )

    def widen(field):
        return with_halo(field, (("gx", 0), ("gy", 1)), 2)

    speed, epsilon, delta, tilt = (fields[0], fields[1], fields[2], fields[3])
    model_change = (fields[4], fields[5], fields[6])
    u_prev, u_curr, l_prev, l_curr = (fields[7], fields[8], fields[9], fields[10])
    ext_x = own_x + 2 * margin
    ext_y = own_y + 2 * margin
    start_x = lax.axis_index("gx") * own_x - margin
    start_y = lax.axis_index("gy") * own_y - margin
    whole_x = own_x * lax.axis_size("gx")
    whole_y = own_y * lax.axis_size("gy")
    cells = receiver_cells[0]
    cell_x = cells // (whole_y * depth) - start_x
    cell_y = cells // depth % whole_y - start_y
    cell_z = cells % depth
    inside = (cell_x >= 0) & (cell_x < ext_x) & (cell_y >= 0) & (cell_y < ext_y)
    rec_x = jnp.where(inside, cell_x, ext_x)
    rec_y = jnp.where(inside, cell_y, ext_y)
    counts = (
        jnp.zeros((ext_x, ext_y, depth), jnp.float32).at[rec_x, rec_y, cell_z].add(1.0, mode="drop")
    )
    lateral_x = start_x + lax.iota(jnp.int32, ext_x)
    lateral_y = start_y + lax.iota(jnp.int32, ext_y)
    inside_x = (lateral_x >= 0) & (lateral_x < whole_x)
    inside_y = (lateral_y >= 0) & (lateral_y < whole_y)
    at_depth = lax.iota(jnp.int32, depth) == source_cell[0]
    source_plane = jnp.where(
        inside_x[:, None, None] & inside_y[None, :, None] & at_depth[None, None, :], 1.0, 0.0
    ).astype(jnp.float32)
    speed_own, epsilon_own, delta_own = (speed, epsilon, delta)
    parts_u = derivs(widen(u_curr))
    parts_b = None
    b_curr = None
    d_curr = None
    result = 0.0
    for level in range(levels):
        parts_l = derivs(widen(l_curr))
        u_next = 2.0 * u_curr - u_prev + operate(parts_u, speed, epsilon, delta, tilt)
        u_next = u_next + wavelet[0, level] * source_plane
        b_next = born_source(parts_u, speed, epsilon, delta, model_change)
        l_next = 2.0 * l_curr - l_prev + operate(parts_l, speed, epsilon, delta, tilt)
        d_next = born_source(parts_l, speed, epsilon, delta, model_change)
        if b_curr is not None:
            parts_d = derivs(widen(d_curr))
            b_next = b_next + 2.0 * b_curr + operate(parts_b, speed, epsilon, delta, tilt)
            d_next = (
                d_next
                + 2.0 * d_curr
                + operate(parts_d, speed, epsilon, delta, tilt)
                + counts * b_curr
            )
        parts_u = derivs(widen(u_next))
        parts_b = derivs(widen(b_next))
        cropped_u = tuple((piece for piece in parts_u))
        cropped_b = tuple((piece for piece in parts_b))
        term = (
            imaging(cropped_u, speed_own, epsilon_own, delta_own) * d_next
            + imaging(cropped_b, speed_own, epsilon_own, delta_own) * l_next
        )
        result = result + term
        u_prev, u_curr = (u_curr, u_next)
        b_curr = b_next
        l_prev, l_curr = (l_curr, l_next)
        d_curr = d_next
    return lax.psum_scatter(result, "shot", scatter_dimension=3, tiled=True)


def solution(mesh):
    placed = (
        P("gx", "gy", None),
        P("gx", "gy", None),
        P("gx", "gy", None),
        P("gx", "gy", None),
        P(None, "gx", "gy", "shot"),
        P("shot", "gx", "gy", None),
        P("shot", "gx", "gy", None),
        P("shot", "gx", "gy", None),
        P("shot", "gx", "gy", None),
        P("shot", None),
        P("shot"),
        P("shot", None),
    )
    return jax.shard_map(
        per_device,
        mesh=mesh,
        in_specs=placed,
        out_specs=P(None, "gx", "gy", "shot"),
        check_vma=False,
    )
```

profile of v0, /device:TPU:32, one launch (start us, length us, event | category | flops | bytes accessed | tf_op | source)
XLA Modules:
  0.0 293.8 jit_solution(8325317234936071203)
XLA Ops:
  7.3 1.7 collective-permute-start.8
  9.1 1.4 collective-permute-start.9
  10.5 2.0 copy.63
  13.3 4.3 %collective-permute-start = (f32[2,8,256]{2,1,0:T(8,128)S(1)}, f32[2,8,256]{2,1,0:T(8,128)S(1)}, u32[]{:S(2)}, u32[]{:S(2)}) collective-permute-start(f32[2,8,256]{2,1,0:T(8,128)S(1)} %get-tuple-element.66), channel_id=1, source_target_pairs={{0,8},{8,16},{16,24},{1,9},{9,17},{17,25},{2,10},{10,18},{18,26},{... | collective-permute-start | bytes 49160 | tf_op jit(solution)/shard_map/ppermute | solution.py:17
  17.6 1.3 collective-permute-start.1
  21.8 8.7 %scatter_custom_fusion = f32[98304]{0:T(1024)S(1)} fusion(s32[1536]{0:T(1024)S(1)} %broadcast_select_fusion, f32[1536]{0:T(1024)S(1)} %broadcast.487, f32[]{:T(128)} %constant.78.clone.1), kind=kCustom, calls=%fused_computation.547 | custom fusion | flops 1536 | bytes 393220
  31.5 3.8 %collective-permute-start.10 = (f32[52,2,256]{2,1,0:T(2,128)S(1)}, f32[52,2,256]{2,1,0:T(2,128)S(1)}, u32[]{:S(2)}, u32[]{:S(2)}) collective-permute-start(f32[52,2,256]{2,1,0:T(2,128)S(1)} %get-tuple-element.47), channel_id=1, source_target_pairs={{0,1},{1,2},{2,3},{3,4},{4,5},{5,6},{6,7},{8,9},{9,10},{10,11},{11... | collective-permute-start | bytes 319496 | tf_op jit(solution)/shard_map/ppermute | solution.py:17
  35.3 2.0 collective-permute-start.11
  37.4 3.8 %collective-permute-start.2 = (f32[52,2,256]{2,1,0:T(2,128)S(1)}, f32[52,2,256]{2,1,0:T(2,128)S(1)}, u32[]{:S(2)}, u32[]{:S(2)}) collective-permute-start(f32[52,2,256]{2,1,0:T(2,128)S(1)} %get-tuple-element.41), channel_id=1, source_target_pairs={{0,1},{1,2},{2,3},{3,4},{4,5},{5,6},{6,7},{8,9},{9,10},{10,11},{11... | collective-permute-start | bytes 319496 | tf_op jit(solution)/shard_map/ppermute | solution.py:17
  41.3 2.0 collective-permute-start.3
  44.2 4.7 %collective-permute-done.3 = f32[52,2,256]{2,1,0:T(2,128)S(1)} collective-permute-done((f32[52,2,256]{2,1,0:T(2,128)S(1)}, f32[52,2,256]{2,1,0:T(2,128)S(1)}, u32[]{:S(2)}, u32[]{:S(2)}) %collective-permute-start.3) | collective-permute-done | bytes 106528 | tf_op jit(solution)/shard_map/ppermute | solution.py:18
  51.0 34.3 %all-gather.2.cloned.1.call-done = f32[3,48,8,256]{1,2,0,3:T(8,128)} async-done(((f32[3,48,8,32]{1,2,0,3:T(8,128)}), f32[3,48,8,256]{1,2,0,3:T(8,128)}) %all-gather.2.cloned.1.call-update) | async-done | bytes 1179664 | tf_op jit(solution)/shard_map/all_gather | solution.py:83
  85.3 3.4 %fusion.333 = (f32[1,48,8,256]{1,2,0,3:T(8,128)S(1)}, f32[1,48,8,256]{1,2,0,3:T(8,128)}, f32[1,48,8,256]{1,2,0,3:T(8,128)}) fusion(f32[3,48,8,256]{1,2,0,3:T(8,128)} %all-gather.2.cloned.1.call-done), kind=kLoop, calls=%fused_computation.605 | loop fusion | bytes 2359296 | tf_op jit(solution)/shard_map/slice | solution.py:90
  89.8 2.4 copy.70
  92.2 2.3 copy.71
  94.6 5.9 %fusion.301 = (f32[48,8,256]{2,1,0:T(8,128)S(1)}, f32[48,8,256]{2,1,0:T(8,128)S(1)}, f32[48,8,256]{2,1,0:T(8,128)S(1)}) fusion(f32[48,8,256]{2,1,0:T(8,128)S(1)} %copy-done.2, f32[1,48,8,256]{3,2,1,0:T(8,128)} %copy.71, f32[1,48,8,256]{3,2,1,0:T(8,128)} %copy.70, f32[1,48,8,256]{3,2,1,0:T(8,128)} %copy.69, f32[48,8,256]{2,1,0:T(8,128)S(1)} %copy-done, ...), kind=kLoop, calls=%fused_computation.511 | loop fusion | flops 4718592 | bytes 5210112 | tf_op jit(solution)/shard_map/add | solution.py:58
  100.5 1.3 collective-permute-start.24
  101.8 1.3 collective-permute-start.25
  103.6 3.8 %collective-permute-start.20 = (f32[2,8,256]{2,1,0:T(8,128)S(1)}, f32[2,8,256]{2,1,0:T(8,128)S(1)}, u32[]{:S(2)}, u32[]{:S(2)}) collective-permute-start(f32[2,8,256]{2,1,0:T(8,128)S(1)} %get-tuple-element.68), channel_id=1, source_target_pairs={{0,8},{8,16},{16,24},{1,9},{9,17},{17,25},{2,10},{10,18},{18,26},{... | collective-permute-start | bytes 49160 | tf_op jit(solution)/shard_map/ppermute | solution.py:17
  107.4 1.3 collective-permute-start.21
  108.8 3.5 %collective-permute-start.26 = (f32[52,2,256]{2,1,0:T(2,128)S(1)}, f32[52,2,256]{2,1,0:T(2,128)S(1)}, u32[]{:S(2)}, u32[]{:S(2)}) collective-permute-start(f32[52,2,256]{2,1,0:T(2,128)S(1)} %get-tuple-element.45), channel_id=1, source_target_pairs={{0,1},{1,2},{2,3},{3,4},{4,5},{5,6},{6,7},{8,9},{9,10},{10,11},{11... | collective-permute-start | bytes 319496 | tf_op jit(solution)/shard_map/ppermute | solution.py:17
  112.3 2.4 collective-permute-start.27
  114.8 3.5 %collective-permute-start.22 = (f32[52,2,256]{2,1,0:T(2,128)S(1)}, f32[52,2,256]{2,1,0:T(2,128)S(1)}, u32[]{:S(2)}, u32[]{:S(2)}) collective-permute-start(f32[52,2,256]{2,1,0:T(2,128)S(1)} %get-tuple-element.43), channel_id=1, source_target_pairs={{0,1},{1,2},{2,3},{3,4},{4,5},{5,6},{6,7},{8,9},{9,10},{10,11},{11... | collective-permute-start | bytes 319496 | tf_op jit(solution)/shard_map/ppermute | solution.py:17
  118.2 2.6 collective-permute-start.23
  122.0 3.1 %collective-permute-done.23 = f32[52,2,256]{2,1,0:T(2,128)S(1)} collective-permute-done((f32[52,2,256]{2,1,0:T(2,128)S(1)}, f32[52,2,256]{2,1,0:T(2,128)S(1)}, u32[]{:S(2)}, u32[]{:S(2)}) %collective-permute-start.23) | collective-permute-done | bytes 106528 | tf_op jit(solution)/shard_map/ppermute | solution.py:18
  126.3 4.1 %fusion.72 = (f32[48,8,256]{2,1,0:T(8,128)S(1)}, f32[48,8,256]{2,1,0:T(8,128)S(1)}, f32[48,8,256]{2,1,0:T(8,128)S(1)}, f32[48,8,256]{2,1,0:T(8,128)S(1)}, f32[48,8,256]{2,1,0:T(8,128)S(1)}) fusion(f32[48,8,256]{2,1,0:T(8,128)S(1)} %copy-done.2, f32[48,8,256]{2,1,0:T(8,128)S(1)} %copy-done.1, f32[48,8,256]{2,1,0:T(8,128)S(1)} %get-tuple-element.14, ...), kind=kLoop, calls=%fused_computation.175 | loop fusion | flops 15728640 | bytes 12877824 | tf_op jit(solution)/shard_map/add | solution.py:146
  130.4 2.9 collective-permute-start.12
  133.3 1.3 collective-permute-start.13
  135.8 5.7 %collective-permute-start.4 = (f32[2,8,256]{2,1,0:T(8,128)S(1)}, f32[2,8,256]{2,1,0:T(8,128)S(1)}, u32[]{:S(2)}, u32[]{:S(2)}) collective-permute-start(f32[2,8,256]{2,1,0:T(8,128)S(1)} %get-tuple-element.62), channel_id=1, source_target_pairs={{0,8},{8,16},{16,24},{1,9},{9,17},{17,25},{2,10},{10,18},{18,26},{... | collective-permute-start | bytes 49160 | tf_op jit(solution)/shard_map/ppermute | solution.py:17
  141.4 1.3 collective-permute-start.5
  142.8 5.1 %collective-permute-start.14 = (f32[52,2,256]{2,1,0:T(2,128)S(1)}, f32[52,2,256]{2,1,0:T(2,128)S(1)}, u32[]{:S(2)}, u32[]{:S(2)}) collective-permute-start(f32[52,2,256]{2,1,0:T(2,128)S(1)} %get-tuple-element.39), channel_id=1, source_target_pairs={{0,1},{1,2},{2,3},{3,4},{4,5},{5,6},{6,7},{8,9},{9,10},{10,11},{11... | collective-permute-start | bytes 319496 | tf_op jit(solution)/shard_map/ppermute | solution.py:17
  148.0 1.9 collective-permute-start.15
  150.0 5.1 %collective-permute-start.6 = (f32[52,2,256]{2,1,0:T(2,128)S(1)}, f32[52,2,256]{2,1,0:T(2,128)S(1)}, u32[]{:S(2)}, u32[]{:S(2)}) collective-permute-start(f32[52,2,256]{2,1,0:T(2,128)S(1)} %get-tuple-element.37), channel_id=1, source_target_pairs={{0,1},{1,2},{2,3},{3,4},{4,5},{5,6},{6,7},{8,9},{9,10},{10,11},{11... | collective-permute-start | bytes 319496 | tf_op jit(solution)/shard_map/ppermute | solution.py:17
  155.2 1.9 collective-permute-start.7
  158.2 3.9 %collective-permute-done.7 = f32[52,2,256]{2,1,0:T(2,128)S(1)} collective-permute-done((f32[52,2,256]{2,1,0:T(2,128)S(1)}, f32[52,2,256]{2,1,0:T(2,128)S(1)}, u32[]{:S(2)}, u32[]{:S(2)}) %collective-permute-start.7) | collective-permute-done | bytes 106528 | tf_op jit(solution)/shard_map/ppermute | solution.py:18
  163.2 2.9 fusion.213
  167.2 2.5 collective-permute-start.16
  169.7 1.3 collective-permute-start.17
  171.1 5.7 %collective-permute-start.28 = (f32[2,8,256]{2,1,0:T(8,128)S(1)}, f32[2,8,256]{2,1,0:T(8,128)S(1)}, u32[]{:S(2)}, u32[]{:S(2)}) collective-permute-start(f32[2,8,256]{2,1,0:T(8,128)S(1)} %get-tuple-element.58), channel_id=1, source_target_pairs={{0,8},{8,16},{16,24},{1,9},{9,17},{17,25},{2,10},{10,18},{18,26},{... | collective-permute-start | bytes 49160 | tf_op jit(solution)/shard_map/ppermute | solution.py:17
  176.7 1.3 collective-permute-start.29
  178.1 3.9 %collective-permute-start.18 = (f32[52,2,256]{2,1,0:T(2,128)S(1)}, f32[52,2,256]{2,1,0:T(2,128)S(1)}, u32[]{:S(2)}, u32[]{:S(2)}) collective-permute-start(f32[52,2,256]{2,1,0:T(2,128)S(1)} %get-tuple-element.35), channel_id=1, source_target_pairs={{0,1},{1,2},{2,3},{3,4},{4,5},{5,6},{6,7},{8,9},{9,10},{10,11},{11... | collective-permute-start | bytes 319496 | tf_op jit(solution)/shard_map/ppermute | solution.py:17
  182.1 1.9 collective-permute-start.19
  184.1 4.3 %collective-permute-start.30 = (f32[52,2,256]{2,1,0:T(2,128)S(1)}, f32[52,2,256]{2,1,0:T(2,128)S(1)}, u32[]{:S(2)}, u32[]{:S(2)}) collective-permute-start(f32[52,2,256]{2,1,0:T(2,128)S(1)} %get-tuple-element.33), channel_id=1, source_target_pairs={{0,1},{1,2},{2,3},{3,4},{4,5},{5,6},{6,7},{8,9},{9,10},{10,11},{11... | collective-permute-start | bytes 319496 | tf_op jit(solution)/shard_map/ppermute | solution.py:17
  188.4 2.1 collective-permute-start.31
  192.2 3.2 %collective-permute-done.31 = f32[52,2,256]{2,1,0:T(2,128)S(1)} collective-permute-done((f32[52,2,256]{2,1,0:T(2,128)S(1)}, f32[52,2,256]{2,1,0:T(2,128)S(1)}, u32[]{:S(2)}, u32[]{:S(2)}) %collective-permute-start.31) | collective-permute-done | bytes 106528 | tf_op jit(solution)/shard_map/ppermute | solution.py:18
  198.3 2.2 copy.67
  200.5 84.6 %reduce-scatter.2.cloned.1.call-done = f32[3,48,8,32]{1,2,0,3:T(8,128)} async-done(((f32[3,48,8,256]{1,2,0,3:T(8,128)}), f32[3,48,8,32]{1,2,0,3:T(8,128)}) %reduce-scatter.2.cloned.1.call-update) | async-done | bytes 147472 | tf_op jit(solution)/shard_map/reduce_scatter | solution.py:164
  285.1 1.8 copy.68
  (131 shorter events, 20.9 us)
Async XLA Ops:
  6.5 13.9 %copy-start.22 = (s32[3]{0:T(128)S(1)}, s32[3]{0:T(128)}, u32[]{:S(2)}) copy-start(s32[3]{0:T(128)} %constant.120) | copy-start | bytes 40
  6.5 14.0 %copy-start.23 = (s32[3]{0:T(128)S(1)}, s32[3]{0:T(128)}, u32[]{:S(2)}) copy-start(s32[3]{0:T(128)} %constant.123) | copy-start | bytes 40
  6.5 12.4 %copy-start.19 = (s32[1,1536]{1,0:T(1,128)S(1)}, s32[1,1536]{1,0:T(1,128)}, u32[]{:S(2)}) copy-start(s32[1,1536]{1,0:T(1,128)} %param.23) | copy-start | bytes 18436
  6.5 13.3 %copy-start.20 = (f32[1,2]{1,0:T(1,128)S(1)}, f32[1,2]{1,0:T(1,128)}, u32[]{:S(2)}) copy-start(f32[1,2]{1,0:T(1,128)} %param.21) | copy-start | bytes 28
  6.5 78.7 %all-gather.2.cloned.1.call-start = ((), (), s32[]{:S(2)}) async-start(), calls=%async_computation.1 | async-start | bytes 3538944 | tf_op jit(solution)/shard_map/all_gather | solution.py:83
  7.3 24.0 %collective-permute-start.8 = (f32[2,8,256]{2,1,0:T(8,128)S(1)}, f32[2,8,256]{2,1,0:T(8,128)S(1)}, u32[]{:S(2)}, u32[]{:S(2)}) collective-permute-start(f32[2,8,256]{2,1,0:T(8,128)S(1)} %get-tuple-element.72), channel_id=1, source_target_pairs={{0,8},{8,16},{16,24},{1,9},{9,17},{17,25},{2,10},{10,18},{18,26},{... | collective-permute-start | bytes 49160 | tf_op jit(solution)/shard_map/ppermute | solution.py:17
  9.1 22.3 %copy-start.4 = (f32[1,48,8,256]{3,2,1,0:T(8,128)S(1)}, f32[1,48,8,256]{3,2,1,0:T(8,128)}, u32[]{:S(2)}) copy-start(f32[1,48,8,256]{3,2,1,0:T(8,128)} %param.20) | copy-start | bytes 1179652
  9.1 22.3 %collective-permute-start.9 = (f32[2,8,256]{2,1,0:T(8,128)S(1)}, f32[2,8,256]{2,1,0:T(8,128)S(1)}, u32[]{:S(2)}, u32[]{:S(2)}) collective-permute-start(f32[2,8,256]{2,1,0:T(8,128)S(1)} %get-tuple-element.73), channel_id=1, source_target_pairs={{8,0},{16,8},{24,16},{9,1},{17,9},{25,17},{10,2},{18,10},{26,18},{... | collective-permute-start | bytes 49160 | tf_op jit(solution)/shard_map/ppermute | solution.py:18
  12.5 24.9 %copy-start.3 = (f32[1,48,8,256]{3,2,1,0:T(8,128)S(1)}, f32[1,48,8,256]{3,2,1,0:T(8,128)}, u32[]{:S(2)}) copy-start(f32[1,48,8,256]{3,2,1,0:T(8,128)} %param.18) | copy-start | bytes 1179652
  12.5 272.6 %reduce-scatter.2.cloned.1.call-start = ((), (), s32[]{:S(2)}) async-start(), calls=%async_computation.2 | async-start | bytes 3538944 | tf_op jit(solution)/shard_map/reduce_scatter | solution.py:164
  13.3 24.0 %collective-permute-start = (f32[2,8,256]{2,1,0:T(8,128)S(1)}, f32[2,8,256]{2,1,0:T(8,128)S(1)}, u32[]{:S(2)}, u32[]{:S(2)}) collective-permute-start(f32[2,8,256]{2,1,0:T(8,128)S(1)} %get-tuple-element.66), channel_id=1, source_target_pairs={{0,8},{8,16},{16,24},{1,9},{9,17},{17,25},{2,10},{10,18},{18,26},{... | collective-permute-start | bytes 49160 | tf_op jit(solution)/shard_map/ppermute | solution.py:17
  17.6 19.7 %collective-permute-start.1 = (f32[2,8,256]{2,1,0:T(8,128)S(1)}, f32[2,8,256]{2,1,0:T(8,128)S(1)}, u32[]{:S(2)}, u32[]{:S(2)}) collective-permute-start(f32[2,8,256]{2,1,0:T(8,128)S(1)} %get-tuple-element.67), channel_id=1, source_target_pairs={{8,0},{16,8},{24,16},{9,1},{17,9},{25,17},{10,2},{18,10},{26,18},{... | collective-permute-start | bytes 49160 | tf_op jit(solution)/shard_map/ppermute | solution.py:18
  31.5 11.8 %collective-permute-start.10 = (f32[52,2,256]{2,1,0:T(2,128)S(1)}, f32[52,2,256]{2,1,0:T(2,128)S(1)}, u32[]{:S(2)}, u32[]{:S(2)}) collective-permute-start(f32[52,2,256]{2,1,0:T(2,128)S(1)} %get-tuple-element.47), channel_id=1, source_target_pairs={{0,1},{1,2},{2,3},{3,4},{4,5},{5,6},{6,7},{8,9},{9,10},{10,11},{11... | collective-permute-start | bytes 319496 | tf_op jit(solution)/shard_map/ppermute | solution.py:17
  35.3 8.0 %collective-permute-start.11 = (f32[52,2,256]{2,1,0:T(2,128)S(1)}, f32[52,2,256]{2,1,0:T(2,128)S(1)}, u32[]{:S(2)}, u32[]{:S(2)}) collective-permute-start(f32[52,2,256]{2,1,0:T(2,128)S(1)} %get-tuple-element.48), channel_id=1, source_target_pairs={{1,0},{2,1},{3,2},{4,3},{5,4},{6,5},{7,6},{9,8},{10,9},{11,10},{12... | collective-permute-start | bytes 319496 | tf_op jit(solution)/shard_map/ppermute | solution.py:18
  37.4 6.7 %collective-permute-start.2 = (f32[52,2,256]{2,1,0:T(2,128)S(1)}, f32[52,2,256]{2,1,0:T(2,128)S(1)}, u32[]{:S(2)}, u32[]{:S(2)}) collective-permute-start(f32[52,2,256]{2,1,0:T(2,128)S(1)} %get-tuple-element.41), channel_id=1, source_target_pairs={{0,1},{1,2},{2,3},{3,4},{4,5},{5,6},{6,7},{8,9},{9,10},{10,11},{11... | collective-permute-start | bytes 319496 | tf_op jit(solution)/shard_map/ppermute | solution.py:17
  41.3 7.6 %collective-permute-start.3 = (f32[52,2,256]{2,1,0:T(2,128)S(1)}, f32[52,2,256]{2,1,0:T(2,128)S(1)}, u32[]{:S(2)}, u32[]{:S(2)}) collective-permute-start(f32[52,2,256]{2,1,0:T(2,128)S(1)} %get-tuple-element.42), channel_id=1, source_target_pairs={{1,0},{2,1},{3,2},{4,3},{5,4},{6,5},{7,6},{9,8},{10,9},{11,10},{12... | collective-permute-start | bytes 319496 | tf_op jit(solution)/shard_map/ppermute | solution.py:18
  43.5 5.6 %copy-start.9 = (f32[52,12,256]{2,1,0:T(8,128)}, f32[52,12,256]{2,1,0:T(8,128)S(1)}, u32[]{:S(2)}) copy-start(f32[52,12,256]{2,1,0:T(8,128)S(1)} %pad_maximum_fusion.2) | copy-start | bytes 1916932
  89.8 4.7 %copy-start.2 = (f32[48,8,256]{2,1,0:T(8,128)S(1)}, f32[48,8,256]{2,1,0:T(8,128)}, u32[]{:S(2)}) copy-start(f32[48,8,256]{2,1,0:T(8,128)} %param.12) | copy-start | bytes 1179652
  94.6 8.6 %copy-start.5 = (f32[1,48,8,256]{3,2,1,0:T(8,128)S(1)}, f32[1,48,8,256]{3,2,1,0:T(8,128)}, u32[]{:S(2)}) copy-start(f32[1,48,8,256]{3,2,1,0:T(8,128)} %param.20) | copy-start | bytes 1179652
  94.6 8.6 %copy-start.6 = (f32[48,8,256]{2,1,0:T(8,128)S(1)}, f32[48,8,256]{2,1,0:T(8,128)}, u32[]{:S(2)}) copy-start(f32[48,8,256]{2,1,0:T(8,128)} %param.15) | copy-start | bytes 1179652
  94.6 8.6 %copy-start.16 = (f32[1,48,8,256]{3,2,1,0:T(8,128)S(1)}, f32[1,48,8,256]{3,2,1,0:T(8,128)}, u32[]{:S(2)}) copy-start(f32[1,48,8,256]{3,2,1,0:T(8,128)} %param.19) | copy-start | bytes 1179652
  100.5 8.2 %collective-permute-start.24 = (f32[2,8,256]{2,1,0:T(8,128)S(1)}, f32[2,8,256]{2,1,0:T(8,128)S(1)}, u32[]{:S(2)}, u32[]{:S(2)}) collective-permute-start(f32[2,8,256]{2,1,0:T(8,128)S(1)} %get-tuple-element.70), channel_id=1, source_target_pairs={{0,8},{8,16},{16,24},{1,9},{9,17},{17,25},{2,10},{10,18},{18,26},{... | collective-permute-start | bytes 49160 | tf_op jit(solution)/shard_map/ppermute | solution.py:17
  101.8 6.9 %collective-permute-start.25 = (f32[2,8,256]{2,1,0:T(8,128)S(1)}, f32[2,8,256]{2,1,0:T(8,128)S(1)}, u32[]{:S(2)}, u32[]{:S(2)}) collective-permute-start(f32[2,8,256]{2,1,0:T(8,128)S(1)} %get-tuple-element.71), channel_id=1, source_target_pairs={{8,0},{16,8},{24,16},{9,1},{17,9},{25,17},{10,2},{18,10},{26,18},{... | collective-permute-start | bytes 49160 | tf_op jit(solution)/shard_map/ppermute | solution.py:18
  103.6 11.1 %collective-permute-start.20 = (f32[2,8,256]{2,1,0:T(8,128)S(1)}, f32[2,8,256]{2,1,0:T(8,128)S(1)}, u32[]{:S(2)}, u32[]{:S(2)}) collective-permute-start(f32[2,8,256]{2,1,0:T(8,128)S(1)} %get-tuple-element.68), channel_id=1, source_target_pairs={{0,8},{8,16},{16,24},{1,9},{9,17},{17,25},{2,10},{10,18},{18,26},{... | collective-permute-start | bytes 49160 | tf_op jit(solution)/shard_map/ppermute | solution.py:17
  107.4 7.3 %collective-permute-start.21 = (f32[2,8,256]{2,1,0:T(8,128)S(1)}, f32[2,8,256]{2,1,0:T(8,128)S(1)}, u32[]{:S(2)}, u32[]{:S(2)}) collective-permute-start(f32[2,8,256]{2,1,0:T(8,128)S(1)} %get-tuple-element.69), channel_id=1, source_target_pairs={{8,0},{16,8},{24,16},{9,1},{17,9},{25,17},{10,2},{18,10},{26,18},{... | collective-permute-start | bytes 49160 | tf_op jit(solution)/shard_map/ppermute | solution.py:18
  108.8 12.0 %collective-permute-start.26 = (f32[52,2,256]{2,1,0:T(2,128)S(1)}, f32[52,2,256]{2,1,0:T(2,128)S(1)}, u32[]{:S(2)}, u32[]{:S(2)}) collective-permute-start(f32[52,2,256]{2,1,0:T(2,128)S(1)} %get-tuple-element.45), channel_id=1, source_target_pairs={{0,1},{1,2},{2,3},{3,4},{4,5},{5,6},{6,7},{8,9},{9,10},{10,11},{11... | collective-permute-start | bytes 319496 | tf_op jit(solution)/shard_map/ppermute | solution.py:17
  112.3 8.5 %collective-permute-start.27 = (f32[52,2,256]{2,1,0:T(2,128)S(1)}, f32[52,2,256]{2,1,0:T(2,128)S(1)}, u32[]{:S(2)}, u32[]{:S(2)}) collective-permute-start(f32[52,2,256]{2,1,0:T(2,128)S(1)} %get-tuple-element.46), channel_id=1, source_target_pairs={{1,0},{2,1},{3,2},{4,3},{5,4},{6,5},{7,6},{9,8},{10,9},{11,10},{12... | collective-permute-start | bytes 319496 | tf_op jit(solution)/shard_map/ppermute | solution.py:18
  114.8 7.2 %collective-permute-start.22 = (f32[52,2,256]{2,1,0:T(2,128)S(1)}, f32[52,2,256]{2,1,0:T(2,128)S(1)}, u32[]{:S(2)}, u32[]{:S(2)}) collective-permute-start(f32[52,2,256]{2,1,0:T(2,128)S(1)} %get-tuple-element.43), channel_id=1, source_target_pairs={{0,1},{1,2},{2,3},{3,4},{4,5},{5,6},{6,7},{8,9},{9,10},{10,11},{11... | collective-permute-start | bytes 319496 | tf_op jit(solution)/shard_map/ppermute | solution.py:17
  118.2 6.9 %collective-permute-start.23 = (f32[52,2,256]{2,1,0:T(2,128)S(1)}, f32[52,2,256]{2,1,0:T(2,128)S(1)}, u32[]{:S(2)}, u32[]{:S(2)}) collective-permute-start(f32[52,2,256]{2,1,0:T(2,128)S(1)} %get-tuple-element.44), channel_id=1, source_target_pairs={{1,0},{2,1},{3,2},{4,3},{5,4},{6,5},{7,6},{9,8},{10,9},{11,10},{12... | collective-permute-start | bytes 319496 | tf_op jit(solution)/shard_map/ppermute | solution.py:18
  126.3 8.3 %copy-start.17 = (f32[1,48,8,256]{3,2,1,0:T(8,128)S(1)}, f32[1,48,8,256]{3,2,1,0:T(8,128)}, u32[]{:S(2)}) copy-start(f32[1,48,8,256]{3,2,1,0:T(8,128)} %param.17) | copy-start | bytes 1179652
  126.3 8.3 %copy-start.18 = (pred[48,8]{1,0:T(8,128)(4,1)S(1)}, pred[48,8]{1,0:T(8,128)(4,1)}, u32[]{:S(2)}) copy-start(pred[48,8]{1,0:T(8,128)(4,1)} %broadcast_and_fusion) | copy-start | bytes 1156
  126.3 8.3 %copy-start.21 = (pred[256]{0:T(512)(128)(4,1)S(1)}, pred[256]{0:T(512)(128)(4,1)}, u32[]{:S(2)}) copy-start(pred[256]{0:T(512)(128)(4,1)} %iota_compare_fusion.2) | copy-start | bytes 772
  130.4 12.4 %collective-permute-start.12 = (f32[2,8,256]{2,1,0:T(8,128)S(1)}, f32[2,8,256]{2,1,0:T(8,128)S(1)}, u32[]{:S(2)}, u32[]{:S(2)}) collective-permute-start(f32[2,8,256]{2,1,0:T(8,128)S(1)} %get-tuple-element.64), channel_id=1, source_target_pairs={{0,8},{8,16},{16,24},{1,9},{9,17},{17,25},{2,10},{10,18},{18,26},{... | collective-permute-start | bytes 49160 | tf_op jit(solution)/shard_map/ppermute | solution.py:17
  133.3 9.5 %collective-permute-start.13 = (f32[2,8,256]{2,1,0:T(8,128)S(1)}, f32[2,8,256]{2,1,0:T(8,128)S(1)}, u32[]{:S(2)}, u32[]{:S(2)}) collective-permute-start(f32[2,8,256]{2,1,0:T(8,128)S(1)} %get-tuple-element.65), channel_id=1, source_target_pairs={{8,0},{16,8},{24,16},{9,1},{17,9},{25,17},{10,2},{18,10},{26,18},{... | collective-permute-start | bytes 49160 | tf_op jit(solution)/shard_map/ppermute | solution.py:18
  135.8 14.2 %collective-permute-start.4 = (f32[2,8,256]{2,1,0:T(8,128)S(1)}, f32[2,8,256]{2,1,0:T(8,128)S(1)}, u32[]{:S(2)}, u32[]{:S(2)}) collective-permute-start(f32[2,8,256]{2,1,0:T(8,128)S(1)} %get-tuple-element.62), channel_id=1, source_target_pairs={{0,8},{8,16},{16,24},{1,9},{9,17},{17,25},{2,10},{10,18},{18,26},{... | collective-permute-start | bytes 49160 | tf_op jit(solution)/shard_map/ppermute | solution.py:17
  141.4 8.5 %collective-permute-start.5 = (f32[2,8,256]{2,1,0:T(8,128)S(1)}, f32[2,8,256]{2,1,0:T(8,128)S(1)}, u32[]{:S(2)}, u32[]{:S(2)}) collective-permute-start(f32[2,8,256]{2,1,0:T(8,128)S(1)} %get-tuple-element.63), channel_id=1, source_target_pairs={{8,0},{16,8},{24,16},{9,1},{17,9},{25,17},{10,2},{18,10},{26,18},{... | collective-permute-start | bytes 49160 | tf_op jit(solution)/shard_map/ppermute | solution.py:18
  142.8 14.2 %collective-permute-start.14 = (f32[52,2,256]{2,1,0:T(2,128)S(1)}, f32[52,2,256]{2,1,0:T(2,128)S(1)}, u32[]{:S(2)}, u32[]{:S(2)}) collective-permute-start(f32[52,2,256]{2,1,0:T(2,128)S(1)} %get-tuple-element.39), channel_id=1, source_target_pairs={{0,1},{1,2},{2,3},{3,4},{4,5},{5,6},{6,7},{8,9},{9,10},{10,11},{11... | collective-permute-start | bytes 319496 | tf_op jit(solution)/shard_map/ppermute | solution.py:17
  148.0 9.1 %collective-permute-start.15 = (f32[52,2,256]{2,1,0:T(2,128)S(1)}, f32[52,2,256]{2,1,0:T(2,128)S(1)}, u32[]{:S(2)}, u32[]{:S(2)}) collective-permute-start(f32[52,2,256]{2,1,0:T(2,128)S(1)} %get-tuple-element.40), channel_id=1, source_target_pairs={{1,0},{2,1},{3,2},{4,3},{5,4},{6,5},{7,6},{9,8},{10,9},{11,10},{12... | collective-permute-start | bytes 319496 | tf_op jit(solution)/shard_map/ppermute | solution.py:18
  150.0 8.2 %collective-permute-start.6 = (f32[52,2,256]{2,1,0:T(2,128)S(1)}, f32[52,2,256]{2,1,0:T(2,128)S(1)}, u32[]{:S(2)}, u32[]{:S(2)}) collective-permute-start(f32[52,2,256]{2,1,0:T(2,128)S(1)} %get-tuple-element.37), channel_id=1, source_target_pairs={{0,1},{1,2},{2,3},{3,4},{4,5},{5,6},{6,7},{8,9},{9,10},{10,11},{11... | collective-permute-start | bytes 319496 | tf_op jit(solution)/shard_map/ppermute | solution.py:17
  155.2 6.9 %collective-permute-start.7 = (f32[52,2,256]{2,1,0:T(2,128)S(1)}, f32[52,2,256]{2,1,0:T(2,128)S(1)}, u32[]{:S(2)}, u32[]{:S(2)}) collective-permute-start(f32[52,2,256]{2,1,0:T(2,128)S(1)} %get-tuple-element.38), channel_id=1, source_target_pairs={{1,0},{2,1},{3,2},{4,3},{5,4},{6,5},{7,6},{9,8},{10,9},{11,10},{12... | collective-permute-start | bytes 319496 | tf_op jit(solution)/shard_map/ppermute | solution.py:18
  167.2 10.8 %collective-permute-start.16 = (f32[2,8,256]{2,1,0:T(8,128)S(1)}, f32[2,8,256]{2,1,0:T(8,128)S(1)}, u32[]{:S(2)}, u32[]{:S(2)}) collective-permute-start(f32[2,8,256]{2,1,0:T(8,128)S(1)} %get-tuple-element.60), channel_id=1, source_target_pairs={{0,8},{8,16},{16,24},{1,9},{9,17},{17,25},{2,10},{10,18},{18,26},{... | collective-permute-start | bytes 49160 | tf_op jit(solution)/shard_map/ppermute | solution.py:17
  169.7 8.3 %collective-permute-start.17 = (f32[2,8,256]{2,1,0:T(8,128)S(1)}, f32[2,8,256]{2,1,0:T(8,128)S(1)}, u32[]{:S(2)}, u32[]{:S(2)}) collective-permute-start(f32[2,8,256]{2,1,0:T(8,128)S(1)} %get-tuple-element.61), channel_id=1, source_target_pairs={{8,0},{16,8},{24,16},{9,1},{17,9},{25,17},{10,2},{18,10},{26,18},{... | collective-permute-start | bytes 49160 | tf_op jit(solution)/shard_map/ppermute | solution.py:18
  171.1 12.9 %collective-permute-start.28 = (f32[2,8,256]{2,1,0:T(8,128)S(1)}, f32[2,8,256]{2,1,0:T(8,128)S(1)}, u32[]{:S(2)}, u32[]{:S(2)}) collective-permute-start(f32[2,8,256]{2,1,0:T(8,128)S(1)} %get-tuple-element.58), channel_id=1, source_target_pairs={{0,8},{8,16},{16,24},{1,9},{9,17},{17,25},{2,10},{10,18},{18,26},{... | collective-permute-start | bytes 49160 | tf_op jit(solution)/shard_map/ppermute | solution.py:17
  176.7 7.3 %collective-permute-start.29 = (f32[2,8,256]{2,1,0:T(8,128)S(1)}, f32[2,8,256]{2,1,0:T(8,128)S(1)}, u32[]{:S(2)}, u32[]{:S(2)}) collective-permute-start(f32[2,8,256]{2,1,0:T(8,128)S(1)} %get-tuple-element.59), channel_id=1, source_target_pairs={{8,0},{16,8},{24,16},{9,1},{17,9},{25,17},{10,2},{18,10},{26,18},{... | collective-permute-start | bytes 49160 | tf_op jit(solution)/shard_map/ppermute | solution.py:18
  178.1 12.5 %collective-permute-start.18 = (f32[52,2,256]{2,1,0:T(2,128)S(1)}, f32[52,2,256]{2,1,0:T(2,128)S(1)}, u32[]{:S(2)}, u32[]{:S(2)}) collective-permute-start(f32[52,2,256]{2,1,0:T(2,128)S(1)} %get-tuple-element.35), channel_id=1, source_target_pairs={{0,1},{1,2},{2,3},{3,4},{4,5},{5,6},{6,7},{8,9},{9,10},{10,11},{11... | collective-permute-start | bytes 319496 | tf_op jit(solution)/shard_map/ppermute | solution.py:17
  182.1 8.5 %collective-permute-start.19 = (f32[52,2,256]{2,1,0:T(2,128)S(1)}, f32[52,2,256]{2,1,0:T(2,128)S(1)}, u32[]{:S(2)}, u32[]{:S(2)}) collective-permute-start(f32[52,2,256]{2,1,0:T(2,128)S(1)} %get-tuple-element.36), channel_id=1, source_target_pairs={{1,0},{2,1},{3,2},{4,3},{5,4},{6,5},{7,6},{9,8},{10,9},{11,10},{12... | collective-permute-start | bytes 319496 | tf_op jit(solution)/shard_map/ppermute | solution.py:18
  184.1 8.1 %collective-permute-start.30 = (f32[52,2,256]{2,1,0:T(2,128)S(1)}, f32[52,2,256]{2,1,0:T(2,128)S(1)}, u32[]{:S(2)}, u32[]{:S(2)}) collective-permute-start(f32[52,2,256]{2,1,0:T(2,128)S(1)} %get-tuple-element.33), channel_id=1, source_target_pairs={{0,1},{1,2},{2,3},{3,4},{4,5},{5,6},{6,7},{8,9},{9,10},{10,11},{11... | collective-permute-start | bytes 319496 | tf_op jit(solution)/shard_map/ppermute | solution.py:17
  188.4 6.9 %collective-permute-start.31 = (f32[52,2,256]{2,1,0:T(2,128)S(1)}, f32[52,2,256]{2,1,0:T(2,128)S(1)}, u32[]{:S(2)}, u32[]{:S(2)}) collective-permute-start(f32[52,2,256]{2,1,0:T(2,128)S(1)} %get-tuple-element.34), channel_id=1, source_target_pairs={{1,0},{2,1},{3,2},{4,3},{5,4},{6,5},{7,6},{9,8},{10,9},{11,10},{12... | collective-permute-start | bytes 319496 | tf_op jit(solution)/shard_map/ppermute | solution.py:18
  (10 other events, 34.6 us)
Sparse Core Ops, SparseCore 0:
  12.6 72.5 all-gather.1
  200.7 84.4 reduce-scatter.1
where the time goes:
time: 295 us; the launch traced here: 294 us
  waiting for transfers between devices  135 us (46%)
  starting transfers between devices  88.4 us (30%)
  other arithmetic  37.2 us (13%)
  local copies, waits for them, and re-layouts  18.5 us (6%)
  between operations  15.1 us (5%)
    reduce_scatter x1, waiting for transfers between devices, per_device(): return lax.psum_scatter(result, 'shot', scatter_dimension=3, tiled=True)  84.6 us
    ppermute x16, starting transfers between devices, with_halo(): before = lax.ppermute(last, axis, up)  61 us
    all_gather x1, waiting for transfers between devices, per_device(): change = lax.all_gather(perturbation, 'shot', axis=3, tiled=True)  34.3 us
    ppermute x16, starting transfers between devices, with_halo(): after = lax.ppermute(first, axis, down)  27.4 us
    ppermute x16, waiting for transfers between devices, with_halo(): after = lax.ppermute(first, axis, down)  15 us
    unnamed x4, other arithmetic  8.88 us
    unnamed x53, local copies, waits for them, and re-layouts  7.95 us
  transfers between devices with their start and end apart: 34, of which 7 were waited for; matrix products, arithmetic and copies ran while one was open for 8% of the time, Pallas kernels for 0%

commit v1 on v0

v1 whole, which is shorter than its diff:
```python
import functools

import jax
import jax.numpy as jnp
from jax import lax
from jax.experimental import pallas as pl
from jax.experimental.pallas import tpu as pltpu
from jax.sharding import PartitionSpec as P

F32 = jnp.float32
VM = pl.BlockSpec(memory_space=pltpu.VMEM)
SM = pl.BlockSpec(memory_space=pltpu.SMEM)
LIMIT = 24 * 1024 * 1024

S0, S1, S2 = -2.5, 4.0 / 3.0, -1.0 / 12.0
D1, D2 = 2.0 / 3.0, -1.0 / 12.0


def call(kernel, outs, ins, scratch=(), smem=(), cost=None, name=None):
    return pl.pallas_call(
        kernel,
        out_shape=[jax.ShapeDtypeStruct(shape, F32) for shape in outs],
        in_specs=[SM if i in smem else VM for i in range(len(ins))],
        out_specs=[VM] * len(outs),
        scratch_shapes=list(scratch),
        compiler_params=pltpu.CompilerParams(vmem_limit_bytes=LIMIT),
        cost_estimate=cost,
        name=name,
    )(*ins)


def cycle(value, axis, step):
    size = lax.axis_size(axis)
    return lax.ppermute(value, axis, [(i, (i + step) % size) for i in range(size)])


def rows():
    return lax.broadcasted_iota(jnp.int32, (8, 128), 0)


def lanes():
    return lax.broadcasted_iota(jnp.int32, (8, 128), 1)


def pack_y(fields, up, down):
    row = rows()
    nx = fields[0].shape[0]
    pieces = 4 // len(fields)
    step = nx // pieces

    def body(i, _):
        for h in (0, 128):
            tile = pl.ds(h, 128)
            for out, base in ((up, 6), (down, 0)):
                acc = None
                for piece in range(pieces):
                    for f, field in enumerate(fields):
                        at = 2 * (piece * len(fields) + f)
                        value = field[i + piece * step, :, tile]
                        value = pltpu.roll(value, (at - base) % 8, 0) if at != base else value
                        acc = value if acc is None else jnp.where(row >= at, value, acc)
                out[i, :, tile] = acc
        return 0

    lax.fori_loop(0, step, body, 0, unroll=2)


def pack_x(fields, up, down):
    for f, field in enumerate(fields):
        n = field.shape[0]
        up[2 * f : 2 * f + 2] = field[n - 2 : n]
        down[2 * f : 2 * f + 2] = field[0:2]


def fill(pad, field, before, after, f, gx, last_x):
    n = field.shape[0]
    pad[2 : n + 2] = field[...]
    pad[0:2] = jnp.where(gx > 0, before[2 * f : 2 * f + 2], 0.0)
    pad[n + 2 : n + 4] = jnp.where(gx < last_x, after[2 * f : 2 * f + 2], 0.0)


def edge_rows(before, after, i, at, tile, first, last):
    row = rows()
    lower = before[i, :, tile]
    upper = after[i, :, tile]
    if at != 6:
        lower = pltpu.roll(lower, (6 - at) % 8, 0)
    if at != 0:
        upper = pltpu.roll(upper, (-at) % 8, 0)
    return jnp.where((row >= 6) & first, lower, jnp.where((row <= 1) & last, upper, 0.0))


def z_shifts(a, b):
    lane = lanes()
    out = []
    for k in (1, 2):
        ra, rb = pltpu.roll(a, k, 1), pltpu.roll(b, k, 1)
        low = (jnp.where(lane < k, 0.0, ra), jnp.where(lane < k, ra, rb))
        ra, rb = pltpu.roll(a, 128 - k, 1), pltpu.roll(b, 128 - k, 1)
        high = (jnp.where(lane >= 128 - k, rb, ra), jnp.where(lane >= 128 - k, 0.0, rb))
        out.append((low, high))
    return out


def second_z(pair):
    (l1, h1), (l2, h2) = z_shifts(*pair)
    return [S0 * pair[t] + S1 * (l1[t] + h1[t]) + S2 * (l2[t] + h2[t]) for t in (0, 1)]


def first_z(pair):
    (l1, h1), (l2, h2) = z_shifts(*pair)
    return [D1 * (h1[t] - l1[t]) + D2 * (h2[t] - l2[t]) for t in (0, 1)]


def lateral(pad, x, edge, slope=True):
    row = rows()
    horizontal, slopes, centre = [], [], []
    for t in (0, 1):
        tile = pl.ds(128 * t, 128)
        c = pad[x + 2, :, tile]
        xl, xh, xl2, xh2 = (pad[x + k, :, tile] for k in (1, 3, 0, 4))
        e = edge[t]
        yl = pltpu.roll(jnp.where(row == 7, e, c), 1, 0)
        yl2 = pltpu.roll(jnp.where(row >= 6, e, c), 2, 0)
        yh = pltpu.roll(jnp.where(row == 0, e, c), 7, 0)
        yh2 = pltpu.roll(jnp.where(row <= 1, e, c), 6, 0)
        horizontal.append(2.0 * S0 * c + S1 * ((xl + xh) + (yl + yh)) + S2 * ((xl2 + xh2) + (yl2 + yh2)))
        if slope:
            slopes.append(D1 * ((xh - xl) + (yh - yl)) + D2 * ((xh2 - xl2) + (yh2 - yl2)))
        centre.append(c)
    return horizontal, slopes, centre


def derivs(pad, x, edge):
    horizontal, slopes, centre = lateral(pad, x, edge)
    return horizontal, second_z(centre), first_z(slopes), centre


def places():
    return lax.axis_index("gx"), lax.axis_index("gy")


def chunk_of(array, shot, lane_shift):
    half = array[:, :, pl.ds(pl.multiple_of((shot // 4) * 128, 128), 128)]
    return pltpu.roll(half, lane_shift, 2)


def prepare_kernel(u, l, p, speed, epsilon, delta, yup, ydn, xup, xdn, chunk, model, pbuf):
    fields = [u.at[0], l.at[0]]
    pack_y(fields, yup, ydn)
    pack_x(fields, xup, xdn)
    shot = lax.axis_index("shot")
    shift = lax.rem(128 - 32 * lax.rem(shot, 4), 128)
    for k, array in enumerate((speed, epsilon, delta)):
        model[k] = chunk_of(array, shot, shift)
    pbuf[:, :, :, 0:32] = p[...]
    lane = lanes()
    group = p.shape[1] // 4
    for i in range(group):
        parts = [[], []]
        for g in range(4):
            x = g * group + i
            p0, p1, p2 = (pbuf[k, x] for k in range(3))
            s, e, d = (model[k, x] for k in range(3))
            for f, q in enumerate((p0 * e + s * p1, p0 * d + s * p2)):
                parts[f].append(pltpu.roll(q, 32 * g, 1) if g else q)
        for f in (0, 1):
            a, b, c, d = parts[f]
            chunk[f * group + i] = jnp.where(
                lane < 32, a, jnp.where(lane < 64, b, jnp.where(lane < 96, c, d))
            )


def first_kernel(
    wavelet, source, u, um, l, lm, ylo, yhi, xlo, xhi, speed, epsilon, delta, tilt,
    u1, l1, hu, vu, hl, vl, padu, padl,
):
    gx, gy = places()
    first, last = gy > 0, gy < lax.axis_size("gy") - 1
    for f, (pad, w) in enumerate(((padu, u), (padl, l))):
        fill(pad, w.at[0], xlo, xhi, f, gx, lax.axis_size("gx") - 1)
    nx = u.shape[1]
    half = nx // 2
    lane = lanes()
    amount, depth = wavelet[0, 0], source[0]
    for piece in (0, 1):

        def body(i, _):
            x = i + piece * half
            for f, (pad, prev, nxt, h_out, v_out) in enumerate(
                ((padu, um, u1, hu, vu), (padl, lm, l1, hl, vl))
            ):
                edge = [
                    edge_rows(ylo, yhi, i, 4 * piece + 2 * f, pl.ds(128 * t, 128), first, last)
                    for t in (0, 1)
                ]
                hh, vv, mm, cc = derivs(pad, x, edge)
                for t in (0, 1):
                    tile = pl.ds(128 * t, 128)
                    h_out[x, :, tile] = hh[t]
                    v_out[x, :, tile] = vv[t]
                    new = 2.0 * cc[t] - prev[0, x, :, tile] + (
                        speed[x, :, tile] * (epsilon[x, :, tile] * hh[t] + delta[x, :, tile] * vv[t])
                        + tilt[x, :, tile] * mm[t]
                    )
                    if f == 0:
                        new = new + jnp.where(lane + 128 * t == depth, amount, 0.0)
                    nxt[x, :, tile] = new
            return 0

        lax.fori_loop(0, half, body, 0, unroll=2)


def born_kernel(
    mine, from1, from2, from3, u1, l1, hu, vu, hl, vl,
    q1, q2, b1, d1, yup, ydn, xup, xdn, chunks,
):
    shot = lax.axis_index("shot")
    y, xh = shot // 2, lax.rem(shot, 2)
    group = u1.shape[0] // 4
    for k, pair in enumerate((mine, from1, from2, from3)):
        there = lax.rem(y + 4 - k, 4) * 2
        chunks[there + xh] = pair[0 : 2 * group]
        chunks[there + 1 - xh] = pair[2 * group : 4 * group]
    lane = lanes()
    for g in range(4):

        def body(i, _):
            x = g * group + i
            for t in (0, 1):
                tile = pl.ds(128 * t, 128)
                both = []
                for f in (0, 1):
                    parts = []
                    for k in range(4):
                        part = chunks[4 * t + k, f * group + i]
                        parts.append(pltpu.roll(part, (32 * (k - g)) % 128, 1) if k != g else part)
                    a, b, c, d = parts
                    both.append(jnp.where(lane < 32, a, jnp.where(lane < 64, b, jnp.where(lane < 96, c, d))))
                q1[x, :, tile], q2[x, :, tile] = both
                b1[x, :, tile] = both[0] * hu[x, :, tile] + both[1] * vu[x, :, tile]
                d1[x, :, tile] = both[0] * hl[x, :, tile] + both[1] * vl[x, :, tile]
            return 0

        lax.fori_loop(0, group, body, 0, unroll=2)
    fields = [u1, b1, l1, d1]
    pack_y(fields, yup, ydn)
    pack_x(fields, xup, xdn)


def second_kernel(
    wavelet, source, u, u1, b1, q1, q2, ylo, yhi, xlo, xhi, speed, epsilon, delta, tilt,
    u2, b2, hu, vu, hb, vb, yup, ydn, xup, xdn, padu, padb,
):
    gx, gy = places()
    first, last = gy > 0, gy < lax.axis_size("gy") - 1
    for f, (pad, w) in enumerate(((padu, u1), (padb, b1))):
        fill(pad, w, xlo, xhi, f, gx, lax.axis_size("gx") - 1)
    lane = lanes()
    amount, depth = wavelet[0, 1], source[0]

    def body(x, _):
        edges = [
            [edge_rows(ylo, yhi, x, 2 * f, pl.ds(128 * t, 128), first, last) for t in (0, 1)] for f in (0, 1)
        ]
        h0, v0, m0, c0 = derivs(padu, x, edges[0])
        h1, v1, m1, c1 = derivs(padb, x, edges[1])
        for t in (0, 1):
            tile = pl.ds(128 * t, 128)
            s, e, d, k = (w[x, :, tile] for w in (speed, epsilon, delta, tilt))
            u2[x, :, tile] = (
                2.0 * c0[t] - u[0, x, :, tile] + (s * (e * h0[t] + d * v0[t]) + k * m0[t])
                + jnp.where(lane + 128 * t == depth, amount, 0.0)
            )
            b2[x, :, tile] = (
                2.0 * c1[t] + (s * (e * h1[t] + d * v1[t]) + k * m1[t])
                + (q1[x, :, tile] * h0[t] + q2[x, :, tile] * v0[t])
            )
            hu[x, :, tile], vu[x, :, tile] = h0[t], v0[t]
            hb[x, :, tile], vb[x, :, tile] = h1[t], v1[t]
        return 0

    lax.fori_loop(0, u1.shape[0], body, 0, unroll=2)
    fields = [u2, b2]
    pack_y(fields, yup, ydn)
    pack_x(fields, xup, xdn)


def counts_kernel(cells, out, *, size_y, depth):
    nx, ny = out.shape[0], out.shape[1]
    gx, gy = places()
    index = cells[...]
    cx = lax.div(index, size_y * depth) - gx * nx
    cy = lax.rem(lax.div(index, depth), size_y) - gy * ny
    cz = lax.rem(index, depth)
    inside = (cx >= 0) & (cx < nx) & (cy >= 0) & (cy < ny)
    place = jnp.where(inside, cx * ny + cy, -1)
    n = index.shape[1]
    left = jnp.where(lax.broadcasted_iota(jnp.int32, (nx * ny, n), 0) == place, 1.0, 0.0).astype(jnp.bfloat16)
    right = jnp.where(lax.broadcasted_iota(jnp.int32, (depth, n), 0) == cz, 1.0, 0.0).astype(jnp.bfloat16)
    total = lax.dot_general(left, right, (((1,), (1,)), ((), ())), preferred_element_type=F32)
    out[...] = total.reshape(nx, ny, depth)


def adjoint_kernel(
    l, l1, d1, b1, q1, q2, counts, hu, vu, hb, vb, u2, b2, ylo, yhi, xlo, xhi, speed, epsilon, delta, tilt,
    l2, d2, a1, c1, padl, padd,
):
    gx, gy = places()
    first, last = gy > 0, gy < lax.axis_size("gy") - 1
    for f, (pad, w) in enumerate(((padl, l1), (padd, d1))):
        fill(pad, w, xlo, xhi, f + 2, gx, lax.axis_size("gx") - 1)

    def body(x, _):
        edges = [
            [edge_rows(ylo, yhi, x, 4 + 2 * f, pl.ds(128 * t, 128), first, last) for t in (0, 1)]
            for f in (0, 1)
        ]
        hl, vl, ml, cl = derivs(padl, x, edges[0])
        hd, vd, md, cd = derivs(padd, x, edges[1])
        vu2 = second_z([u2[x, :, pl.ds(128 * t, 128)] for t in (0, 1)])
        vb2 = second_z([b2[x, :, pl.ds(128 * t, 128)] for t in (0, 1)])
        for t in (0, 1):
            tile = pl.ds(128 * t, 128)
            s, e, d, k = (w[x, :, tile] for w in (speed, epsilon, delta, tilt))
            new_l = 2.0 * cl[t] - l[0, x, :, tile] + (s * (e * hl[t] + d * vl[t]) + k * ml[t])
            new_d = (
                2.0 * cd[t] + (s * (e * hd[t] + d * vd[t]) + k * md[t])
                + (q1[x, :, tile] * hl[t] + q2[x, :, tile] * vl[t]) + counts[x, :, tile] * b1[x, :, tile]
            )
            l2[x, :, tile] = new_l
            d2[x, :, tile] = new_d
            a1[x, :, tile] = hu[x, :, tile] * cd[t] + hb[x, :, tile] * cl[t]
            c1[x, :, tile] = (
                vu[x, :, tile] * cd[t] + vb[x, :, tile] * cl[t] + vu2[t] * new_d + vb2[t] * new_l
            )
        return 0

    lax.fori_loop(0, l1.shape[0], body, 0, unroll=2)


def image_kernel(u2, b2, ylo, yhi, xlo, xhi, l2, d2, a1, c1, *rest):
    outs, (padu, padb, total, chunks) = rest[:8], rest[8:]
    gx, gy = places()
    first, last = gy > 0, gy < lax.axis_size("gy") - 1
    for f, (pad, w) in enumerate(((padu, u2), (padb, b2))):
        fill(pad, w, xlo, xhi, f, gx, lax.axis_size("gx") - 1)
    nx = u2.shape[0]
    half = nx // 2
    for piece in (0, 1):

        def body(i, _):
            x = i + piece * half
            edges = [
                [
                    edge_rows(ylo, yhi, i, 4 * piece + 2 * f, pl.ds(128 * t, 128), first, last)
                    for t in (0, 1)
                ]
                for f in (0, 1)
            ]
            hu = lateral(padu, x, edges[0], False)[0]
            hb = lateral(padb, x, edges[1], False)[0]
            for t in (0, 1):
                tile = pl.ds(128 * t, 128)
                total[x, :, tile] = a1[x, :, tile] + hu[t] * d2[x, :, tile] + hb[t] * l2[x, :, tile]
            return 0

        lax.fori_loop(0, half, body, 0, unroll=2)
    lane = lanes()
    group = nx // 4

    def pack(i, _):
        for f, array in enumerate((total, c1)):
            for t in (0, 1):
                parts = [array[g * group + i, :, pl.ds(128 * t, 128)] for g in range(4)]
                for k in range(4):
                    a, b, c, d = (
                        pltpu.roll(part, (32 * (g - k)) % 128, 1) if g != k else part
                        for g, part in enumerate(parts)
                    )
                    chunks[4 * t + k, f * group + i] = jnp.where(
                        lane < 32, a, jnp.where(lane < 64, b, jnp.where(lane < 96, c, d))
                    )
        return 0

    lax.fori_loop(0, group, pack, 0, unroll=2)
    shot = lax.axis_index("shot")
    for m, out in enumerate(outs):
        out[...] = chunks[shot ^ m]


def sum_kernel(model, *rest):
    parts, out = rest[:-1], rest[-1]
    group = out.shape[1] // 4
    for i in range(group):
        sums = []
        for f in (0, 1):
            value = parts[0][f * group + i]
            for part in parts[1:]:
                value = value + part[f * group + i]
            sums.append(value)
        for g in range(4):
            x = g * group + i
            a, c = (pltpu.roll(v, (128 - 32 * g) % 128, 1) if g else v for v in sums)
            s, e, d = (model[k, x] for k in range(3))
            out[0, x] = (e * a + d * c)[:, 0:32]
            out[1, x] = (s * a)[:, 0:32]
            out[2, x] = (s * c)[:, 0:32]


def per_device(
    speed, epsilon, delta, tilt, perturbation, forward_prev, forward_now, adjoint_prev, adjoint_now,
    wavelet, source_cell, receiver_cells,
):
    nx, ny, nz = speed.shape
    whole = (nx, ny, nz)
    pad = pltpu.VMEM((nx + 4, ny, nz), F32)
    half_rows = (nx // 2, ny, nz)
    packed = (nx // 2, ny, 128)
    model = (speed, epsilon, delta)

    yup, ydn, xup, xdn, mine, slices = call(
        prepare_kernel,
        [half_rows, half_rows, (4, ny, nz), (4, ny, nz), packed, (3, nx, ny, 128)],
        (forward_now, adjoint_now, perturbation) + model,
        [pltpu.VMEM((3, nx, ny, 128), F32)],
        name="prepare",
    )

    def exchange(yup, ydn, xup, xdn):
        return cycle(yup, "gy", 1), cycle(ydn, "gy", -1), cycle(xup, "gx", 1), cycle(xdn, "gx", -1)

    partner = lax.ppermute(mine, "shot", [(i, i ^ 1) for i in range(8)])
    halo = exchange(yup, ydn, xup, xdn)
    pair = jnp.concatenate([mine, partner], axis=0)
    others = [
        lax.ppermute(pair, "shot", [(i, (i // 2 + k) % 4 * 2 + i % 2) for i in range(8)]) for k in (1, 2, 3)
    ]
    (counts,) = call(
        functools.partial(counts_kernel, size_y=ny * lax.axis_size("gy"), depth=nz),
        [whole],
        (receiver_cells,),
        name="counts",
    )
    u1, l1, hu0, vu0, hl0, vl0 = call(
        first_kernel,
        [whole] * 6,
        (wavelet, source_cell, forward_now, forward_prev, adjoint_now, adjoint_prev)
        + halo + model + (tilt,),
        [pad, pad],
        (0, 1),
        name="first",
    )
    q1, q2, b1, d1, yup, ydn, xup, xdn = call(
        born_kernel,
        [whole] * 4 + [whole] * 2 + [(8, ny, nz)] * 2,
        (pair, *others, u1, l1, hu0, vu0, hl0, vl0),
        [pltpu.VMEM((8, nx // 2, ny, 128), F32)],
        name="born",
    )
    halo = exchange(yup, ydn, xup, xdn)
    u2, b2, hu1, vu1, hb1, vb1, yup, ydn, xup, xdn = call(
        second_kernel,
        [whole] * 6 + [half_rows] * 2 + [(4, ny, nz)] * 2,
        (wavelet, source_cell, forward_now, u1, b1, q1, q2) + halo + model + (tilt,),
        [pad, pad],
        (0, 1),
        name="second",
    )
    halo2 = exchange(yup, ydn, xup, xdn)
    l2, d2, a1, c1 = call(
        adjoint_kernel,
        [whole] * 4,
        (adjoint_now, l1, d1, b1, q1, q2, counts, hu1, vu1, hb1, vb1, u2, b2) + halo + model + (tilt,),
        [pad, pad],
        name="adjoint",
    )
    terms = call(
        image_kernel,
        [packed] * 8,
        (u2, b2) + halo2 + (l2, d2, a1, c1),
        [pad, pad, pltpu.VMEM(whole, F32), pltpu.VMEM((8, nx // 2, ny, 128), F32)],
        name="image",
    )
    arrived = [terms[0]] + [
        lax.ppermute(terms[m], "shot", [(i, i ^ m) for i in range(8)]) for m in range(1, 8)
    ]
    (out,) = call(sum_kernel, [(3, nx, ny, nz // 8)], (slices, *arrived), name="sum")
    return out


def solution(mesh):
    placed = (
        P("gx", "gy", None),
        P("gx", "gy", None),
        P("gx", "gy", None),
        P("gx", "gy", None),
        P(None, "gx", "gy", "shot"),
        P("shot", "gx", "gy", None),
        P("shot", "gx", "gy", None),
        P("shot", "gx", "gy", None),
        P("shot", "gx", "gy", None),
        P("shot", None),
        P("shot"),
        P("shot", None),
    )
    return jax.shard_map(
        per_device,
        mesh=mesh,
        in_specs=placed,
        out_specs=P(None, "gx", "gy", "shot"),
        check_vma=False,
    )
```

time: 295 us -> 82.6 us (0.28)
  the two profiles are of different devices: /device:TPU:32 before, /device:TPU:4 now
where the time goes in v1:
time: 82.6 us; the launch traced here: 82.3 us
  starting transfers between devices  39.8 us (48%)
  Pallas kernels  18.5 us (22%)
  waiting for transfers between devices  17.8 us (22%)
  local copies, waits for them, and re-layouts  5.34 us (6%)
  between operations  0.91 us (1%)
    pallas_call x8, Pallas kernels, call(): pl.pallas_call(kernel, out_shape=[jax.ShapeDtypeStruct(shape, F32) for sh...  18.5 us
    ppermute x12, starting transfers between devices, cycle(): lax.ppermute(value, axis, [(i, (i + step) % size) for i in range(size)])  17.9 us
    ppermute x7, starting transfers between devices, per_device(): lax.ppermute(terms[m], 'shot', [(i, i ^ m) for i in range(8)])  15.5 us
    ppermute x7, waiting for transfers between devices, per_device(): lax.ppermute(terms[m], 'shot', [(i, i ^ m) for i in range(8)])  6.47 us
    ppermute x3, starting transfers between devices, per_device(): lax.ppermute(pair, 'shot', [(i, (i // 2 + k) % 4 * 2 + i % 2) for i in ra...  5.92 us
    ppermute x1, waiting for transfers between devices, per_device(): partner = lax.ppermute(mine, 'shot', [(i, i ^ 1) for i in range(8)])  5.61 us
    ppermute x12, waiting for transfers between devices, cycle(): lax.ppermute(value, axis, [(i, (i + step) % size) for i in range(size)])  4.47 us
    unnamed x28, local copies, waits for them, and re-layouts  4.36 us
  transfers between devices with their start and end apart: 23, of which 7 were waited for; matrix products, arithmetic and copies ran while one was open for 0% of the time, Pallas kernels for 11%

profile of v1, /device:TPU:4, one launch (start us, length us, event | category | flops | bytes accessed | tf_op | source)
XLA Modules:
  0.0 82.3 jit_solution(247405393633263729)
XLA Ops:
  0.0 1.3 %copy.13.p = f32[3,48,8,32]{3,2,1,0:T(8,128)S(1)} copy(f32[3,48,8,32]{1,3,2,0:T(8,128)} %param.16) | data formatting | bytes 294912 | tf_op args[4]
  1.4 0.0 copy-start.2
  1.4 1.0 %copy-done.2 = f32[48,8,256]{2,1,0:T(8,128)S(1)} copy-done((f32[48,8,256]{2,1,0:T(8,128)S(1)}, f32[48,8,256]{2,1,0:T(8,128)}, u32[]{:S(2)}) %copy-start.2) | copy-done | bytes 393240
  2.4 1.0 %copy-done.4 = f32[1,48,8,256]{3,2,1,0:T(8,128)S(1)} copy-done((f32[1,48,8,256]{3,2,1,0:T(8,128)S(1)}, f32[1,48,8,256]{3,2,1,0:T(8,128)}, u32[]{:S(2)}) %copy-start.4) | copy-done | bytes 393240
  3.3 1.0 %copy-done.6 = f32[1,48,8,256]{3,2,1,0:T(8,128)S(1)} copy-done((f32[1,48,8,256]{3,2,1,0:T(8,128)S(1)}, f32[1,48,8,256]{3,2,1,0:T(8,128)}, u32[]{:S(2)}) %copy-start.6) | copy-done | bytes 393240
  4.3 0.5 prepare.1
  4.8 0.0 copy-start.8
  4.8 2.0 %collective-permute-start = (f32[24,8,256]{2,1,0:T(8,128)S(1)}, f32[24,8,256]{2,1,0:T(8,128)S(1)}, u32[]{:S(2)}, u32[]{:S(2)}) collective-permute-start(f32[24,8,256]{2,1,0:T(8,128)S(1)} %get-tuple-element.48), channel_id=1, source_target_pairs={{0,1},{1,2},{2,3},{3,4},{4,5},{5,6},{6,7},{7,0},{8,9},{9,10},{10,1... | collective-permute-start | bytes 589832 | tf_op jit(solution)/shard_map/ppermute | solution.py:34
  6.8 4.0 %collective-permute-start.1 = (f32[24,8,256]{2,1,0:T(8,128)S(1)}, f32[24,8,256]{2,1,0:T(8,128)S(1)}, u32[]{:S(2)}, u32[]{:S(2)}) collective-permute-start(f32[24,8,256]{2,1,0:T(8,128)S(1)} %get-tuple-element.49), channel_id=1, source_target_pairs={{0,7},{1,0},{2,1},{3,2},{4,3},{5,4},{6,5},{7,6},{8,15},{9,8},{10,9... | collective-permute-start | bytes 589832 | tf_op jit(solution)/shard_map/ppermute | solution.py:34
  10.9 0.0 collective-permute-start.2
  10.9 1.7 %collective-permute-start.3 = (f32[4,8,256]{2,1,0:T(8,128)S(1)}, f32[4,8,256]{2,1,0:T(8,128)S(1)}, u32[]{:S(2)}, u32[]{:S(2)}) collective-permute-start(f32[4,8,256]{2,1,0:T(8,128)S(1)} %get-tuple-element.51), channel_id=1, source_target_pairs={{0,24},{8,0},{16,8},{24,16},{1,25},{9,1},{17,9},{25,17},{2,26},{10... | collective-permute-start | bytes 98312 | tf_op jit(solution)/shard_map/ppermute | solution.py:34
  12.6 0.5 collective-permute-start.4
  13.1 5.6 %collective-permute-done.4 = f32[24,8,128]{2,1,0:T(8,128)S(1)} collective-permute-done((f32[24,8,128]{2,1,0:T(8,128)S(1)}, f32[24,8,128]{2,1,0:T(8,128)S(1)}, u32[]{:S(2)}, u32[]{:S(2)}) %collective-permute-start.4) | collective-permute-done | bytes 98336 | tf_op jit(solution)/shard_map/ppermute | solution.py:433
  18.7 0.0 copy-start.12
  18.8 1.7 %collective-permute-start.5 = (f32[48,8,128]{2,1,0:T(8,128)S(1)}, f32[48,8,128]{2,1,0:T(8,128)S(1)}, u32[]{:S(2)}, u32[]{:S(2)}) collective-permute-start(f32[48,8,128]{2,1,0:T(8,128)S(1)} %constant_dynamic-update-slice_fusion.mine), channel_id=1, source_target_pairs={{0,64},{32,96},{64,128},{96,160},{128,192},{160,224},{192,0},{224,... | collective-permute-start | bytes 589832 | tf_op jit(solution)/shard_map/ppermute | solution.py:437
  20.4 0.0 collective-permute-done.2.xlo
  20.4 2.9 %collective-permute-start.6 = (f32[48,8,128]{2,1,0:T(8,128)S(1)}, f32[48,8,128]{2,1,0:T(8,128)S(1)}, u32[]{:S(2)}, u32[]{:S(2)}) collective-permute-start(f32[48,8,128]{2,1,0:T(8,128)S(1)} %constant_dynamic-update-slice_fusion.mine), channel_id=1, source_target_pairs={{0,128},{32,160},{64,192},{96,224},{128,0},{160,32},{192,64},{224,... | collective-permute-start | bytes 589832 | tf_op jit(solution)/shard_map/ppermute | solution.py:437
  23.3 1.3 %collective-permute-start.7 = (f32[48,8,128]{2,1,0:T(8,128)S(1)}, f32[48,8,128]{2,1,0:T(8,128)S(1)}, u32[]{:S(2)}, u32[]{:S(2)}) collective-permute-start(f32[48,8,128]{2,1,0:T(8,128)S(1)} %constant_dynamic-update-slice_fusion.mine), channel_id=1, source_target_pairs={{0,192},{32,224},{64,0},{96,32},{128,64},{160,96},{192,128},{224,1... | collective-permute-start | bytes 589832 | tf_op jit(solution)/shard_map/ppermute | solution.py:437
  25.4 4.1 %first.1 = (f32[48,8,256]{2,1,0:T(8,128)S(1)}, f32[48,8,256]{2,1,0:T(8,128)S(1)}, f32[48,8,256]{2,1,0:T(8,128)S(1)}, f32[48,8,256]{2,1,0:T(8,128)S(1)}, f32[48,8...) custom-call(f32[1,2]{1,0:T(1,128)S(1)} %copy-done.12, s32[1]{0:T(128)S(6)} %copy.16.source, f32[1,48,8,256]{3,2,1,0:T(8,128)S(1)} %copy-done.4, ...), custom_call_target="tpu_custom_call" | custom-call | tf_op jit(solution)/shard_map/first/pallas_call | solution.py:20
  29.5 1.2 %collective-permute-done.6.from2 = f32[48,8,128]{2,1,0:T(8,128)S(1)} collective-permute-done((f32[48,8,128]{2,1,0:T(8,128)S(1)}, f32[48,8,128]{2,1,0:T(8,128)S(1)}, u32[]{:S(2)}, u32[]{:S(2)}) %collective-permute-start.6) | collective-permute-done | bytes 196640 | tf_op jit(solution)/shard_map/ppermute | solution.py:437
  30.7 2.7 %born.1 = (f32[48,8,256]{2,1,0:T(8,128)S(1)}, f32[48,8,256]{2,1,0:T(8,128)S(1)}, f32[48,8,256]{2,1,0:T(8,128)S(1)}, f32[48,8,256]{2,1,0:T(8,128)S(1)}, f32[48,8,...) custom-call(f32[48,8,128]{2,1,0:T(8,128)S(1)} %constant_dynamic-update-slice_, ...), custom_call_target="tpu_custom_call" | custom-call | tf_op jit(solution)/shard_map/born/pallas_call | solution.py:20
  33.4 0.1 collective-permute-start.8
  33.5 3.2 %collective-permute-start.9 = (f32[48,8,256]{2,1,0:T(8,128)S(1)}, f32[48,8,256]{2,1,0:T(8,128)S(1)}, u32[]{:S(2)}, u32[]{:S(2)}) collective-permute-start(f32[48,8,256]{2,1,0:T(8,128)S(1)} %get-tuple-element.63), channel_id=1, source_target_pairs={{0,7},{1,0},{2,1},{3,2},{4,3},{5,4},{6,5},{7,6},{8,15},{9,8},{10,9... | collective-permute-start | bytes 1179656 | tf_op jit(solution)/shard_map/ppermute | solution.py:34
  36.7 1.7 %collective-permute-start.11 = (f32[8,8,256]{2,1,0:T(8,128)S(1)}, f32[8,8,256]{2,1,0:T(8,128)S(1)}, u32[]{:S(2)}, u32[]{:S(2)}) collective-permute-start(f32[8,8,256]{2,1,0:T(8,128)S(1)} %get-tuple-element.65), channel_id=1, source_target_pairs={{0,24},{8,0},{16,8},{24,16},{1,25},{9,1},{17,9},{25,17},{2,26},{10... | collective-permute-start | bytes 196616 | tf_op jit(solution)/shard_map/ppermute | solution.py:34
  38.5 1.9 %collective-permute-done.10.xlo = f32[8,8,256]{2,1,0:T(8,128)S(1)} collective-permute-done((f32[8,8,256]{2,1,0:T(8,128)S(1)}, f32[8,8,256]{2,1,0:T(8,128)S(1)}, u32[]{:S(2)}, u32[]{:S(2)}) %collective-permute-start.10) | collective-permute-done | bytes 65568 | tf_op jit(solution)/shard_map/ppermute | solution.py:34
  40.4 2.5 %collective-permute-done.8.ylo = f32[48,8,256]{2,1,0:T(8,128)S(1)} collective-permute-done((f32[48,8,256]{2,1,0:T(8,128)S(1)}, f32[48,8,256]{2,1,0:T(8,128)S(1)}, u32[]{:S(2)}, u32[]{:S(2)}) %collective-permute-start.8) | collective-permute-done | bytes 393248 | tf_op jit(solution)/shard_map/ppermute | solution.py:34
  43.0 0.0 copy-start.11
  43.0 4.3 %second.1 = (f32[48,8,256]{2,1,0:T(8,128)S(1)}, f32[48,8,256]{2,1,0:T(8,128)S(1)}, f32[48,8,256]{2,1,0:T(8,128)S(1)}, f32[48,8,256]{2,1,0:T(8,128)S(1)}, f32[48,...) custom-call(f32[1,2]{1,0:T(1,128)S(1)} %copy-done.12, ...), custom_call_target="tpu_custom_call" | custom-call | tf_op jit(solution)/shard_map/second/pallas_call | solution.py:20
  47.2 0.0 copy-start.7
  47.2 0.3 collective-permute-start.12
  47.6 3.0 %collective-permute-start.13 = (f32[24,8,256]{2,1,0:T(8,128)S(1)}, f32[24,8,256]{2,1,0:T(8,128)S(1)}, u32[]{:S(2)}, u32[]{:S(2)}) collective-permute-start(f32[24,8,256]{2,1,0:T(8,128)S(1)} %get-tuple-element.69), channel_id=1, source_target_pairs={{0,7},{1,0},{2,1},{3,2},{4,3},{5,4},{6,5},{7,6},{8,15},{9,8},{10,9... | collective-permute-start | bytes 589832 | tf_op jit(solution)/shard_map/ppermute | solution.py:34
  50.6 0.0 collective-permute-start.14
  50.6 1.7 %collective-permute-start.15 = (f32[4,8,256]{2,1,0:T(8,128)S(1)}, f32[4,8,256]{2,1,0:T(8,128)S(1)}, u32[]{:S(2)}, u32[]{:S(2)}) collective-permute-start(f32[4,8,256]{2,1,0:T(8,128)S(1)} %get-tuple-element.71), channel_id=1, source_target_pairs={{0,24},{8,0},{16,8},{24,16},{1,25},{9,1},{17,9},{25,17},{2,26},{10... | collective-permute-start | bytes 98312 | tf_op jit(solution)/shard_map/ppermute | solution.py:34
  52.3 0.5 counts.1
  52.8 4.4 %adjoint.1 = (f32[48,8,256]{2,1,0:T(8,128)S(1)}, f32[48,8,256]{2,1,0:T(8,128)S(1)}, f32[48,8,256]{2,1,0:T(8,128)S(1)}, f32[48,8,256]{2,1,0:T(8,128)S(1)}) custom-call(f32[1,48,8,256]{3,2,1,0:T(8,128)S(1)} %copy-done.7, f32[48,8,256]{2,1,0:T(8,128)S(1)} %get-tuple-element.54.l1, f32[48,8,256]{2,1,0:T(8,128)S(1)} %get-tuple-element.72.d1, ...), custom_call_target="tpu_custom_call" | custom-call | tf_op jit(solution)/shard_map/adjoint/pallas_call | solution.py:20
  57.3 2.0 %image.1 = (f32[24,8,128]{2,1,0:T(8,128)S(1)}, f32[24,8,128]{2,1,0:T(8,128)S(1)}, f32[24,8,128]{2,1,0:T(8,128)S(1)}, f32[24,8,128]{2,1,0:T(8,128)S(1)}, f32[24,8...) custom-call(f32[48,8,256]{2,1,0:T(8,128)S(1)} %get-tuple-element.66.u2, ...), custom_call_target="tpu_custom_call" | custom-call | tf_op jit(solution)/shard_map/image/pallas_call | solution.py:20
  59.2 2.8 %collective-permute-start.16 = (f32[24,8,128]{2,1,0:T(8,128)S(1)}, f32[24,8,128]{2,1,0:T(8,128)S(1)}, u32[]{:S(2)}, u32[]{:S(2)}) collective-permute-start(f32[24,8,128]{2,1,0:T(8,128)S(1)} %get-tuple-element.82), channel_id=1, source_target_pairs={{0,32},{32,0},{64,96},{96,64},{128,160},{160,128},{192,224},{224,1... | collective-permute-start | bytes 294920 | tf_op jit(solution)/shard_map/ppermute | solution.py:486
  62.0 2.2 %collective-permute-start.17 = (f32[24,8,128]{2,1,0:T(8,128)S(1)}, f32[24,8,128]{2,1,0:T(8,128)S(1)}, u32[]{:S(2)}, u32[]{:S(2)}) collective-permute-start(f32[24,8,128]{2,1,0:T(8,128)S(1)} %get-tuple-element.83), channel_id=1, source_target_pairs={{0,64},{32,96},{64,0},{96,32},{128,192},{160,224},{192,128},{224,1... | collective-permute-start | bytes 294920 | tf_op jit(solution)/shard_map/ppermute | solution.py:486
  64.3 1.3 %collective-permute-start.18 = (f32[24,8,128]{2,1,0:T(8,128)S(1)}, f32[24,8,128]{2,1,0:T(8,128)S(1)}, u32[]{:S(2)}, u32[]{:S(2)}) collective-permute-start(f32[24,8,128]{2,1,0:T(8,128)S(1)} %get-tuple-element.84), channel_id=1, source_target_pairs={{0,96},{32,64},{64,32},{96,0},{128,224},{160,192},{192,160},{224,1... | collective-permute-start | bytes 294920 | tf_op jit(solution)/shard_map/ppermute | solution.py:486
  65.6 1.5 %collective-permute-start.19 = (f32[24,8,128]{2,1,0:T(8,128)S(1)}, f32[24,8,128]{2,1,0:T(8,128)S(1)}, u32[]{:S(2)}, u32[]{:S(2)}) collective-permute-start(f32[24,8,128]{2,1,0:T(8,128)S(1)} %get-tuple-element.85), channel_id=1, source_target_pairs={{0,128},{32,160},{64,192},{96,224},{128,0},{160,32},{192,64},{224,... | collective-permute-start | bytes 294920 | tf_op jit(solution)/shard_map/ppermute | solution.py:486
  67.0 3.1 %collective-permute-start.20 = (f32[24,8,128]{2,1,0:T(8,128)S(1)}, f32[24,8,128]{2,1,0:T(8,128)S(1)}, u32[]{:S(2)}, u32[]{:S(2)}) collective-permute-start(f32[24,8,128]{2,1,0:T(8,128)S(1)} %get-tuple-element.86), channel_id=1, source_target_pairs={{0,160},{32,128},{64,224},{96,192},{128,32},{160,0},{192,96},{224,... | collective-permute-start | bytes 294920 | tf_op jit(solution)/shard_map/ppermute | solution.py:486
  70.2 2.8 %collective-permute-start.21 = (f32[24,8,128]{2,1,0:T(8,128)S(1)}, f32[24,8,128]{2,1,0:T(8,128)S(1)}, u32[]{:S(2)}, u32[]{:S(2)}) collective-permute-start(f32[24,8,128]{2,1,0:T(8,128)S(1)} %get-tuple-element.87), channel_id=1, source_target_pairs={{0,192},{32,224},{64,128},{96,160},{128,64},{160,96},{192,0},{224,... | collective-permute-start | bytes 294920 | tf_op jit(solution)/shard_map/ppermute | solution.py:486
  73.0 1.8 %collective-permute-start.22 = (f32[24,8,128]{2,1,0:T(8,128)S(1)}, f32[24,8,128]{2,1,0:T(8,128)S(1)}, u32[]{:S(2)}, u32[]{:S(2)}) collective-permute-start(f32[24,8,128]{2,1,0:T(8,128)S(1)} %get-tuple-element.88), channel_id=1, source_target_pairs={{0,224},{32,192},{64,160},{96,128},{128,96},{160,64},{192,32},{224... | collective-permute-start | bytes 294920 | tf_op jit(solution)/shard_map/ppermute | solution.py:486
  74.8 1.6 %collective-permute-done.20.rest_5_ = f32[24,8,128]{2,1,0:T(8,128)S(1)} collective-permute-done((f32[24,8,128]{2,1,0:T(8,128)S(1)}, f32[24,8,128]{2,1,0:T(8,128)S(1)}, u32[]{:S(2)}, u32[]{:S(2)}) %collective-permute-start.20) | collective-permute-done | bytes 98336 | tf_op jit(solution)/shard_map/ppermute | solution.py:486
  76.4 1.7 %collective-permute-done.21.rest_6_ = f32[24,8,128]{2,1,0:T(8,128)S(1)} collective-permute-done((f32[24,8,128]{2,1,0:T(8,128)S(1)}, f32[24,8,128]{2,1,0:T(8,128)S(1)}, u32[]{:S(2)}, u32[]{:S(2)}) %collective-permute-start.21) | collective-permute-done | bytes 98336 | tf_op jit(solution)/shard_map/ppermute | solution.py:486
  78.1 3.1 %collective-permute-done.22.rest_7_ = f32[24,8,128]{2,1,0:T(8,128)S(1)} collective-permute-done((f32[24,8,128]{2,1,0:T(8,128)S(1)}, f32[24,8,128]{2,1,0:T(8,128)S(1)}, u32[]{:S(2)}, u32[]{:S(2)}) %collective-permute-start.22) | collective-permute-done | bytes 98336 | tf_op jit(solution)/shard_map/ppermute | solution.py:486
  81.2 0.1 sum.1
  81.4 1.0 %copy.14 = f32[3,48,8,32]{1,3,2,0:T(8,128)} copy(f32[3,48,8,32]{3,2,1,0:T(8,128)S(1)} %sum.1) | data formatting | bytes 294912 | tf_op jit(solution)/shard_map/sum/pallas_call | solution.py:20
  (36 shorter events, 0.1 us)
Async XLA Ops:
  0.0 1.3 %copy-start = (f32[48,8,256]{2,1,0:T(8,128)S(1)}, f32[48,8,256]{2,1,0:T(8,128)}, u32[]{:S(2)}) copy-start(f32[48,8,256]{2,1,0:T(8,128)} %speed.7) | copy-start | bytes 1179652
  0.0 1.3 %copy-start.1 = (f32[48,8,256]{2,1,0:T(8,128)S(1)}, f32[48,8,256]{2,1,0:T(8,128)}, u32[]{:S(2)}) copy-start(f32[48,8,256]{2,1,0:T(8,128)} %epsilon.7) | copy-start | bytes 1179652
  1.4 1.0 %copy-start.2 = (f32[48,8,256]{2,1,0:T(8,128)S(1)}, f32[48,8,256]{2,1,0:T(8,128)}, u32[]{:S(2)}) copy-start(f32[48,8,256]{2,1,0:T(8,128)} %delta.7) | copy-start | bytes 1179652
  2.4 1.0 %copy-start.4 = (f32[1,48,8,256]{3,2,1,0:T(8,128)S(1)}, f32[1,48,8,256]{3,2,1,0:T(8,128)}, u32[]{:S(2)}) copy-start(f32[1,48,8,256]{3,2,1,0:T(8,128)} %u.5) | copy-start | bytes 1179652
  3.3 1.0 %copy-start.6 = (f32[1,48,8,256]{3,2,1,0:T(8,128)S(1)}, f32[1,48,8,256]{3,2,1,0:T(8,128)}, u32[]{:S(2)}) copy-start(f32[1,48,8,256]{3,2,1,0:T(8,128)} %l.5) | copy-start | bytes 1179652
  4.3 21.0 %copy-start.9 = (f32[1,48,8,256]{3,2,1,0:T(8,128)S(1)}, f32[1,48,8,256]{3,2,1,0:T(8,128)}, u32[]{:S(2)}) copy-start(f32[1,48,8,256]{3,2,1,0:T(8,128)} %um.1) | copy-start | bytes 1179652
  4.3 21.0 %copy-start.10 = (f32[1,48,8,256]{3,2,1,0:T(8,128)S(1)}, f32[1,48,8,256]{3,2,1,0:T(8,128)}, u32[]{:S(2)}) copy-start(f32[1,48,8,256]{3,2,1,0:T(8,128)} %lm.1) | copy-start | bytes 1179652
  4.8 20.5 %copy-start.8 = (f32[48,8,256]{2,1,0:T(8,128)S(1)}, f32[48,8,256]{2,1,0:T(8,128)}, u32[]{:S(2)}) copy-start(f32[48,8,256]{2,1,0:T(8,128)} %tilt.5) | copy-start | bytes 1179652
  4.8 20.5 %collective-permute-start = (f32[24,8,256]{2,1,0:T(8,128)S(1)}, f32[24,8,256]{2,1,0:T(8,128)S(1)}, u32[]{:S(2)}, u32[]{:S(2)}) collective-permute-start(f32[24,8,256]{2,1,0:T(8,128)S(1)} %get-tuple-element.48), channel_id=1, source_target_pairs={{0,1},{1,2},{2,3},{3,4},{4,5},{5,6},{6,7},{7,0},{8,9},{9,10},{10,1... | collective-permute-start | bytes 589832 | tf_op jit(solution)/shard_map/ppermute | solution.py:34
  6.8 18.5 %collective-permute-start.1 = (f32[24,8,256]{2,1,0:T(8,128)S(1)}, f32[24,8,256]{2,1,0:T(8,128)S(1)}, u32[]{:S(2)}, u32[]{:S(2)}) collective-permute-start(f32[24,8,256]{2,1,0:T(8,128)S(1)} %get-tuple-element.49), channel_id=1, source_target_pairs={{0,7},{1,0},{2,1},{3,2},{4,3},{5,4},{6,5},{7,6},{8,15},{9,8},{10,9... | collective-permute-start | bytes 589832 | tf_op jit(solution)/shard_map/ppermute | solution.py:34
  10.9 9.5 %collective-permute-start.2 = (f32[4,8,256]{2,1,0:T(8,128)S(1)}, f32[4,8,256]{2,1,0:T(8,128)S(1)}, u32[]{:S(2)}, u32[]{:S(2)}) collective-permute-start(f32[4,8,256]{2,1,0:T(8,128)S(1)} %get-tuple-element.50), channel_id=1, source_target_pairs={{0,8},{8,16},{16,24},{24,0},{1,9},{9,17},{17,25},{25,1},{2,10},{10... | collective-permute-start | bytes 98312 | tf_op jit(solution)/shard_map/ppermute | solution.py:34
  10.9 12.5 %collective-permute-start.3 = (f32[4,8,256]{2,1,0:T(8,128)S(1)}, f32[4,8,256]{2,1,0:T(8,128)S(1)}, u32[]{:S(2)}, u32[]{:S(2)}) collective-permute-start(f32[4,8,256]{2,1,0:T(8,128)S(1)} %get-tuple-element.51), channel_id=1, source_target_pairs={{0,24},{8,0},{16,8},{24,16},{1,25},{9,1},{17,9},{25,17},{2,26},{10... | collective-permute-start | bytes 98312 | tf_op jit(solution)/shard_map/ppermute | solution.py:34
  12.6 6.1 %collective-permute-start.4 = (f32[24,8,128]{2,1,0:T(8,128)S(1)}, f32[24,8,128]{2,1,0:T(8,128)S(1)}, u32[]{:S(2)}, u32[]{:S(2)}) collective-permute-start(f32[24,8,128]{2,1,0:T(8,128)S(1)} %get-tuple-element.53), channel_id=1, source_target_pairs={{0,32},{32,0},{64,96},{96,64},{128,160},{160,128},{192,224},{224,1... | collective-permute-start | bytes 294920 | tf_op jit(solution)/shard_map/ppermute | solution.py:433
  18.7 6.6 %copy-start.12 = (f32[1,2]{1,0:T(1,128)S(1)}, f32[1,2]{1,0:T(1,128)}, u32[]{:S(2)}) copy-start(f32[1,2]{1,0:T(1,128)} %wavelet.3) | copy-start | bytes 28
  18.8 10.8 %collective-permute-start.5 = (f32[48,8,128]{2,1,0:T(8,128)S(1)}, f32[48,8,128]{2,1,0:T(8,128)S(1)}, u32[]{:S(2)}, u32[]{:S(2)}) collective-permute-start(f32[48,8,128]{2,1,0:T(8,128)S(1)} %constant_dynamic-update-slice_fusion.mine), channel_id=1, source_target_pairs={{0,64},{32,96},{64,128},{96,160},{128,192},{160,224},{192,0},{224,... | collective-permute-start | bytes 589832 | tf_op jit(solution)/shard_map/ppermute | solution.py:437
  20.4 10.3 %collective-permute-start.6 = (f32[48,8,128]{2,1,0:T(8,128)S(1)}, f32[48,8,128]{2,1,0:T(8,128)S(1)}, u32[]{:S(2)}, u32[]{:S(2)}) collective-permute-start(f32[48,8,128]{2,1,0:T(8,128)S(1)} %constant_dynamic-update-slice_fusion.mine), channel_id=1, source_target_pairs={{0,128},{32,160},{64,192},{96,224},{128,0},{160,32},{192,64},{224,... | collective-permute-start | bytes 589832 | tf_op jit(solution)/shard_map/ppermute | solution.py:437
  23.3 7.4 %collective-permute-start.7 = (f32[48,8,128]{2,1,0:T(8,128)S(1)}, f32[48,8,128]{2,1,0:T(8,128)S(1)}, u32[]{:S(2)}, u32[]{:S(2)}) collective-permute-start(f32[48,8,128]{2,1,0:T(8,128)S(1)} %constant_dynamic-update-slice_fusion.mine), channel_id=1, source_target_pairs={{0,192},{32,224},{64,0},{96,32},{128,64},{160,96},{192,128},{224,1... | collective-permute-start | bytes 589832 | tf_op jit(solution)/shard_map/ppermute | solution.py:437
  30.7 12.2 %copy-start.3 = (f32[48,8,256]{2,1,0:T(8,128)S(1)}, f32[48,8,256]{2,1,0:T(8,128)}, u32[]{:S(2)}) copy-start(f32[48,8,256]{2,1,0:T(8,128)} %delta.7) | copy-start | bytes 1179652
  30.7 12.2 %copy-start.5 = (f32[1,48,8,256]{3,2,1,0:T(8,128)S(1)}, f32[1,48,8,256]{3,2,1,0:T(8,128)}, u32[]{:S(2)}) copy-start(f32[1,48,8,256]{3,2,1,0:T(8,128)} %u.5) | copy-start | bytes 1179652
  33.4 9.5 %collective-permute-start.8 = (f32[48,8,256]{2,1,0:T(8,128)S(1)}, f32[48,8,256]{2,1,0:T(8,128)S(1)}, u32[]{:S(2)}, u32[]{:S(2)}) collective-permute-start(f32[48,8,256]{2,1,0:T(8,128)S(1)} %get-tuple-element.62), channel_id=1, source_target_pairs={{0,1},{1,2},{2,3},{3,4},{4,5},{5,6},{6,7},{7,0},{8,9},{9,10},{10,1... | collective-permute-start | bytes 1179656 | tf_op jit(solution)/shard_map/ppermute | solution.py:34
  33.5 9.4 %collective-permute-start.9 = (f32[48,8,256]{2,1,0:T(8,128)S(1)}, f32[48,8,256]{2,1,0:T(8,128)S(1)}, u32[]{:S(2)}, u32[]{:S(2)}) collective-permute-start(f32[48,8,256]{2,1,0:T(8,128)S(1)} %get-tuple-element.63), channel_id=1, source_target_pairs={{0,7},{1,0},{2,1},{3,2},{4,3},{5,4},{6,5},{7,6},{8,15},{9,8},{10,9... | collective-permute-start | bytes 1179656 | tf_op jit(solution)/shard_map/ppermute | solution.py:34
  36.7 3.7 %collective-permute-start.10 = (f32[8,8,256]{2,1,0:T(8,128)S(1)}, f32[8,8,256]{2,1,0:T(8,128)S(1)}, u32[]{:S(2)}, u32[]{:S(2)}) collective-permute-start(f32[8,8,256]{2,1,0:T(8,128)S(1)} %get-tuple-element.64), channel_id=1, source_target_pairs={{0,8},{8,16},{16,24},{24,0},{1,9},{9,17},{17,25},{25,1},{2,10},{10... | collective-permute-start | bytes 196616 | tf_op jit(solution)/shard_map/ppermute | solution.py:34
  36.7 3.7 %collective-permute-start.11 = (f32[8,8,256]{2,1,0:T(8,128)S(1)}, f32[8,8,256]{2,1,0:T(8,128)S(1)}, u32[]{:S(2)}, u32[]{:S(2)}) collective-permute-start(f32[8,8,256]{2,1,0:T(8,128)S(1)} %get-tuple-element.65), channel_id=1, source_target_pairs={{0,24},{8,0},{16,8},{24,16},{1,25},{9,1},{17,9},{25,17},{2,26},{10... | collective-permute-start | bytes 196616 | tf_op jit(solution)/shard_map/ppermute | solution.py:34
  43.0 9.3 %copy-start.11 = (s32[1,1536]{1,0:T(1,128)S(1)}, s32[1,1536]{1,0:T(1,128)}, u32[]{:S(2)}) copy-start(s32[1,1536]{1,0:T(1,128)} %cells.1) | copy-start | bytes 18436
  47.2 5.6 %copy-start.7 = (f32[1,48,8,256]{3,2,1,0:T(8,128)S(1)}, f32[1,48,8,256]{3,2,1,0:T(8,128)}, u32[]{:S(2)}) copy-start(f32[1,48,8,256]{3,2,1,0:T(8,128)} %l.5) | copy-start | bytes 1179652
  47.2 10.0 %collective-permute-start.12 = (f32[24,8,256]{2,1,0:T(8,128)S(1)}, f32[24,8,256]{2,1,0:T(8,128)S(1)}, u32[]{:S(2)}, u32[]{:S(2)}) collective-permute-start(f32[24,8,256]{2,1,0:T(8,128)S(1)} %get-tuple-element.68), channel_id=1, source_target_pairs={{0,1},{1,2},{2,3},{3,4},{4,5},{5,6},{6,7},{7,0},{8,9},{9,10},{10,1... | collective-permute-start | bytes 589832 | tf_op jit(solution)/shard_map/ppermute | solution.py:34
  47.6 9.7 %collective-permute-start.13 = (f32[24,8,256]{2,1,0:T(8,128)S(1)}, f32[24,8,256]{2,1,0:T(8,128)S(1)}, u32[]{:S(2)}, u32[]{:S(2)}) collective-permute-start(f32[24,8,256]{2,1,0:T(8,128)S(1)} %get-tuple-element.69), channel_id=1, source_target_pairs={{0,7},{1,0},{2,1},{3,2},{4,3},{5,4},{6,5},{7,6},{8,15},{9,8},{10,9... | collective-permute-start | bytes 589832 | tf_op jit(solution)/shard_map/ppermute | solution.py:34
  50.6 6.7 %collective-permute-start.14 = (f32[4,8,256]{2,1,0:T(8,128)S(1)}, f32[4,8,256]{2,1,0:T(8,128)S(1)}, u32[]{:S(2)}, u32[]{:S(2)}) collective-permute-start(f32[4,8,256]{2,1,0:T(8,128)S(1)} %get-tuple-element.70), channel_id=1, source_target_pairs={{0,8},{8,16},{16,24},{24,0},{1,9},{9,17},{17,25},{25,1},{2,10},{10... | collective-permute-start | bytes 98312 | tf_op jit(solution)/shard_map/ppermute | solution.py:34
  50.6 6.7 %collective-permute-start.15 = (f32[4,8,256]{2,1,0:T(8,128)S(1)}, f32[4,8,256]{2,1,0:T(8,128)S(1)}, u32[]{:S(2)}, u32[]{:S(2)}) collective-permute-start(f32[4,8,256]{2,1,0:T(8,128)S(1)} %get-tuple-element.71), channel_id=1, source_target_pairs={{0,24},{8,0},{16,8},{24,16},{1,25},{9,1},{17,9},{25,17},{2,26},{10... | collective-permute-start | bytes 98312 | tf_op jit(solution)/shard_map/ppermute | solution.py:34
  59.2 11.0 %collective-permute-start.16 = (f32[24,8,128]{2,1,0:T(8,128)S(1)}, f32[24,8,128]{2,1,0:T(8,128)S(1)}, u32[]{:S(2)}, u32[]{:S(2)}) collective-permute-start(f32[24,8,128]{2,1,0:T(8,128)S(1)} %get-tuple-element.82), channel_id=1, source_target_pairs={{0,32},{32,0},{64,96},{96,64},{128,160},{160,128},{192,224},{224,1... | collective-permute-start | bytes 294920 | tf_op jit(solution)/shard_map/ppermute | solution.py:486
  62.0 11.0 %collective-permute-start.17 = (f32[24,8,128]{2,1,0:T(8,128)S(1)}, f32[24,8,128]{2,1,0:T(8,128)S(1)}, u32[]{:S(2)}, u32[]{:S(2)}) collective-permute-start(f32[24,8,128]{2,1,0:T(8,128)S(1)} %get-tuple-element.83), channel_id=1, source_target_pairs={{0,64},{32,96},{64,0},{96,32},{128,192},{160,224},{192,128},{224,1... | collective-permute-start | bytes 294920 | tf_op jit(solution)/shard_map/ppermute | solution.py:486
  64.3 10.5 %collective-permute-start.18 = (f32[24,8,128]{2,1,0:T(8,128)S(1)}, f32[24,8,128]{2,1,0:T(8,128)S(1)}, u32[]{:S(2)}, u32[]{:S(2)}) collective-permute-start(f32[24,8,128]{2,1,0:T(8,128)S(1)} %get-tuple-element.84), channel_id=1, source_target_pairs={{0,96},{32,64},{64,32},{96,0},{128,224},{160,192},{192,160},{224,1... | collective-permute-start | bytes 294920 | tf_op jit(solution)/shard_map/ppermute | solution.py:486
  65.6 9.2 %collective-permute-start.19 = (f32[24,8,128]{2,1,0:T(8,128)S(1)}, f32[24,8,128]{2,1,0:T(8,128)S(1)}, u32[]{:S(2)}, u32[]{:S(2)}) collective-permute-start(f32[24,8,128]{2,1,0:T(8,128)S(1)} %get-tuple-element.85), channel_id=1, source_target_pairs={{0,128},{32,160},{64,192},{96,224},{128,0},{160,32},{192,64},{224,... | collective-permute-start | bytes 294920 | tf_op jit(solution)/shard_map/ppermute | solution.py:486
  67.0 9.4 %collective-permute-start.20 = (f32[24,8,128]{2,1,0:T(8,128)S(1)}, f32[24,8,128]{2,1,0:T(8,128)S(1)}, u32[]{:S(2)}, u32[]{:S(2)}) collective-permute-start(f32[24,8,128]{2,1,0:T(8,128)S(1)} %get-tuple-element.86), channel_id=1, source_target_pairs={{0,160},{32,128},{64,224},{96,192},{128,32},{160,0},{192,96},{224,... | collective-permute-start | bytes 294920 | tf_op jit(solution)/shard_map/ppermute | solution.py:486
  70.2 8.0 %collective-permute-start.21 = (f32[24,8,128]{2,1,0:T(8,128)S(1)}, f32[24,8,128]{2,1,0:T(8,128)S(1)}, u32[]{:S(2)}, u32[]{:S(2)}) collective-permute-start(f32[24,8,128]{2,1,0:T(8,128)S(1)} %get-tuple-element.87), channel_id=1, source_target_pairs={{0,192},{32,224},{64,128},{96,160},{128,64},{160,96},{192,0},{224,... | collective-permute-start | bytes 294920 | tf_op jit(solution)/shard_map/ppermute | solution.py:486
  73.0 8.2 %collective-permute-start.22 = (f32[24,8,128]{2,1,0:T(8,128)S(1)}, f32[24,8,128]{2,1,0:T(8,128)S(1)}, u32[]{:S(2)}, u32[]{:S(2)}) collective-permute-start(f32[24,8,128]{2,1,0:T(8,128)S(1)} %get-tuple-element.88), channel_id=1, source_target_pairs={{0,224},{32,192},{64,160},{96,128},{128,96},{160,64},{192,32},{224... | collective-permute-start | bytes 294920 | tf_op jit(solution)/shard_map/ppermute | solution.py:486

commit v2 on v1

v2 whole, which is shorter than its diff:
```python
import functools

import jax
import jax.numpy as jnp
from jax import lax
from jax.experimental import pallas as pl
from jax.experimental.pallas import tpu as pltpu
from jax.sharding import PartitionSpec as P

F32 = jnp.float32
BF16 = jnp.bfloat16
GROUP = 16
LIMIT = 24 * 1024 * 1024

S0, S1, S2 = -2.5, 4.0 / 3.0, -1.0 / 12.0
D1, D2 = 2.0 / 3.0, -1.0 / 12.0


def call(kernel, outs, ins, scratch=(), smem=(), hbm=(), after=(), name=None):
    place = {**dict.fromkeys(smem, pltpu.SMEM), **dict.fromkeys(hbm, pltpu.HBM)}
    place |= {len(ins) + i: pl.ANY for i in range(len(after))}
    ins = (*ins, *after)
    typed = [out if out[-1] is BF16 else (out, F32) for out in outs]
    return pl.pallas_call(
        kernel,
        out_shape=[jax.ShapeDtypeStruct(*out) for out in typed],
        in_specs=[pl.BlockSpec(memory_space=place.get(i, pltpu.VMEM)) for i in range(len(ins))],
        out_specs=[pl.BlockSpec(memory_space=pltpu.VMEM)] * len(outs),
        scratch_shapes=list(scratch),
        compiler_params=pltpu.CompilerParams(vmem_limit_bytes=LIMIT),
        name=name,
    )(*ins)


def cycle(value, axis, step):
    size = lax.axis_size(axis)
    return lax.ppermute(value, axis, [(i, (i + step) % size) for i in range(size)])


def across(value):
    return lax.ppermute(value, "shot", [(i, i ^ 1) for i in range(8)])


def along(value, step):
    return lax.ppermute(value, "shot", [(i, (i // 2 + step) % 4 * 2 + i % 2) for i in range(8)])


def rows():
    return lax.broadcasted_iota(jnp.int32, (8, 128), 0)


def lanes():
    return lax.broadcasted_iota(jnp.int32, (8, 128), 1)


def pack_y(fields, up, down):
    row = rows()
    nx = fields[0].shape[0]
    for i in range(nx // 2):
        for h in (0, 128):
            tile = pl.ds(h, 128)
            for out, base in ((up, 6), (down, 0)):
                acc = None
                for piece in (0, 1):
                    for f, field in enumerate(fields):
                        at = 4 * piece + 2 * f
                        value = field[i + piece * (nx // 2), :, tile]
                        value = pltpu.roll(value, (at - base) % 8, 0) if at != base else value
                        acc = value if acc is None else jnp.where(row >= at, value, acc)
                out[i, :, tile] = acc


def pack_x(fields, up, down):
    for f, field in enumerate(fields):
        n = field.shape[0]
        up[2 * f : 2 * f + 2] = field[n - 2 : n]
        down[2 * f : 2 * f + 2] = field[0:2]


def fill(pad, field, before, after, f):
    n = field.shape[0]
    gx = lax.axis_index("gx")
    pad[2 : n + 2] = field[...]
    pad[0:2] = jnp.where(gx > 0, before[2 * f : 2 * f + 2], 0.0)
    pad[n + 2 : n + 4] = jnp.where(gx < lax.axis_size("gx") - 1, after[2 * f : 2 * f + 2], 0.0)


def edge_rows(before, after, x, f, half):
    row = rows()
    gy = lax.axis_index("gy")
    first, last = gy > 0, gy < lax.axis_size("gy") - 1
    i, at = x % half, 4 * (x // half) + 2 * f
    out = []
    for t in (0, 1):
        tile = pl.ds(128 * t, 128)
        lower, upper = before[i, :, tile], after[i, :, tile]
        lower = pltpu.roll(lower, (6 - at) % 8, 0) if at != 6 else lower
        upper = pltpu.roll(upper, (-at) % 8, 0) if at != 0 else upper
        out.append(jnp.where((row >= 6) & first, lower, jnp.where((row <= 1) & last, upper, 0.0)))
    return out


def along_z(values, matrix):
    total = None
    for _ in range(3):
        part = values.astype(BF16)
        values = values - part.astype(F32)
        term = jnp.dot(part, matrix, preferred_element_type=F32)
        total = term if total is None else total + term
    return total * (1.0 / 12.0)


def lateral(pad, x, edge, slope=True):
    row = rows()
    horizontal, slopes, centre = [], [], []
    for t in (0, 1):
        tile = pl.ds(128 * t, 128)
        c = pad[x + 2, :, tile]
        xl, xh, xl2, xh2 = (pad[x + k, :, tile] for k in (1, 3, 0, 4))
        e = edge[t]
        yl = pltpu.roll(jnp.where(row == 7, e, c), 1, 0)
        yl2 = pltpu.roll(jnp.where(row >= 6, e, c), 2, 0)
        yh = pltpu.roll(jnp.where(row == 0, e, c), 7, 0)
        yh2 = pltpu.roll(jnp.where(row <= 1, e, c), 6, 0)
        horizontal.append(2.0 * S0 * c + S1 * ((xl + xh) + (yl + yh)) + S2 * ((xl2 + xh2) + (yl2 + yh2)))
        if slope:
            slopes.append(D1 * ((xh - xl) + (yh - yl)) + D2 * ((xh2 - xl2) + (yh2 - yl2)))
        centre.append(c)
    return horizontal, slopes, centre


def slabs(lists):
    return jnp.concatenate([jnp.concatenate(pair, axis=1) for pair in lists], axis=0)


def derivs(pad, before, after, f, zmat, emit):
    nx = pad.shape[0] - 4
    for at in range(0, nx, GROUP):
        found = [lateral(pad, x, edge_rows(before, after, x, f, nx // 2)) for x in range(at, at + GROUP)]
        vertical = along_z(slabs([c for _, _, c in found]), zmat[0])
        mixed = along_z(slabs([s for _, s, _ in found]), zmat[1])
        for j, (horizontal, _, centre) in enumerate(found):
            for t in (0, 1):
                part = (slice(8 * j, 8 * j + 8), slice(128 * t, 128 * t + 128))
                emit(at + j, t, horizontal[t], vertical[part], mixed[part], centre[t])


def second_z(field, zmat, emit):
    for at in range(0, field.shape[0], GROUP):
        vertical = along_z(field[at : at + GROUP].reshape(GROUP * 8, field.shape[2]), zmat[0])
        for j in range(GROUP):
            for t in (0, 1):
                emit(at + j, t, vertical[8 * j : 8 * j + 8, 128 * t : 128 * t + 128])


def operate(model, x, tile, h, v, m):
    s, e, d, k = (w[x, :, tile] for w in model)
    return s * (e * h + d * v) + k * m


def chunk_kernel(p, speed, epsilon, delta, chunk, model, zmat, pbuf, half, sems):
    shot = lax.axis_index("shot")
    lower = pl.ds(pl.multiple_of((shot // 4) * 128, 128), 128)
    copies = [
        pltpu.make_async_copy(array.at[:, :, lower], half.at[k], sems.at[k])
        for k, array in enumerate((speed, epsilon, delta))
    ]
    for copy in copies:
        copy.start()
    depth = zmat.shape[1]
    offset = lax.broadcasted_iota(jnp.int32, (depth, depth), 0) - lax.broadcasted_iota(
        jnp.int32, (depth, depth), 1
    )
    far = jnp.abs(offset)
    second = jnp.where(far == 0, -30.0, jnp.where(far == 1, 16.0, jnp.where(far == 2, -1.0, 0.0)))
    first = jnp.where(far == 1, 8.0, jnp.where(far == 2, -1.0, 0.0))
    zmat[0] = second.astype(BF16)
    zmat[1] = jnp.where(offset > 0, first, -first).astype(BF16)
    pbuf[:, :, :, 0:32] = p[...]
    for copy in copies:
        copy.wait()
    shift = lax.rem(128 - 32 * lax.rem(shot, 4), 128)
    lane = lanes()
    group = p.shape[1] // 4
    for i in range(group):
        parts = [[], []]
        for g in range(4):
            x = g * group + i
            p0, p1, p2 = (pbuf[k, x] for k in range(3))
            s, e, d = (pltpu.roll(half[k, x], shift, 1) for k in range(3))
            for k, w in enumerate((s, e, d)):
                model[k, x] = w
            for f, q in enumerate((p0 * e + s * p1, p0 * d + s * p2)):
                parts[f].append(pltpu.roll(q, 32 * g, 1) if g else q)
        for f in (0, 1):
            a, b, c, d = parts[f]
            chunk[f * group + i] = jnp.where(
                lane < 32, a, jnp.where(lane < 64, b, jnp.where(lane < 96, c, d))
            )


def y_kernel(a, b, *rest):
    pack_y([a, b], *rest[-2:])


def x_kernel(a, b, *rest):
    pack_x([a, b], *rest[-2:])


def first_kernel(
    wavelet, source, zmat, u, um, l, lm, ylo, yhi, xlo, xhi, speed, epsilon, delta, tilt,
    u1, l1, hu, vu, hl, vl, padu, padl,
):
    model = (speed, epsilon, delta, tilt)
    lane = lanes()
    amount, depth = wavelet[0, 0], source[0]
    for f, (pad, w, prev, new, h_out, v_out) in enumerate(
        ((padu, u, um, u1, hu, vu), (padl, l, lm, l1, hl, vl))
    ):
        fill(pad, w.at[0], xlo, xhi, f)

        def emit(x, t, h, v, m, c, f=f, prev=prev, new=new, h_out=h_out, v_out=v_out):
            tile = pl.ds(128 * t, 128)
            h_out[x, :, tile] = h
            v_out[x, :, tile] = v
            value = 2.0 * c - prev[0, x, :, tile] + operate(model, x, tile, h, v, m)
            if f == 0:
                value = value + jnp.where(lane + 128 * t == depth, amount, 0.0)
            new[x, :, tile] = value

        derivs(pad, ylo, yhi, f, zmat, emit)


def born_kernel(
    mine, partner, before, behind, opposite, beside, u1, l1, hu, vu, hl, vl, q1, q2, b1, d1, yup, ydn, xup, xdn, chunks,
):
    shot = lax.axis_index("shot")
    y, xh = shot // 2, lax.rem(shot, 2)
    group = hu.shape[0] // 4
    n = 2 * group
    for k, same, other in (
        (0, mine[...], partner[...]),
        (3, before[...], beside[0:n]),
        (1, behind[...], beside[n : 2 * n]),
        (2, opposite[0:n], opposite[n : 2 * n]),
    ):
        there = lax.rem(y + k, 4) * 2
        chunks[there + xh] = same
        chunks[there + 1 - xh] = other
    lane = lanes()
    for x in range(4 * group):
        g, i = x // group, x % group
        for t in (0, 1):
            tile = pl.ds(128 * t, 128)
            both = []
            for f in (0, 1):
                parts = []
                for k in range(4):
                    part = chunks[4 * t + k, f * group + i]
                    parts.append(pltpu.roll(part, (32 * (k - g)) % 128, 1) if k != g else part)
                a, b, c, d = parts
                both.append(jnp.where(lane < 32, a, jnp.where(lane < 64, b, jnp.where(lane < 96, c, d))))
            q1[x, :, tile], q2[x, :, tile] = both
            b1[x, :, tile] = both[0] * hu[x, :, tile] + both[1] * vu[x, :, tile]
            d1[x, :, tile] = both[0] * hl[x, :, tile] + both[1] * vl[x, :, tile]
    pack_y([u1, b1], yup, ydn)
    pack_x([u1, b1, l1, d1], xup, xdn)


def second_kernel(
    wavelet, source, zmat, u, u1, b1, q1, q2, ylo, yhi, xlo, xhi, speed, epsilon, delta, tilt,
    u2, b2, hu, vu, hb, vb, yup, ydn, xup, xdn, padu, padb,
):
    model = (speed, epsilon, delta, tilt)
    lane = lanes()
    amount, depth = wavelet[0, 1], source[0]
    fill(padu, u1, xlo, xhi, 0)
    fill(padb, b1, xlo, xhi, 1)

    def emit_u(x, t, h, v, m, c):
        tile = pl.ds(128 * t, 128)
        hu[x, :, tile] = h
        vu[x, :, tile] = v
        u2[x, :, tile] = (
            2.0 * c - u[0, x, :, tile] + operate(model, x, tile, h, v, m)
            + jnp.where(lane + 128 * t == depth, amount, 0.0)
        )

    def emit_b(x, t, h, v, m, c):
        tile = pl.ds(128 * t, 128)
        hb[x, :, tile] = h
        vb[x, :, tile] = v
        b2[x, :, tile] = (
            2.0 * c + operate(model, x, tile, h, v, m)
            + (q1[x, :, tile] * hu[x, :, tile] + q2[x, :, tile] * vu[x, :, tile])
        )

    derivs(padu, ylo, yhi, 0, zmat, emit_u)
    derivs(padb, ylo, yhi, 1, zmat, emit_b)
    fields = [u2, b2]
    pack_y(fields, yup, ydn)
    pack_x(fields, xup, xdn)


def counts_kernel(cells, out, *, size_y, depth):
    nx, ny = out.shape[0], out.shape[1]
    gx, gy = lax.axis_index("gx"), lax.axis_index("gy")
    index = cells[...]
    cx = lax.div(index, size_y * depth) - gx * nx
    cy = lax.rem(lax.div(index, depth), size_y) - gy * ny
    cz = lax.rem(index, depth)
    inside = (cx >= 0) & (cx < nx) & (cy >= 0) & (cy < ny)
    place = jnp.where(inside, cx * ny + cy, -1)
    n = index.shape[1]
    left = jnp.where(lax.broadcasted_iota(jnp.int32, (nx * ny, n), 0) == place, 1.0, 0.0).astype(BF16)
    right = jnp.where(lax.broadcasted_iota(jnp.int32, (depth, n), 0) == cz, 1.0, 0.0).astype(BF16)
    total = lax.dot_general(left, right, (((1,), (1,)), ((), ())), preferred_element_type=F32)
    out[...] = total.reshape(nx, ny, depth)


def adjoint_kernel(
    zmat, l, l1, d1, b1, q1, q2, counts, hu, vu, hb, vb, u2, b2, ylo, yhi, xlo, xhi,
    speed, epsilon, delta, tilt, l2, d2, a1, c1, padl, padd, hl, vl,
):
    model = (speed, epsilon, delta, tilt)
    fill(padl, l1, xlo, xhi, 2)
    fill(padd, d1, xlo, xhi, 3)

    def emit_l(x, t, h, v, m, c):
        tile = pl.ds(128 * t, 128)
        hl[x, :, tile] = h
        vl[x, :, tile] = v
        l2[x, :, tile] = 2.0 * c - l[0, x, :, tile] + operate(model, x, tile, h, v, m)

    def emit_d(x, t, h, v, m, c):
        tile = pl.ds(128 * t, 128)
        d2[x, :, tile] = (
            2.0 * c + operate(model, x, tile, h, v, m)
            + (q1[x, :, tile] * hl[x, :, tile] + q2[x, :, tile] * vl[x, :, tile])
            + counts[x, :, tile] * b1[x, :, tile]
        )
        a1[x, :, tile] = hu[x, :, tile] * c + hb[x, :, tile] * l1[x, :, tile]
        c1[x, :, tile] = vu[x, :, tile] * c + vb[x, :, tile] * l1[x, :, tile]

    derivs(padl, ylo, yhi, 0, zmat, emit_l)
    derivs(padd, ylo, yhi, 1, zmat, emit_d)

    for field, other in ((u2, d2), (b2, l2)):

        def add(x, t, v, other=other):
            tile = pl.ds(128 * t, 128)
            c1[x, :, tile] = c1[x, :, tile] + v * other[x, :, tile]

        second_z(field, zmat, add)


def image_kernel(
    u2, b2, ylo, yhi, xlo, xhi, l2, d2, a1, c1, keep, opposite, beside, padu, padb, total, chunks,
):
    for f, (pad, w) in enumerate(((padu, u2), (padb, b2))):
        fill(pad, w, xlo, xhi, f)
    nx = u2.shape[0]
    for x in range(nx):
        hu, hb = (
            lateral(pad, x, edge_rows(ylo, yhi, x, f, nx // 2), False)[0] for f, pad in enumerate((padu, padb))
        )
        for t in (0, 1):
            tile = pl.ds(128 * t, 128)
            total[x, :, tile] = a1[x, :, tile] + hu[t] * d2[x, :, tile] + hb[t] * l2[x, :, tile]
    lane = lanes()
    group = nx // 4
    for i in range(group):
        for f, array in enumerate((total, c1)):
            for t in (0, 1):
                parts = [array[g * group + i, :, pl.ds(128 * t, 128)] for g in range(4)]
                for k in range(4):
                    a, b, c, d = (
                        pltpu.roll(part, (32 * (g - k)) % 128, 1) if g != k else part
                        for g, part in enumerate(parts)
                    )
                    chunks[4 * t + k, f * group + i] = jnp.where(
                        lane < 32, a, jnp.where(lane < 64, b, jnp.where(lane < 96, c, d))
                    )
    shot = lax.axis_index("shot")
    y, xh = shot // 2, lax.rem(shot, 2)

    def chunk_at(step, same):
        return chunks[lax.rem(y + step, 4) * 2 + (xh if same else 1 - xh)]

    for out, wanted in (
        (keep, ((0, True), (0, False), (1, True), (3, True))),
        (opposite, ((2, True), (2, False))),
        (beside, ((1, False), (3, False))),
    ):
        for i, (step, same) in enumerate(wanted):
            out[i] = chunk_at(step, same)


def merge_kernel(keep, opposite, beside, own, other, up, down):
    own[...] = keep[0] + opposite[0]
    other[...] = keep[1] + opposite[1]
    up[...] = keep[2] + beside[0]
    down[...] = keep[3] + beside[1]


def sum_kernel(model, own, other, up, down, out):
    group = out.shape[1] // 4
    for i in range(group):
        sums = []
        for f in (0, 1):
            j = f * group + i
            sums.append((own[j] + other[j]) + (up[j] + down[j]))
        for g in range(4):
            x = g * group + i
            a, c = (pltpu.roll(v, (128 - 32 * g) % 128, 1) if g else v for v in sums)
            s, e, d = (model[k, x] for k in range(3))
            out[0, x] = (e * a + d * c)[:, 0:32]
            out[1, x] = (s * a)[:, 0:32]
            out[2, x] = (s * c)[:, 0:32]


def per_device(
    speed, epsilon, delta, tilt, perturbation, forward_prev, forward_now, adjoint_prev, adjoint_now,
    wavelet, source_cell, receiver_cells,
):
    nx, ny, nz = speed.shape
    whole = (nx, ny, nz)
    pad = pltpu.VMEM((nx + 4, ny, nz), F32)
    half_rows = (nx // 2, ny, nz)
    layers = [half_rows] * 2 + [(4, ny, nz)] * 2
    packed = (nx // 2, ny, 128)
    model = (speed, epsilon, delta, tilt)

    def exchange_y(up, down):
        return cycle(up, "gy", 1), cycle(down, "gy", -1)

    def exchange_x(up, down):
        return cycle(up, "gx", 1), cycle(down, "gx", -1)

    mine, slices, zmat = call(
        chunk_kernel,
        [packed, (3, nx, ny, 128), ((2, nz, nz), BF16)],
        (perturbation, speed, epsilon, delta),
        [pltpu.VMEM((3, nx, ny, 128), F32), pltpu.VMEM((3, nx, ny, 128), F32), pltpu.SemaphoreType.DMA((3,))],
        hbm=(1, 2, 3),
        name="chunk",
    )
    partner, before, behind = across(mine), along(mine, 1), along(mine, -1)
    now = (forward_now[0], adjoint_now[0])
    y0 = exchange_y(*call(y_kernel, layers[:2], now, after=(mine,), name="layers_y"))
    opposite = along(jnp.concatenate([mine, partner], axis=0), 2)
    beside = across(jnp.concatenate([before, behind], axis=0))
    x0 = exchange_x(*call(x_kernel, layers[2:], now, after=y0, name="layers_x"))
    (counts,) = call(
        functools.partial(counts_kernel, size_y=ny * lax.axis_size("gy"), depth=nz),
        [whole],
        (receiver_cells,),
        name="counts",
    )
    u1, l1, hu0, vu0, hl0, vl0 = call(
        first_kernel,
        [whole] * 6,
        (wavelet, source_cell, zmat, forward_now, forward_prev, adjoint_now, adjoint_prev) + y0 + x0 + model,
        [pad, pad],
        (0, 1),
        name="first",
    )
    q1, q2, b1, d1, yup, ydn, xup, xdn = call(
        born_kernel,
        [whole] * 4 + layers[:2] + [(8, ny, nz)] * 2,
        (mine, partner, before, behind, opposite, beside, u1, l1, hu0, vu0, hl0, vl0),
        [pltpu.VMEM((8, nx // 2, ny, 128), F32)],
        name="born",
    )
    y_ub = exchange_y(yup, ydn)
    x1 = exchange_x(xup, xdn)
    y_ld = exchange_y(*call(y_kernel, layers[:2], (l1, d1), name="adjoint_y"))
    u2, b2, hu1, vu1, hb1, vb1, yup, ydn, xup, xdn = call(
        second_kernel,
        [whole] * 6 + layers,
        (wavelet, source_cell, zmat, forward_now, u1, b1, q1, q2) + y_ub + x1 + model,
        [pad, pad],
        (0, 1),
        name="second",
    )
    halo = exchange_y(yup, ydn) + exchange_x(xup, xdn)
    l2, d2, a1, c1 = call(
        adjoint_kernel,
        [whole] * 4,
        (zmat, adjoint_now, l1, d1, b1, q1, q2, counts, hu1, vu1, hb1, vb1, u2, b2) + y_ld + x1 + model,
        [pad, pad, pltpu.VMEM(whole, F32), pltpu.VMEM(whole, F32)],
        name="adjoint",
    )
    keep, opposite, beside = call(
        image_kernel,
        [(4,) + packed, (2,) + packed, (2,) + packed],
        (u2, b2) + halo + (l2, d2, a1, c1),
        [pad, pad, pltpu.VMEM(whole, F32), pltpu.VMEM((8,) + packed, F32)],
        name="image",
    )
    own, other, up, down = call(
        merge_kernel, [packed] * 4, (keep, along(opposite, 2), across(beside)), name="merge"
    )
    (out,) = call(
        sum_kernel,
        [(3, nx, ny, nz // 8)],
        (slices, own, across(other), along(up, 1), along(down, -1)),
        name="sum",
    )
    return out


def solution(mesh):
    placed = (
        P("gx", "gy", None),
        P("gx", "gy", None),
        P("gx", "gy", None),
        P("gx", "gy", None),
        P(None, "gx", "gy", "shot"),
        P("shot", "gx", "gy", None),
        P("shot", "gx", "gy", None),
        P("shot", "gx", "gy", None),
        P("shot", "gx", "gy", None),
        P("shot", None),
        P("shot"),
        P("shot", None),
    )
    return jax.shard_map(
        per_device,
        mesh=mesh,
        in_specs=placed,
        out_specs=P(None, "gx", "gy", "shot"),
        check_vma=False,
    )
```

time: 82.6 us -> 66.9 us (0.81)
  the two profiles are of different devices: /device:TPU:4 before, /device:TPU:32 now
where the time goes in v2:
time: 66.9 us; the launch traced here: 66.4 us
  starting transfers between devices  37.6 us (56%)
  waiting for transfers between devices  13.6 us (20%)
  Pallas kernels  10.9 us (16%)
  local copies, waits for them, and re-layouts  3.34 us (5%)
  between operations  0.91 us (1%)
    ppermute x14, starting transfers between devices, cycle(): lax.ppermute(value, axis, [(i, (i + step) % size) for i in range(size)])  17.5 us
    pallas_call x12, Pallas kernels, call(): pl.pallas_call(kernel, out_shape=[jax.ShapeDtypeStruct(*out) for out in t...  10.9 us
    ppermute x4, starting transfers between devices, across(): return lax.ppermute(value, 'shot', [(i, i ^ 1) for i in range(8)])  10.3 us
    ppermute x6, starting transfers between devices, along(): lax.ppermute(value, 'shot', [(i, (i // 2 + step) % 4 * 2 + i % 2) for i i...  9.86 us
    ppermute x14, waiting for transfers between devices, cycle(): lax.ppermute(value, axis, [(i, (i + step) % size) for i in range(size)])  6.32 us
    ppermute x6, waiting for transfers between devices, along(): lax.ppermute(value, 'shot', [(i, (i // 2 + step) % 4 * 2 + i % 2) for i i...  5.8 us
    unnamed x23, local copies, waits for them, and re-layouts  2.36 us
    ppermute x4, waiting for transfers between devices, across(): return lax.ppermute(value, 'shot', [(i, i ^ 1) for i in range(8)])  1.51 us
  transfers between devices with their start and end apart: 24, of which 8 were waited for; matrix products, arithmetic and copies ran while one was open for 0% of the time, Pallas kernels for 12%

profile of v2, /device:TPU:32, one launch (start us, length us, event | category | flops | bytes accessed | tf_op | source)
XLA Modules:
  0.0 66.4 jit_solution(8363276437627541251)
XLA Ops:
  0.0 1.3 %copy.13.p = f32[3,48,8,32]{3,2,1,0:T(8,128)S(1)} copy(f32[3,48,8,32]{1,3,2,0:T(8,128)} %param.16) | data formatting | bytes 294912 | tf_op args[4]
  1.4 0.0 copy-start.2
  1.4 1.0 %copy-done.2 = f32[48,8,256]{2,1,0:T(8,128)S(1)} copy-done((f32[48,8,256]{2,1,0:T(8,128)S(1)}, f32[48,8,256]{2,1,0:T(8,128)}, u32[]{:S(2)}) %copy-start.2) | copy-done | bytes 393240
  2.4 1.4 %chunk.1 = (f32[24,8,128]{2,1,0:T(8,128)S(1)}, f32[3,48,8,128]{3,2,1,0:T(8,128)S(1)}, bf16[2,256,256]{2,1,0:T(8,128)(2,1)S(1)}) custom-call(f32[3,48,8,32]{3,2,1,0:T(8,128)S(1)} %copy.13.p, f32[48,8,256]{2,1,0:T(8,128)S(1)} %copy-done, f32[48,8,256]{2,1,0:T(8,128)S(1)} %copy-done.1, f32[48,8,256]{2,1,0:T(8,128)S(1)} %copy-done.2), custom_call_target="tpu_custom_call" | custom-call | tf_op jit(solution)/shard_map/chunk/pallas_call | solution.py:24
  3.8 3.1 %collective-permute-start.4 = (f32[24,8,128]{2,1,0:T(8,128)S(1)}, f32[24,8,128]{2,1,0:T(8,128)S(1)}, u32[]{:S(2)}, u32[]{:S(2)}) collective-permute-start(f32[24,8,128]{2,1,0:T(8,128)S(1)} %get-tuple-element.51.rest_0_.mine), channel_id=1, source_target_pairs={{0,32},{32,0},{64,96},{96,64},{128,160},{160,128},{192,224},{224,1... | collective-permute-start | bytes 294920 | tf_op jit(solution)/shard_map/ppermute | solution.py:41
  6.9 1.6 %collective-permute-start.5 = (f32[24,8,128]{2,1,0:T(8,128)S(1)}, f32[24,8,128]{2,1,0:T(8,128)S(1)}, u32[]{:S(2)}, u32[]{:S(2)}) collective-permute-start(f32[24,8,128]{2,1,0:T(8,128)S(1)} %get-tuple-element.51.rest_0_.mine), channel_id=1, source_target_pairs={{0,64},{32,96},{64,128},{96,160},{128,192},{160,224},{192,0},{224,... | collective-permute-start | bytes 294920 | tf_op jit(solution)/shard_map/ppermute | solution.py:45
  8.5 1.7 %collective-permute-start.6 = (f32[24,8,128]{2,1,0:T(8,128)S(1)}, f32[24,8,128]{2,1,0:T(8,128)S(1)}, u32[]{:S(2)}, u32[]{:S(2)}) collective-permute-start(f32[24,8,128]{2,1,0:T(8,128)S(1)} %get-tuple-element.51.rest_0_.mine), channel_id=1, source_target_pairs={{0,192},{32,224},{64,0},{96,32},{128,64},{160,96},{192,128},{224,1... | collective-permute-start | bytes 294920 | tf_op jit(solution)/shard_map/ppermute | solution.py:45
  10.1 0.1 layers_y.1
  10.2 2.0 %collective-permute-start = (f32[24,8,256]{2,1,0:T(8,128)S(1)}, f32[24,8,256]{2,1,0:T(8,128)S(1)}, u32[]{:S(2)}, u32[]{:S(2)}) collective-permute-start(f32[24,8,256]{2,1,0:T(8,128)S(1)} %get-tuple-element.52), channel_id=1, source_target_pairs={{0,1},{1,2},{2,3},{3,4},{4,5},{5,6},{6,7},{7,0},{8,9},{9,10},{10,1... | collective-permute-start | bytes 589832 | tf_op jit(solution)/shard_map/ppermute | solution.py:37
  12.2 0.1 collective-permute-start.1
  12.3 2.1 %collective-permute-start.7 = (f32[48,8,128]{2,1,0:T(8,128)S(1)}, f32[48,8,128]{2,1,0:T(8,128)S(1)}, u32[]{:S(2)}, u32[]{:S(2)}) collective-permute-start(f32[48,8,128]{2,1,0:T(8,128)S(1)} %pad_maximum_fusion), channel_id=1, source_target_pairs={{0,128},{32,160},{64,192},{96,224},{128,0},{160,32},{192,64},{224,... | collective-permute-start | bytes 589832 | tf_op jit(solution)/shard_map/ppermute | solution.py:45
  14.4 0.0 copy-start.3
  14.4 0.0 copy-start.6
  14.5 0.0 copy-start.7
  14.5 2.0 %collective-permute-start.8 = (f32[48,8,128]{2,1,0:T(8,128)S(1)}, f32[48,8,128]{2,1,0:T(8,128)S(1)}, u32[]{:S(2)}, u32[]{:S(2)}) collective-permute-start(f32[48,8,128]{2,1,0:T(8,128)S(1)} %pad_maximum_fusion.1), channel_id=1, source_target_pairs={{0,32},{32,0},{64,96},{96,64},{128,160},{160,128},{192,224},{224,1... | collective-permute-start | bytes 589832 | tf_op jit(solution)/shard_map/ppermute | solution.py:41
  16.5 1.5 %collective-permute-done.1.rest_1_.yhi = f32[24,8,256]{2,1,0:T(8,128)S(1)} collective-permute-done((f32[24,8,256]{2,1,0:T(8,128)S(1)}, f32[24,8,256]{2,1,0:T(8,128)S(1)}, u32[]{:S(2)}, u32[]{:S(2)}) %collective-permute-start.1) | collective-permute-done | bytes 196640 | tf_op jit(solution)/shard_map/ppermute | solution.py:37
  18.0 1.7 %collective-permute-start.3 = (f32[4,8,256]{2,1,0:T(8,128)S(1)}, f32[4,8,256]{2,1,0:T(8,128)S(1)}, u32[]{:S(2)}, u32[]{:S(2)}) collective-permute-start(f32[4,8,256]{2,1,0:T(8,128)S(1)} %get-tuple-element.55), channel_id=1, source_target_pairs={{0,24},{8,0},{16,8},{24,16},{1,25},{9,1},{17,9},{25,17},{2,26},{10... | collective-permute-start | bytes 98312 | tf_op jit(solution)/shard_map/ppermute | solution.py:37
  20.4 0.0 copy-start.10
  20.4 0.9 %collective-permute-done.2.xlo = f32[4,8,256]{2,1,0:T(8,128)S(1)} collective-permute-done((f32[4,8,256]{2,1,0:T(8,128)S(1)}, f32[4,8,256]{2,1,0:T(8,128)S(1)}, u32[]{:S(2)}, u32[]{:S(2)}) %collective-permute-start.2) | collective-permute-done | bytes 32800 | tf_op jit(solution)/shard_map/ppermute | solution.py:37
  21.3 0.0 collective-permute-done.3.xhi
  21.3 2.3 %first.1 = (f32[48,8,256]{2,1,0:T(8,128)S(1)}, f32[48,8,256]{2,1,0:T(8,128)S(1)}, f32[48,8,256]{2,1,0:T(8,128)S(1)}, f32[48,8,256]{2,1,0:T(8,128)S(1)}, f32[48,8...) custom-call(f32[1,2]{1,0:T(1,128)S(1)} %copy-done.10, s32[1]{0:T(128)S(6)} %copy.15.source, ...), custom_call_target="tpu_custom_call" | custom-call | tf_op jit(solution)/shard_map/first/pallas_call | solution.py:24
  23.7 0.8 %born.1 = (f32[48,8,256]{2,1,0:T(8,128)S(1)}, f32[48,8,256]{2,1,0:T(8,128)S(1)}, f32[48,8,256]{2,1,0:T(8,128)S(1)}, f32[48,8,256]{2,1,0:T(8,128)S(1)}, f32[24,8,...) custom-call(f32[24,8,128]{2,1,0:T(8,128)S(1)} %get-tuple-element.51.rest_0_.m, ...), custom_call_target="tpu_custom_call" | custom-call | tf_op jit(solution)/shard_map/born/pallas_call | solution.py:24
  24.4 3.2 %collective-permute-start.9 = (f32[24,8,256]{2,1,0:T(8,128)S(1)}, f32[24,8,256]{2,1,0:T(8,128)S(1)}, u32[]{:S(2)}, u32[]{:S(2)}) collective-permute-start(f32[24,8,256]{2,1,0:T(8,128)S(1)} %get-tuple-element.65), channel_id=1, source_target_pairs={{0,1},{1,2},{2,3},{3,4},{4,5},{5,6},{6,7},{7,0},{8,9},{9,10},{10,1... | collective-permute-start | bytes 589832 | tf_op jit(solution)/shard_map/ppermute | solution.py:37
  27.6 0.4 collective-permute-start.11
  28.1 1.3 %collective-permute-start.12 = (f32[8,8,256]{2,1,0:T(8,128)S(1)}, f32[8,8,256]{2,1,0:T(8,128)S(1)}, u32[]{:S(2)}, u32[]{:S(2)}) collective-permute-start(f32[8,8,256]{2,1,0:T(8,128)S(1)} %get-tuple-element.68), channel_id=1, source_target_pairs={{0,24},{8,0},{16,8},{24,16},{1,25},{9,1},{17,9},{25,17},{2,26},{10... | collective-permute-start | bytes 196616 | tf_op jit(solution)/shard_map/ppermute | solution.py:37
  29.4 0.1 adjoint_y.1
  29.5 3.1 %collective-permute-start.17 = (f32[24,8,256]{2,1,0:T(8,128)S(1)}, f32[24,8,256]{2,1,0:T(8,128)S(1)}, u32[]{:S(2)}, u32[]{:S(2)}) collective-permute-start(f32[24,8,256]{2,1,0:T(8,128)S(1)} %get-tuple-element.80), channel_id=1, source_target_pairs={{0,1},{1,2},{2,3},{3,4},{4,5},{5,6},{6,7},{7,0},{8,9},{9,10},{10,1... | collective-permute-start | bytes 589832 | tf_op jit(solution)/shard_map/ppermute | solution.py:37
  32.6 1.7 %collective-permute-start.18 = (f32[24,8,256]{2,1,0:T(8,128)S(1)}, f32[24,8,256]{2,1,0:T(8,128)S(1)}, u32[]{:S(2)}, u32[]{:S(2)}) collective-permute-start(f32[24,8,256]{2,1,0:T(8,128)S(1)} %get-tuple-element.81), channel_id=1, source_target_pairs={{0,7},{1,0},{2,1},{3,2},{4,3},{5,4},{6,5},{7,6},{8,15},{9,8},{10,9... | collective-permute-start | bytes 589832 | tf_op jit(solution)/shard_map/ppermute | solution.py:37
  34.3 2.1 %collective-permute-done.10.yhi = f32[24,8,256]{2,1,0:T(8,128)S(1)} collective-permute-done((f32[24,8,256]{2,1,0:T(8,128)S(1)}, f32[24,8,256]{2,1,0:T(8,128)S(1)}, u32[]{:S(2)}, u32[]{:S(2)}) %collective-permute-start.10) | collective-permute-done | bytes 196640 | tf_op jit(solution)/shard_map/ppermute | solution.py:37
  36.4 2.4 %second.1 = (f32[48,8,256]{2,1,0:T(8,128)S(1)}, f32[48,8,256]{2,1,0:T(8,128)S(1)}, f32[48,8,256]{2,1,0:T(8,128)S(1)}, f32[48,8,256]{2,1,0:T(8,128)S(1)}, f32[48,...) custom-call(f32[1,2]{1,0:T(1,128)S(1)} %copy-done.10, ...), custom_call_target="tpu_custom_call" | custom-call | tf_op jit(solution)/shard_map/second/pallas_call | solution.py:24
  38.9 2.0 %collective-permute-start.13 = (f32[24,8,256]{2,1,0:T(8,128)S(1)}, f32[24,8,256]{2,1,0:T(8,128)S(1)}, u32[]{:S(2)}, u32[]{:S(2)}) collective-permute-start(f32[24,8,256]{2,1,0:T(8,128)S(1)} %get-tuple-element.71), channel_id=1, source_target_pairs={{0,1},{1,2},{2,3},{3,4},{4,5},{5,6},{6,7},{7,0},{8,9},{9,10},{10,1... | collective-permute-start | bytes 589832 | tf_op jit(solution)/shard_map/ppermute | solution.py:37
  40.9 0.1 collective-permute-start.14
  41.0 1.7 %collective-permute-start.16 = (f32[4,8,256]{2,1,0:T(8,128)S(1)}, f32[4,8,256]{2,1,0:T(8,128)S(1)}, u32[]{:S(2)}, u32[]{:S(2)}) collective-permute-start(f32[4,8,256]{2,1,0:T(8,128)S(1)} %get-tuple-element.74), channel_id=1, source_target_pairs={{0,24},{8,0},{16,8},{24,16},{1,25},{9,1},{17,9},{25,17},{2,26},{10... | collective-permute-start | bytes 98312 | tf_op jit(solution)/shard_map/ppermute | solution.py:37
  42.7 0.5 counts.1
  43.3 2.3 %adjoint.1 = (f32[48,8,256]{2,1,0:T(8,128)S(1)}, f32[48,8,256]{2,1,0:T(8,128)S(1)}, f32[48,8,256]{2,1,0:T(8,128)S(1)}, f32[48,8,256]{2,1,0:T(8,128)S(1)}) custom-call(bf16[2,256,256]{2,1,0:T(8,128)(2,1)S(1)} %get-tuple-element.50.zmat, f32[1,48,8,256]{3,2,1,0:T(8,128)S(1)} %copy-done.4, f32[48,8,256]{2,1,0:T(8,128)S(1)} %get-tuple-element.57.l1.a, ...), custom_call_target="tpu_custom_call" | custom-call | tf_op jit(solution)/shard_map/adjoint/pallas_call | solution.py:24
  45.6 1.8 %collective-permute-done.14.yhi = f32[24,8,256]{2,1,0:T(8,128)S(1)} collective-permute-done((f32[24,8,256]{2,1,0:T(8,128)S(1)}, f32[24,8,256]{2,1,0:T(8,128)S(1)}, u32[]{:S(2)}, u32[]{:S(2)}) %collective-permute-start.14) | collective-permute-done | bytes 196640 | tf_op jit(solution)/shard_map/ppermute | solution.py:37
  47.4 0.9 %image.1 = (f32[4,24,8,128]{3,2,1,0:T(8,128)S(1)}, f32[2,24,8,128]{3,2,1,0:T(8,128)S(1)}, f32[2,24,8,128]{3,2,1,0:T(8,128)S(1)}) custom-call(f32[48,8,256]{2,1,0:T(8,128)S(1)} %get-tuple-element.69.u2, f32[48,8,256]{2,1,0:T(8,128)S(1)} %get-tuple-element.70.b2, f32[24,8,256]{2,1,0:T(8,128)S(1)} %collective-permute-done.13.ylo, ...), custom_call_target="tpu_custom_call" | custom-call | tf_op jit(solution)/shard_map/image/pallas_call | solution.py:24
  48.2 1.3 %collective-permute-start.19 = (f32[2,24,8,128]{3,2,1,0:T(8,128)S(1)}, f32[2,24,8,128]{3,2,1,0:T(8,128)S(1)}, u32[]{:S(2)}, u32[]{:S(2)}) collective-permute-start(f32[2,24,8,128]{3,2,1,0:T(8,128)S(1)} %get-tuple-element.87), channel_id=1, source_target_pairs={{0,128},{32,160},{64,192},{96,224},{128,0},{160,32},{192,64},{224,... | collective-permute-start | bytes 589832 | tf_op jit(solution)/shard_map/ppermute | solution.py:45
  49.5 2.5 %collective-permute-start.20 = (f32[2,24,8,128]{3,2,1,0:T(8,128)S(1)}, f32[2,24,8,128]{3,2,1,0:T(8,128)S(1)}, u32[]{:S(2)}, u32[]{:S(2)}) collective-permute-start(f32[2,24,8,128]{3,2,1,0:T(8,128)S(1)} %get-tuple-element.88), channel_id=1, source_target_pairs={{0,32},{32,0},{64,96},{96,64},{128,160},{160,128},{192,224},{224,1... | collective-permute-start | bytes 589832 | tf_op jit(solution)/shard_map/ppermute | solution.py:41
  52.0 3.5 %collective-permute-done.19.opposite = f32[2,24,8,128]{3,2,1,0:T(8,128)S(1)} collective-permute-done((f32[2,24,8,128]{3,2,1,0:T(8,128)S(1)}, f32[2,24,8,128]{3,2,1,0:T(8,128)S(1)}, u32[]{:S(2)}, u32[]{:S(2)}) %collective-permute-start.19) | collective-permute-done | bytes 196640 | tf_op jit(solution)/shard_map/ppermute | solution.py:45
  55.5 1.2 %collective-permute-done.20.beside = f32[2,24,8,128]{3,2,1,0:T(8,128)S(1)} collective-permute-done((f32[2,24,8,128]{3,2,1,0:T(8,128)S(1)}, f32[2,24,8,128]{3,2,1,0:T(8,128)S(1)}, u32[]{:S(2)}, u32[]{:S(2)}) %collective-permute-start.20) | collective-permute-done | bytes 196640 | tf_op jit(solution)/shard_map/ppermute | solution.py:41
  56.8 2.7 %collective-permute-start.21 = (f32[24,8,128]{2,1,0:T(8,128)S(1)}, f32[24,8,128]{2,1,0:T(8,128)S(1)}, u32[]{:S(2)}, u32[]{:S(2)}) collective-permute-start(f32[24,8,128]{2,1,0:T(8,128)S(1)} %get-tuple-element.90), channel_id=1, source_target_pairs={{0,32},{32,0},{64,96},{96,64},{128,160},{160,128},{192,224},{224,1... | collective-permute-start | bytes 294920 | tf_op jit(solution)/shard_map/ppermute | solution.py:41
  59.5 0.4 collective-permute-start.22
  59.8 2.9 %collective-permute-start.23 = (f32[24,8,128]{2,1,0:T(8,128)S(1)}, f32[24,8,128]{2,1,0:T(8,128)S(1)}, u32[]{:S(2)}, u32[]{:S(2)}) collective-permute-start(f32[24,8,128]{2,1,0:T(8,128)S(1)} %get-tuple-element.92), channel_id=1, source_target_pairs={{0,192},{32,224},{64,0},{96,32},{128,64},{160,96},{192,128},{224,1... | collective-permute-start | bytes 294920 | tf_op jit(solution)/shard_map/ppermute | solution.py:45
  62.7 0.3 collective-permute-done.21.other
  63.0 2.3 %collective-permute-done.22.up = f32[24,8,128]{2,1,0:T(8,128)S(1)} collective-permute-done((f32[24,8,128]{2,1,0:T(8,128)S(1)}, f32[24,8,128]{2,1,0:T(8,128)S(1)}, u32[]{:S(2)}, u32[]{:S(2)}) %collective-permute-start.22) | collective-permute-done | bytes 98336 | tf_op jit(solution)/shard_map/ppermute | solution.py:45
  65.3 0.1 sum.1
  65.5 1.0 %copy.14 = f32[3,48,8,32]{1,3,2,0:T(8,128)} copy(f32[3,48,8,32]{3,2,1,0:T(8,128)S(1)} %sum.1) | data formatting | bytes 294912 | tf_op jit(solution)/shard_map/sum/pallas_call | solution.py:24
  (38 shorter events, 0.2 us)
Async XLA Ops:
  0.0 1.3 %copy-start = (f32[48,8,256]{2,1,0:T(8,128)S(1)}, f32[48,8,256]{2,1,0:T(8,128)}, u32[]{:S(2)}) copy-start(f32[48,8,256]{2,1,0:T(8,128)} %speed.7) | copy-start | bytes 1179652
  0.0 1.3 %copy-start.1 = (f32[48,8,256]{2,1,0:T(8,128)S(1)}, f32[48,8,256]{2,1,0:T(8,128)}, u32[]{:S(2)}) copy-start(f32[48,8,256]{2,1,0:T(8,128)} %epsilon.7) | copy-start | bytes 1179652
  1.4 1.0 %copy-start.2 = (f32[48,8,256]{2,1,0:T(8,128)S(1)}, f32[48,8,256]{2,1,0:T(8,128)}, u32[]{:S(2)}) copy-start(f32[48,8,256]{2,1,0:T(8,128)} %delta.7) | copy-start | bytes 1179652
  2.4 7.8 %copy-start.4 = (f32[1,48,8,256]{3,2,1,0:T(8,128)S(1)}, f32[1,48,8,256]{3,2,1,0:T(8,128)}, u32[]{:S(2)}) copy-start(f32[1,48,8,256]{3,2,1,0:T(8,128)} %l.3) | copy-start | bytes 1179652
  2.4 7.8 %copy-start.5 = (f32[1,48,8,256]{3,2,1,0:T(8,128)S(1)}, f32[1,48,8,256]{3,2,1,0:T(8,128)}, u32[]{:S(2)}) copy-start(f32[1,48,8,256]{3,2,1,0:T(8,128)} %u.3) | copy-start | bytes 1179652
  3.8 8.5 %collective-permute-start.4 = (f32[24,8,128]{2,1,0:T(8,128)S(1)}, f32[24,8,128]{2,1,0:T(8,128)S(1)}, u32[]{:S(2)}, u32[]{:S(2)}) collective-permute-start(f32[24,8,128]{2,1,0:T(8,128)S(1)} %get-tuple-element.51.rest_0_.mine), channel_id=1, source_target_pairs={{0,32},{32,0},{64,96},{96,64},{128,160},{160,128},{192,224},{224,1... | collective-permute-start | bytes 294920 | tf_op jit(solution)/shard_map/ppermute | solution.py:41
  6.9 7.5 %collective-permute-start.5 = (f32[24,8,128]{2,1,0:T(8,128)S(1)}, f32[24,8,128]{2,1,0:T(8,128)S(1)}, u32[]{:S(2)}, u32[]{:S(2)}) collective-permute-start(f32[24,8,128]{2,1,0:T(8,128)S(1)} %get-tuple-element.51.rest_0_.mine), channel_id=1, source_target_pairs={{0,64},{32,96},{64,128},{96,160},{128,192},{160,224},{192,0},{224,... | collective-permute-start | bytes 294920 | tf_op jit(solution)/shard_map/ppermute | solution.py:45
  8.5 6.0 %collective-permute-start.6 = (f32[24,8,128]{2,1,0:T(8,128)S(1)}, f32[24,8,128]{2,1,0:T(8,128)S(1)}, u32[]{:S(2)}, u32[]{:S(2)}) collective-permute-start(f32[24,8,128]{2,1,0:T(8,128)S(1)} %get-tuple-element.51.rest_0_.mine), channel_id=1, source_target_pairs={{0,192},{32,224},{64,0},{96,32},{128,64},{160,96},{192,128},{224,1... | collective-permute-start | bytes 294920 | tf_op jit(solution)/shard_map/ppermute | solution.py:45
  10.2 6.3 %collective-permute-start = (f32[24,8,256]{2,1,0:T(8,128)S(1)}, f32[24,8,256]{2,1,0:T(8,128)S(1)}, u32[]{:S(2)}, u32[]{:S(2)}) collective-permute-start(f32[24,8,256]{2,1,0:T(8,128)S(1)} %get-tuple-element.52), channel_id=1, source_target_pairs={{0,1},{1,2},{2,3},{3,4},{4,5},{5,6},{6,7},{7,0},{8,9},{9,10},{10,1... | collective-permute-start | bytes 589832 | tf_op jit(solution)/shard_map/ppermute | solution.py:37
  12.2 5.8 %collective-permute-start.1 = (f32[24,8,256]{2,1,0:T(8,128)S(1)}, f32[24,8,256]{2,1,0:T(8,128)S(1)}, u32[]{:S(2)}, u32[]{:S(2)}) collective-permute-start(f32[24,8,256]{2,1,0:T(8,128)S(1)} %get-tuple-element.53), channel_id=1, source_target_pairs={{0,7},{1,0},{2,1},{3,2},{4,3},{5,4},{6,5},{7,6},{8,15},{9,8},{10,9... | collective-permute-start | bytes 589832 | tf_op jit(solution)/shard_map/ppermute | solution.py:37
  12.3 11.3 %collective-permute-start.7 = (f32[48,8,128]{2,1,0:T(8,128)S(1)}, f32[48,8,128]{2,1,0:T(8,128)S(1)}, u32[]{:S(2)}, u32[]{:S(2)}) collective-permute-start(f32[48,8,128]{2,1,0:T(8,128)S(1)} %pad_maximum_fusion), channel_id=1, source_target_pairs={{0,128},{32,160},{64,192},{96,224},{128,0},{160,32},{192,64},{224,... | collective-permute-start | bytes 589832 | tf_op jit(solution)/shard_map/ppermute | solution.py:45
  14.4 6.9 %copy-start.8 = (f32[1,48,8,256]{3,2,1,0:T(8,128)S(1)}, f32[1,48,8,256]{3,2,1,0:T(8,128)}, u32[]{:S(2)}) copy-start(f32[1,48,8,256]{3,2,1,0:T(8,128)} %lm.1) | copy-start | bytes 1179652
  14.4 6.9 %copy-start.3 = (f32[48,8,256]{2,1,0:T(8,128)S(1)}, f32[48,8,256]{2,1,0:T(8,128)}, u32[]{:S(2)}) copy-start(f32[48,8,256]{2,1,0:T(8,128)} %delta.7) | copy-start | bytes 1179652
  14.4 6.9 %copy-start.6 = (f32[48,8,256]{2,1,0:T(8,128)S(1)}, f32[48,8,256]{2,1,0:T(8,128)}, u32[]{:S(2)}) copy-start(f32[48,8,256]{2,1,0:T(8,128)} %tilt.5) | copy-start | bytes 1179652
  14.5 6.9 %copy-start.7 = (f32[1,48,8,256]{3,2,1,0:T(8,128)S(1)}, f32[1,48,8,256]{3,2,1,0:T(8,128)}, u32[]{:S(2)}) copy-start(f32[1,48,8,256]{3,2,1,0:T(8,128)} %um.1) | copy-start | bytes 1179652
  14.5 9.2 %collective-permute-start.8 = (f32[48,8,128]{2,1,0:T(8,128)S(1)}, f32[48,8,128]{2,1,0:T(8,128)S(1)}, u32[]{:S(2)}, u32[]{:S(2)}) collective-permute-start(f32[48,8,128]{2,1,0:T(8,128)S(1)} %pad_maximum_fusion.1), channel_id=1, source_target_pairs={{0,32},{32,0},{64,96},{96,64},{128,160},{160,128},{192,224},{224,1... | collective-permute-start | bytes 589832 | tf_op jit(solution)/shard_map/ppermute | solution.py:41
  18.0 3.3 %collective-permute-start.2 = (f32[4,8,256]{2,1,0:T(8,128)S(1)}, f32[4,8,256]{2,1,0:T(8,128)S(1)}, u32[]{:S(2)}, u32[]{:S(2)}) collective-permute-start(f32[4,8,256]{2,1,0:T(8,128)S(1)} %get-tuple-element.54), channel_id=1, source_target_pairs={{0,8},{8,16},{16,24},{24,0},{1,9},{9,17},{17,25},{25,1},{2,10},{10... | collective-permute-start | bytes 98312 | tf_op jit(solution)/shard_map/ppermute | solution.py:37
  18.0 3.3 %collective-permute-start.3 = (f32[4,8,256]{2,1,0:T(8,128)S(1)}, f32[4,8,256]{2,1,0:T(8,128)S(1)}, u32[]{:S(2)}, u32[]{:S(2)}) collective-permute-start(f32[4,8,256]{2,1,0:T(8,128)S(1)} %get-tuple-element.55), channel_id=1, source_target_pairs={{0,24},{8,0},{16,8},{24,16},{1,25},{9,1},{17,9},{25,17},{2,26},{10... | collective-permute-start | bytes 98312 | tf_op jit(solution)/shard_map/ppermute | solution.py:37
  20.4 1.0 %copy-start.10 = (f32[1,2]{1,0:T(1,128)S(1)}, f32[1,2]{1,0:T(1,128)}, u32[]{:S(2)}) copy-start(f32[1,2]{1,0:T(1,128)} %wavelet.3) | copy-start | bytes 28
  24.4 9.9 %collective-permute-start.9 = (f32[24,8,256]{2,1,0:T(8,128)S(1)}, f32[24,8,256]{2,1,0:T(8,128)S(1)}, u32[]{:S(2)}, u32[]{:S(2)}) collective-permute-start(f32[24,8,256]{2,1,0:T(8,128)S(1)} %get-tuple-element.65), channel_id=1, source_target_pairs={{0,1},{1,2},{2,3},{3,4},{4,5},{5,6},{6,7},{7,0},{8,9},{9,10},{10,1... | collective-permute-start | bytes 589832 | tf_op jit(solution)/shard_map/ppermute | solution.py:37
  27.6 8.8 %collective-permute-start.10 = (f32[24,8,256]{2,1,0:T(8,128)S(1)}, f32[24,8,256]{2,1,0:T(8,128)S(1)}, u32[]{:S(2)}, u32[]{:S(2)}) collective-permute-start(f32[24,8,256]{2,1,0:T(8,128)S(1)} %get-tuple-element.66), channel_id=1, source_target_pairs={{0,7},{1,0},{2,1},{3,2},{4,3},{5,4},{6,5},{7,6},{8,15},{9,8},{10,9... | collective-permute-start | bytes 589832 | tf_op jit(solution)/shard_map/ppermute | solution.py:37
  27.6 5.0 %collective-permute-start.11 = (f32[8,8,256]{2,1,0:T(8,128)S(1)}, f32[8,8,256]{2,1,0:T(8,128)S(1)}, u32[]{:S(2)}, u32[]{:S(2)}) collective-permute-start(f32[8,8,256]{2,1,0:T(8,128)S(1)} %get-tuple-element.67), channel_id=1, source_target_pairs={{0,8},{8,16},{16,24},{24,0},{1,9},{9,17},{17,25},{25,1},{2,10},{10... | collective-permute-start | bytes 196616 | tf_op jit(solution)/shard_map/ppermute | solution.py:37
  28.1 6.3 %collective-permute-start.12 = (f32[8,8,256]{2,1,0:T(8,128)S(1)}, f32[8,8,256]{2,1,0:T(8,128)S(1)}, u32[]{:S(2)}, u32[]{:S(2)}) collective-permute-start(f32[8,8,256]{2,1,0:T(8,128)S(1)} %get-tuple-element.68), channel_id=1, source_target_pairs={{0,24},{8,0},{16,8},{24,16},{1,25},{9,1},{17,9},{25,17},{2,26},{10... | collective-permute-start | bytes 196616 | tf_op jit(solution)/shard_map/ppermute | solution.py:37
  29.5 11.5 %collective-permute-start.17 = (f32[24,8,256]{2,1,0:T(8,128)S(1)}, f32[24,8,256]{2,1,0:T(8,128)S(1)}, u32[]{:S(2)}, u32[]{:S(2)}) collective-permute-start(f32[24,8,256]{2,1,0:T(8,128)S(1)} %get-tuple-element.80), channel_id=1, source_target_pairs={{0,1},{1,2},{2,3},{3,4},{4,5},{5,6},{6,7},{7,0},{8,9},{9,10},{10,1... | collective-permute-start | bytes 589832 | tf_op jit(solution)/shard_map/ppermute | solution.py:37
  32.6 10.7 %collective-permute-start.18 = (f32[24,8,256]{2,1,0:T(8,128)S(1)}, f32[24,8,256]{2,1,0:T(8,128)S(1)}, u32[]{:S(2)}, u32[]{:S(2)}) collective-permute-start(f32[24,8,256]{2,1,0:T(8,128)S(1)} %get-tuple-element.81), channel_id=1, source_target_pairs={{0,7},{1,0},{2,1},{3,2},{4,3},{5,4},{6,5},{7,6},{8,15},{9,8},{10,9... | collective-permute-start | bytes 589832 | tf_op jit(solution)/shard_map/ppermute | solution.py:37
  38.9 3.9 %copy-start.9 = (s32[1,1536]{1,0:T(1,128)S(1)}, s32[1,1536]{1,0:T(1,128)}, u32[]{:S(2)}) copy-start(s32[1,1536]{1,0:T(1,128)} %cells.1) | copy-start | bytes 18436
  38.9 6.7 %collective-permute-start.13 = (f32[24,8,256]{2,1,0:T(8,128)S(1)}, f32[24,8,256]{2,1,0:T(8,128)S(1)}, u32[]{:S(2)}, u32[]{:S(2)}) collective-permute-start(f32[24,8,256]{2,1,0:T(8,128)S(1)} %get-tuple-element.71), channel_id=1, source_target_pairs={{0,1},{1,2},{2,3},{3,4},{4,5},{5,6},{6,7},{7,0},{8,9},{9,10},{10,1... | collective-permute-start | bytes 589832 | tf_op jit(solution)/shard_map/ppermute | solution.py:37
  40.9 6.5 %collective-permute-start.14 = (f32[24,8,256]{2,1,0:T(8,128)S(1)}, f32[24,8,256]{2,1,0:T(8,128)S(1)}, u32[]{:S(2)}, u32[]{:S(2)}) collective-permute-start(f32[24,8,256]{2,1,0:T(8,128)S(1)} %get-tuple-element.72), channel_id=1, source_target_pairs={{0,7},{1,0},{2,1},{3,2},{4,3},{5,4},{6,5},{7,6},{8,15},{9,8},{10,9... | collective-permute-start | bytes 589832 | tf_op jit(solution)/shard_map/ppermute | solution.py:37
  41.0 4.6 %collective-permute-start.15 = (f32[4,8,256]{2,1,0:T(8,128)S(1)}, f32[4,8,256]{2,1,0:T(8,128)S(1)}, u32[]{:S(2)}, u32[]{:S(2)}) collective-permute-start(f32[4,8,256]{2,1,0:T(8,128)S(1)} %get-tuple-element.73), channel_id=1, source_target_pairs={{0,8},{8,16},{16,24},{24,0},{1,9},{9,17},{17,25},{25,1},{2,10},{10... | collective-permute-start | bytes 98312 | tf_op jit(solution)/shard_map/ppermute | solution.py:37
  41.0 4.6 %collective-permute-start.16 = (f32[4,8,256]{2,1,0:T(8,128)S(1)}, f32[4,8,256]{2,1,0:T(8,128)S(1)}, u32[]{:S(2)}, u32[]{:S(2)}) collective-permute-start(f32[4,8,256]{2,1,0:T(8,128)S(1)} %get-tuple-element.74), channel_id=1, source_target_pairs={{0,24},{8,0},{16,8},{24,16},{1,25},{9,1},{17,9},{25,17},{2,26},{10... | collective-permute-start | bytes 98312 | tf_op jit(solution)/shard_map/ppermute | solution.py:37
  48.2 7.3 %collective-permute-start.19 = (f32[2,24,8,128]{3,2,1,0:T(8,128)S(1)}, f32[2,24,8,128]{3,2,1,0:T(8,128)S(1)}, u32[]{:S(2)}, u32[]{:S(2)}) collective-permute-start(f32[2,24,8,128]{3,2,1,0:T(8,128)S(1)} %get-tuple-element.87), channel_id=1, source_target_pairs={{0,128},{32,160},{64,192},{96,224},{128,0},{160,32},{192,64},{224,... | collective-permute-start | bytes 589832 | tf_op jit(solution)/shard_map/ppermute | solution.py:45
  49.5 7.2 %collective-permute-start.20 = (f32[2,24,8,128]{3,2,1,0:T(8,128)S(1)}, f32[2,24,8,128]{3,2,1,0:T(8,128)S(1)}, u32[]{:S(2)}, u32[]{:S(2)}) collective-permute-start(f32[2,24,8,128]{3,2,1,0:T(8,128)S(1)} %get-tuple-element.88), channel_id=1, source_target_pairs={{0,32},{32,0},{64,96},{96,64},{128,160},{160,128},{192,224},{224,1... | collective-permute-start | bytes 589832 | tf_op jit(solution)/shard_map/ppermute | solution.py:41
  56.8 6.2 %collective-permute-start.21 = (f32[24,8,128]{2,1,0:T(8,128)S(1)}, f32[24,8,128]{2,1,0:T(8,128)S(1)}, u32[]{:S(2)}, u32[]{:S(2)}) collective-permute-start(f32[24,8,128]{2,1,0:T(8,128)S(1)} %get-tuple-element.90), channel_id=1, source_target_pairs={{0,32},{32,0},{64,96},{96,64},{128,160},{160,128},{192,224},{224,1... | collective-permute-start | bytes 294920 | tf_op jit(solution)/shard_map/ppermute | solution.py:41
  59.5 5.8 %collective-permute-start.22 = (f32[24,8,128]{2,1,0:T(8,128)S(1)}, f32[24,8,128]{2,1,0:T(8,128)S(1)}, u32[]{:S(2)}, u32[]{:S(2)}) collective-permute-start(f32[24,8,128]{2,1,0:T(8,128)S(1)} %get-tuple-element.91), channel_id=1, source_target_pairs={{0,64},{32,96},{64,128},{96,160},{128,192},{160,224},{192,0},{224,... | collective-permute-start | bytes 294920 | tf_op jit(solution)/shard_map/ppermute | solution.py:45
  59.8 5.5 %collective-permute-start.23 = (f32[24,8,128]{2,1,0:T(8,128)S(1)}, f32[24,8,128]{2,1,0:T(8,128)S(1)}, u32[]{:S(2)}, u32[]{:S(2)}) collective-permute-start(f32[24,8,128]{2,1,0:T(8,128)S(1)} %get-tuple-element.92), channel_id=1, source_target_pairs={{0,192},{32,224},{64,0},{96,32},{128,64},{160,96},{192,128},{224,1... | collective-permute-start | bytes 294920 | tf_op jit(solution)/shard_map/ppermute | solution.py:45

commit v3 on v2

--- a/solution.py
+++ b/solution.py
@@ -70,19 +70,29 @@
                 out[i, :, tile] = acc
 
 
-def pack_x(fields, up, down):
+def even_x():
+    return lax.rem(lax.axis_index("gx"), 2) == 0
+
+
+def face_x(first, last, inner, outer, f):
+    even = even_x()
+    inner[2 * f : 2 * f + 2] = jnp.where(even, last, first)
+    outer[2 * f : 2 * f + 2] = jnp.where(even, first, last)
+
+
+def pack_x(fields, inner, outer):
     for f, field in enumerate(fields):
         n = field.shape[0]
-        up[2 * f : 2 * f + 2] = field[n - 2 : n]
-        down[2 * f : 2 * f + 2] = field[0:2]
-
-
-def fill(pad, field, before, after, f):
+        face_x(field[0:2], field[n - 2 : n], inner, outer, f)
+
+
+def fill(pad, field, inner, outer, f):
     n = field.shape[0]
-    gx = lax.axis_index("gx")
+    gx, even = lax.axis_index("gx"), even_x()
+    inner, outer = inner[2 * f : 2 * f + 2], outer[2 * f : 2 * f + 2]
     pad[2 : n + 2] = field[...]
-    pad[0:2] = jnp.where(gx > 0, before[2 * f : 2 * f + 2], 0.0)
-    pad[n + 2 : n + 4] = jnp.where(gx < lax.axis_size("gx") - 1, after[2 * f : 2 * f + 2], 0.0)
+    pad[0:2] = jnp.where(gx > 0, jnp.where(even, outer, inner), 0.0)
+    pad[n + 2 : n + 4] = jnp.where(gx < lax.axis_size("gx") - 1, jnp.where(even, inner, outer), 0.0)
 
 
 def edge_rows(before, after, x, f, half):
@@ -158,28 +168,25 @@
     return s * (e * h + d * v) + k * m
 
 
-def chunk_kernel(p, speed, epsilon, delta, chunk, model, zmat, pbuf, half, sems):
-    shot = lax.axis_index("shot")
-    lower = pl.ds(pl.multiple_of((shot // 4) * 128, 128), 128)
-    copies = [
-        pltpu.make_async_copy(array.at[:, :, lower], half.at[k], sems.at[k])
-        for k, array in enumerate((speed, epsilon, delta))
-    ]
-    for copy in copies:
-        copy.start()
-    depth = zmat.shape[1]
-    offset = lax.broadcasted_iota(jnp.int32, (depth, depth), 0) - lax.broadcasted_iota(
-        jnp.int32, (depth, depth), 1
-    )
+def z_matrices(out):
+    shape = out.shape[1:]
+    offset = lax.broadcasted_iota(jnp.int32, shape, 0) - lax.broadcasted_iota(jnp.int32, shape, 1)
     far = jnp.abs(offset)
     second = jnp.where(far == 0, -30.0, jnp.where(far == 1, 16.0, jnp.where(far == 2, -1.0, 0.0)))
     first = jnp.where(far == 1, 8.0, jnp.where(far == 2, -1.0, 0.0))
-    zmat[0] = second.astype(BF16)
-    zmat[1] = jnp.where(offset > 0, first, -first).astype(BF16)
+    out[0] = second.astype(BF16)
+    out[1] = jnp.where(offset > 0, first, -first).astype(BF16)
+
+
+def own_depth(shot):
+    tile = pl.ds(pl.multiple_of((shot // 4) * 128, 128), 128)
+    return tile, lax.rem(128 - 32 * lax.rem(shot, 4), 128)
+
+
+def chunk_kernel(p, speed, epsilon, delta, *rest):
+    chunk, pbuf = rest[-2:]
     pbuf[:, :, :, 0:32] = p[...]
-    for copy in copies:
-        copy.wait()
-    shift = lax.rem(128 - 32 * lax.rem(shot, 4), 128)
+    tile, shift = own_depth(lax.axis_index("shot"))
     lane = lanes()
     group = p.shape[1] // 4
     for i in range(group):
@@ -187,9 +194,7 @@
         for g in range(4):
             x = g * group + i
             p0, p1, p2 = (pbuf[k, x] for k in range(3))
-            s, e, d = (pltpu.roll(half[k, x], shift, 1) for k in range(3))
-            for k, w in enumerate((s, e, d)):
-                model[k, x] = w
+            s, e, d = (pltpu.roll(w[x, :, tile], shift, 1) for w in (speed, epsilon, delta))
             for f, q in enumerate((p0 * e + s * p1, p0 * d + s * p2)):
                 parts[f].append(pltpu.roll(q, 32 * g, 1) if g else q)
         for f in (0, 1):
@@ -199,16 +204,23 @@
             )
 
 
-def y_kernel(a, b, *rest):
-    pack_y([a, b], *rest[-2:])
-
-
-def x_kernel(a, b, *rest):
-    pack_x([a, b], *rest[-2:])
+def first_x_kernel(u_first, l_first, u_last, l_last, inner, outer):
+    for f, (first, last) in enumerate(((u_first, u_last), (l_first, l_last))):
+        face_x(first[0:2], last[6:8], inner, outer, f)
+
+
+def first_y_kernel(u, l, *rest):
+    up, down, zmat = rest[-3:]
+    pack_y([u, l], up, down)
+    z_matrices(zmat)
+
+
+def y_kernel(a, b, up, down):
+    pack_y([a, b], up, down)
 
 
 def first_kernel(
-    wavelet, source, zmat, u, um, l, lm, ylo, yhi, xlo, xhi, speed, epsilon, delta, tilt,
+    wavelet, source, zmat, u, um, l, lm, ylo, yhi, inner, outer, speed, epsilon, delta, tilt, _,
     u1, l1, hu, vu, hl, vl, padu, padl,
 ):
     model = (speed, epsilon, delta, tilt)
@@ -217,7 +229,7 @@
     for f, (pad, w, prev, new, h_out, v_out) in enumerate(
         ((padu, u, um, u1, hu, vu), (padl, l, lm, l1, hl, vl))
     ):
-        fill(pad, w.at[0], xlo, xhi, f)
+        fill(pad, w.at[0], inner, outer, f)
 
         def emit(x, t, h, v, m, c, f=f, prev=prev, new=new, h_out=h_out, v_out=v_out):
             tile = pl.ds(128 * t, 128)
@@ -232,7 +244,7 @@
 
 
 def born_kernel(
-    mine, partner, before, behind, opposite, beside, u1, l1, hu, vu, hl, vl, q1, q2, b1, d1, yup, ydn, xup, xdn, chunks,
+    mine, partner, before, behind, opposite, beside, u1, l1, hu, vu, hl, vl, q1, q2, b1, d1, yup, ydn, inner_out, outer_out, chunks,
 ):
     shot = lax.axis_index("shot")
     y, xh = shot // 2, lax.rem(shot, 2)
@@ -264,18 +276,18 @@
             b1[x, :, tile] = both[0] * hu[x, :, tile] + both[1] * vu[x, :, tile]
             d1[x, :, tile] = both[0] * hl[x, :, tile] + both[1] * vl[x, :, tile]
     pack_y([u1, b1], yup, ydn)
-    pack_x([u1, b1, l1, d1], xup, xdn)
+    pack_x([u1, b1, l1, d1], inner_out, outer_out)
 
 
 def second_kernel(
-    wavelet, source, zmat, u, u1, b1, q1, q2, ylo, yhi, xlo, xhi, speed, epsilon, delta, tilt,
-    u2, b2, hu, vu, hb, vb, yup, ydn, xup, xdn, padu, padb,
+    wavelet, source, zmat, u, u1, b1, q1, q2, ylo, yhi, inner, outer, speed, epsilon, delta, tilt,
+    u2, b2, hu, vu, hb, vb, yup, ydn, inner_out, outer_out, padu, padb,
 ):
     model = (speed, epsilon, delta, tilt)
     lane = lanes()
     amount, depth = wavelet[0, 1], source[0]
-    fill(padu, u1, xlo, xhi, 0)
-    fill(padb, b1, xlo, xhi, 1)
+    fill(padu, u1, inner, outer, 0)
+    fill(padb, b1, inner, outer, 1)
 
     def emit_u(x, t, h, v, m, c):
         tile = pl.ds(128 * t, 128)
@@ -299,10 +311,11 @@
     derivs(padb, ylo, yhi, 1, zmat, emit_b)
     fields = [u2, b2]
     pack_y(fields, yup, ydn)
-    pack_x(fields, xup, xdn)
-
-
-def counts_kernel(cells, out, *, size_y, depth):
+    pack_x(fields, inner_out, outer_out)
+
+
+def counts_kernel(cells, *rest, size_y, depth):
+    out = rest[-1]
     nx, ny = out.shape[0], out.shape[1]
     gx, gy = lax.axis_index("gx"), lax.axis_index("gy")
     index = cells[...]
@@ -319,12 +332,12 @@
 
 
 def adjoint_kernel(
-    zmat, l, l1, d1, b1, q1, q2, counts, hu, vu, hb, vb, u2, b2, ylo, yhi, xlo, xhi,
+    zmat, l, l1, d1, b1, q1, q2, counts, hu, vu, hb, vb, u2, b2, ylo, yhi, inner, outer,
     speed, epsilon, delta, tilt, l2, d2, a1, c1, padl, padd, hl, vl,
 ):
     model = (speed, epsilon, delta, tilt)
-    fill(padl, l1, xlo, xhi, 2)
-    fill(padd, d1, xlo, xhi, 3)
+    fill(padl, l1, inner, outer, 2)
+    fill(padd, d1, inner, outer, 3)
 
     def emit_l(x, t, h, v, m, c):
         tile = pl.ds(128 * t, 128)
@@ -355,10 +368,10 @@
 
 
 def image_kernel(
-    u2, b2, ylo, yhi, xlo, xhi, l2, d2, a1, c1, keep, opposite, beside, padu, padb, total, chunks,
+    u2, b2, ylo, yhi, inner, outer, l2, d2, a1, c1, near, far, opposite, beside, padu, padb, total, chunks,
 ):
     for f, (pad, w) in enumerate(((padu, u2), (padb, b2))):
-        fill(pad, w, xlo, xhi, f)
+        fill(pad, w, inner, outer, f)
     nx = u2.shape[0]
     for x in range(nx):
         hu, hb = (
@@ -388,7 +401,8 @@
         return chunks[lax.rem(y + step, 4) * 2 + (xh if same else 1 - xh)]
 
     for out, wanted in (
-        (keep, ((0, True), (0, False), (1, True), (3, True))),
+        (near, ((0, True), (0, False))),
+        (far, ((1, True), (3, True))),
         (opposite, ((2, True), (2, False))),
         (beside, ((1, False), (3, False))),
     ):
@@ -396,15 +410,14 @@
             out[i] = chunk_at(step, same)
 
 
-def merge_kernel(keep, opposite, beside, own, other, up, down):
-    own[...] = keep[0] + opposite[0]
-    other[...] = keep[1] + opposite[1]
-    up[...] = keep[2] + beside[0]
-    down[...] = keep[3] + beside[1]
-
-
-def sum_kernel(model, own, other, up, down, out):
+def add_kernel(here, arrived, *outs):
+    for i, out in enumerate(outs):
+        out[...] = here[i] + arrived[i]
+
+
+def sum_kernel(speed, epsilon, delta, own, other, up, down, out):
     group = out.shape[1] // 4
+    tile, shift = own_depth(lax.axis_index("shot"))
     for i in range(group):
         sums = []
         for f in (0, 1):
@@ -413,7 +426,7 @@
         for g in range(4):
             x = g * group + i
             a, c = (pltpu.roll(v, (128 - 32 * g) % 128, 1) if g else v for v in sums)
-            s, e, d = (model[k, x] for k in range(3))
+            s, e, d = (pltpu.roll(w[x, :, tile], shift, 1) for w in (speed, epsilon, delta))
             out[0, x] = (e * a + d * c)[:, 0:32]
             out[1, x] = (s * a)[:, 0:32]
             out[2, x] = (s * c)[:, 0:32]
@@ -434,27 +447,45 @@
     def exchange_y(up, down):
         return cycle(up, "gy", 1), cycle(down, "gy", -1)
 
-    def exchange_x(up, down):
-        return cycle(up, "gx", 1), cycle(down, "gx", -1)
-
-    mine, slices, zmat = call(
+    def exchange_x(inner, outer):
+        n = lax.axis_size("gx")
+        return (
+            lax.ppermute(inner, "gx", [(i, i ^ 1) for i in range(n)]),
+            lax.ppermute(outer, "gx", [(i, ((i + 1) ^ 1) - 1 if 0 < i < n - 1 else n - 1 - i) for i in range(n)]),
+        )
+
+    now = (forward_now[0], adjoint_now[0])
+    sent = pl.pallas_call(
+        first_x_kernel,
+        out_shape=[jax.ShapeDtypeStruct((4, ny, nz), F32)] * 2,
+        in_specs=[pl.BlockSpec((8, ny, nz), lambda i, at=at: (at, 0, 0)) for at in (0, 0, nx // 8 - 1, nx // 8 - 1)],
+        out_specs=[pl.BlockSpec((4, ny, nz), lambda i: (0, 0, 0))] * 2,
+        grid=(1,),
+        compiler_params=pltpu.CompilerParams(vmem_limit_bytes=LIMIT),
+        name="layers_x",
+    )(*now, *now)
+    x0 = exchange_x(*sent)
+    (mine,) = call(
         chunk_kernel,
-        [packed, (3, nx, ny, 128), ((2, nz, nz), BF16)],
+        [packed],
         (perturbation, speed, epsilon, delta),
-        [pltpu.VMEM((3, nx, ny, 128), F32), pltpu.VMEM((3, nx, ny, 128), F32), pltpu.SemaphoreType.DMA((3,))],
-        hbm=(1, 2, 3),
+        [pltpu.VMEM((3, nx, ny, 128), F32)],
+        after=sent,
         name="chunk",
     )
     partner, before, behind = across(mine), along(mine, 1), along(mine, -1)
-    now = (forward_now[0], adjoint_now[0])
-    y0 = exchange_y(*call(y_kernel, layers[:2], now, after=(mine,), name="layers_y"))
-    opposite = along(jnp.concatenate([mine, partner], axis=0), 2)
+    *sent, zmat = call(
+        first_y_kernel, layers[:2] + [((2, nz, nz), BF16)], now, after=(mine, *x0), name="layers_y"
+    )
+    y0 = exchange_y(*sent)
+    pair = jnp.concatenate([mine, partner], axis=0)
+    opposite = along(pair, 2)
     beside = across(jnp.concatenate([before, behind], axis=0))
-    x0 = exchange_x(*call(x_kernel, layers[2:], now, after=y0, name="layers_x"))
     (counts,) = call(
         functools.partial(counts_kernel, size_y=ny * lax.axis_size("gy"), depth=nz),
         [whole],
         (receiver_cells,),
+        after=(pair, *sent),
         name="counts",
     )
     u1, l1, hu0, vu0, hl0, vl0 = call(
@@ -463,9 +494,10 @@
         (wavelet, source_cell, zmat, forward_now, forward_prev, adjoint_now, adjoint_prev) + y0 + x0 + model,
         [pad, pad],
         (0, 1),
+        after=(counts,),
         name="first",
     )
-    q1, q2, b1, d1, yup, ydn, xup, xdn = call(
+    q1, q2, b1, d1, yup, ydn, inner_out, outer_out = call(
         born_kernel,
         [whole] * 4 + layers[:2] + [(8, ny, nz)] * 2,
         (mine, partner, before, behind, opposite, beside, u1, l1, hu0, vu0, hl0, vl0),
@@ -473,9 +505,9 @@
         name="born",
     )
     y_ub = exchange_y(yup, ydn)
-    x1 = exchange_x(xup, xdn)
+    x1 = exchange_x(inner_out, outer_out)
     y_ld = exchange_y(*call(y_kernel, layers[:2], (l1, d1), name="adjoint_y"))
-    u2, b2, hu1, vu1, hb1, vb1, yup, ydn, xup, xdn = call(
+    u2, b2, hu1, vu1, hb1, vb1, yup, ydn, inner_out, outer_out = call(
         second_kernel,
         [whole] * 6 + layers,
         (wavelet, source_cell, zmat, forward_now, u1, b1, q1, q2) + y_ub + x1 + model,
@@ -483,7 +515,7 @@
         (0, 1),
         name="second",
     )
-    halo = exchange_y(yup, ydn) + exchange_x(xup, xdn)
+    halo = exchange_y(yup, ydn) + exchange_x(inner_out, outer_out)
     l2, d2, a1, c1 = call(
         adjoint_kernel,
         [whole] * 4,
@@ -491,20 +523,19 @@
         [pad, pad, pltpu.VMEM(whole, F32), pltpu.VMEM(whole, F32)],
         name="adjoint",
     )
-    keep, opposite, beside = call(
+    near, far, opposite, beside = call(
         image_kernel,
-        [(4,) + packed, (2,) + packed, (2,) + packed],
+        [(2,) + packed] * 4,
         (u2, b2) + halo + (l2, d2, a1, c1),
         [pad, pad, pltpu.VMEM(whole, F32), pltpu.VMEM((8,) + packed, F32)],
         name="image",
     )
-    own, other, up, down = call(
-        merge_kernel, [packed] * 4, (keep, along(opposite, 2), across(beside)), name="merge"
-    )
+    own, other = call(add_kernel, [packed] * 2, (near, along(opposite, 2)), name="add_opposite")
+    up, down = call(add_kernel, [packed] * 2, (far, across(beside)), name="add_beside")
     (out,) = call(
         sum_kernel,
         [(3, nx, ny, nz // 8)],
-        (slices, own, across(other), along(up, 1), along(down, -1)),
+        model[:3] + (own, across(other), along(up, 1), along(down, -1)),
         name="sum",
     )
     return out

time: 66.9 us -> 65.6 us (0.981)
  the two profiles are of different devices: /device:TPU:32 before, /device:TPU:24 now
where the time goes in v3:
time: 65.6 us; the launch traced here: 65.4 us
  starting transfers between devices  35.6 us (54%)
  waiting for transfers between devices  14.7 us (22%)
  Pallas kernels  10.7 us (16%)
  local copies, waits for them, and re-layouts  3.52 us (5%)
  between operations  0.91 us (1%)
    ppermute x8, starting transfers between devices, cycle(): lax.ppermute(value, axis, [(i, (i + step) % size) for i in range(size)])  15.9 us
    pallas_call x12, Pallas kernels, call(): pl.pallas_call(kernel, out_shape=[jax.ShapeDtypeStruct(*out) for out in t...  10.7 us
    ppermute x4, starting transfers between devices, across(): return lax.ppermute(value, 'shot', [(i, i ^ 1) for i in range(8)])  8.7 us
    ppermute x6, waiting for transfers between devices, along(): lax.ppermute(value, 'shot', [(i, (i // 2 + step) % 4 * 2 + i % 2) for i i...  8.35 us
    ppermute x6, starting transfers between devices, along(): lax.ppermute(value, 'shot', [(i, (i // 2 + step) % 4 * 2 + i % 2) for i i...  7.97 us
    ppermute x4, waiting for transfers between devices, across(): return lax.ppermute(value, 'shot', [(i, i ^ 1) for i in range(8)])  3.05 us
    ppermute x3, starting transfers between devices, exchange_x(): lax.ppermute(outer, 'gx', [(i, (i + 1 ^ 1) - 1 if 0 < i < n - 1 else n -...  2.96 us
    unnamed x21, local copies, waits for them, and re-layouts  2.54 us
  transfers between devices with their start and end apart: 24, of which 10 were waited for; matrix products, arithmetic and copies ran while one was open for 0% of the time, Pallas kernels for 12%

profile of v3, /device:TPU:24, one launch (start us, length us, event | category | flops | bytes accessed | tf_op | source)
XLA Modules:
  0.0 65.4 jit_solution(9325865353521922244)
XLA Ops:
  0.0 1.3 %copy.13.p = f32[3,48,8,32]{3,2,1,0:T(8,128)S(1)} copy(f32[3,48,8,32]{1,3,2,0:T(8,128)} %param.16) | data formatting | bytes 294912 | tf_op args[4]
  1.4 0.0 copy-start.1
  1.4 0.9 %copy-done.1 = f32[48,8,256]{2,1,0:T(8,128)S(1)} copy-done((f32[48,8,256]{2,1,0:T(8,128)S(1)}, f32[48,8,256]{2,1,0:T(8,128)}, u32[]{:S(2)}) %copy-start.1) | copy-done | bytes 393240
  2.4 0.1 copy-done.2
  2.5 0.1 copy-done.3
  2.6 1.1 %chunk.1.rest_0_.mine = f32[24,8,128]{2,1,0:T(8,128)S(1)} custom-call(f32[3,48,8,32]{3,2,1,0:T(8,128)S(1)} %copy.13.p, f32[48,8,256]{2,1,0:T(8,128)S(1)} %copy-done.1, f32[48,8,256]{2,1,0:T(8,128)S(1)} %copy-done.2, f32[48,8,256]{2,1,0:T(8,128)S(1)} %copy-done.3, f32[4,8,256]{2,1,0:T(8,128)S(1)} %get-tuple-element.48.rest_0_, ...), custom_call_target="tpu_custom_call" | custom-call | tf_op jit(solution)/shard_map/chunk/pallas_call | solution.py:24
  3.7 3.1 %collective-permute-start.4 = (f32[24,8,128]{2,1,0:T(8,128)S(1)}, f32[24,8,128]{2,1,0:T(8,128)S(1)}, u32[]{:S(2)}, u32[]{:S(2)}) collective-permute-start(f32[24,8,128]{2,1,0:T(8,128)S(1)} %chunk.1.rest_0_.mine), channel_id=1, source_target_pairs={{0,32},{32,0},{64,96},{96,64},{128,160},{160,128},{192,224},{224,1... | collective-permute-start | bytes 294920 | tf_op jit(solution)/shard_map/ppermute | solution.py:41
  6.8 0.7 %collective-permute-start.1 = (f32[4,8,256]{2,1,0:T(8,128)S(1)}, f32[4,8,256]{2,1,0:T(8,128)S(1)}, u32[]{:S(2)}, u32[]{:S(2)}) collective-permute-start(f32[4,8,256]{2,1,0:T(8,128)S(1)} %get-tuple-element.49.rest_1_), channel_id=1, source_target_pairs={{0,24},{8,16},{16,8},{24,0},{1,25},{9,17},{17,9},{25,1},{2,26},{10... | collective-permute-start | bytes 98312 | tf_op jit(solution)/shard_map/ppermute | solution.py:454
  7.5 0.2 collective-permute-start.5
  7.7 1.8 %collective-permute-start.6 = (f32[24,8,128]{2,1,0:T(8,128)S(1)}, f32[24,8,128]{2,1,0:T(8,128)S(1)}, u32[]{:S(2)}, u32[]{:S(2)}) collective-permute-start(f32[24,8,128]{2,1,0:T(8,128)S(1)} %chunk.1.rest_0_.mine), channel_id=1, source_target_pairs={{0,192},{32,224},{64,0},{96,32},{128,64},{160,96},{192,128},{224,1... | collective-permute-start | bytes 294920 | tf_op jit(solution)/shard_map/ppermute | solution.py:45
  9.5 0.8 %collective-permute-done.1.rest_2_.outer = f32[4,8,256]{2,1,0:T(8,128)S(1)} collective-permute-done((f32[4,8,256]{2,1,0:T(8,128)S(1)}, f32[4,8,256]{2,1,0:T(8,128)S(1)}, u32[]{:S(2)}, u32[]{:S(2)}) %collective-permute-start.1) | collective-permute-done | bytes 32800 | tf_op jit(solution)/shard_map/ppermute | solution.py:454
  10.3 0.2 layers_y.1
  10.5 2.0 %collective-permute-start.2 = (f32[24,8,256]{2,1,0:T(8,128)S(1)}, f32[24,8,256]{2,1,0:T(8,128)S(1)}, u32[]{:S(2)}, u32[]{:S(2)}) collective-permute-start(f32[24,8,256]{2,1,0:T(8,128)S(1)} %get-tuple-element.51.rest_1_), channel_id=1, source_target_pairs={{0,1},{1,2},{2,3},{3,4},{4,5},{5,6},{6,7},{7,0},{8,9},{9,10},{10,1... | collective-permute-start | bytes 589832 | tf_op jit(solution)/shard_map/ppermute | solution.py:37
  12.5 4.0 %collective-permute-start.3 = (f32[24,8,256]{2,1,0:T(8,128)S(1)}, f32[24,8,256]{2,1,0:T(8,128)S(1)}, u32[]{:S(2)}, u32[]{:S(2)}) collective-permute-start(f32[24,8,256]{2,1,0:T(8,128)S(1)} %get-tuple-element.52.rest_2_), channel_id=1, source_target_pairs={{0,7},{1,0},{2,1},{3,2},{4,3},{5,4},{6,5},{7,6},{8,15},{9,8},{10,9... | collective-permute-start | bytes 589832 | tf_op jit(solution)/shard_map/ppermute | solution.py:37
  16.5 1.3 %collective-permute-start.7 = (f32[48,8,128]{2,1,0:T(8,128)S(1)}, f32[48,8,128]{2,1,0:T(8,128)S(1)}, u32[]{:S(2)}, u32[]{:S(2)}) collective-permute-start(f32[48,8,128]{2,1,0:T(8,128)S(1)} %pad_maximum_fusion.rest_0_), channel_id=1, source_target_pairs={{0,128},{32,160},{64,192},{96,224},{128,0},{160,32},{192,64},{224,... | collective-permute-start | bytes 589832 | tf_op jit(solution)/shard_map/ppermute | solution.py:45
  17.9 1.3 %collective-permute-start.8 = (f32[48,8,128]{2,1,0:T(8,128)S(1)}, f32[48,8,128]{2,1,0:T(8,128)S(1)}, u32[]{:S(2)}, u32[]{:S(2)}) collective-permute-start(f32[48,8,128]{2,1,0:T(8,128)S(1)} %pad_maximum_fusion.1), channel_id=1, source_target_pairs={{0,32},{32,0},{64,96},{96,64},{128,160},{160,128},{192,224},{224,1... | collective-permute-start | bytes 589832 | tf_op jit(solution)/shard_map/ppermute | solution.py:41
  19.9 0.0 copy-start.6
  19.9 0.5 counts.1._
  20.4 1.4 %collective-permute-done.2.ylo = f32[24,8,256]{2,1,0:T(8,128)S(1)} collective-permute-done((f32[24,8,256]{2,1,0:T(8,128)S(1)}, f32[24,8,256]{2,1,0:T(8,128)S(1)}, u32[]{:S(2)}, u32[]{:S(2)}) %collective-permute-start.2) | collective-permute-done | bytes 196640 | tf_op jit(solution)/shard_map/ppermute | solution.py:37
  21.8 2.3 %first.1 = (f32[48,8,256]{2,1,0:T(8,128)S(1)}, f32[48,8,256]{2,1,0:T(8,128)S(1)}, f32[48,8,256]{2,1,0:T(8,128)S(1)}, f32[48,8,256]{2,1,0:T(8,128)S(1)}, f32[48,8...) custom-call(f32[1,2]{1,0:T(1,128)S(1)} %copy-done.9, s32[1]{0:T(128)S(6)} %copy.15.source, ...), custom_call_target="tpu_custom_call" | custom-call | tf_op jit(solution)/shard_map/first/pallas_call | solution.py:24
  24.1 0.8 %collective-permute-done.7.opposite = f32[48,8,128]{2,1,0:T(8,128)S(1)} collective-permute-done((f32[48,8,128]{2,1,0:T(8,128)S(1)}, f32[48,8,128]{2,1,0:T(8,128)S(1)}, u32[]{:S(2)}, u32[]{:S(2)}) %collective-permute-start.7) | collective-permute-done | bytes 196640 | tf_op jit(solution)/shard_map/ppermute | solution.py:45
  25.0 1.1 %collective-permute-done.8.beside = f32[48,8,128]{2,1,0:T(8,128)S(1)} collective-permute-done((f32[48,8,128]{2,1,0:T(8,128)S(1)}, f32[48,8,128]{2,1,0:T(8,128)S(1)}, u32[]{:S(2)}, u32[]{:S(2)}) %collective-permute-start.8) | collective-permute-done | bytes 196640 | tf_op jit(solution)/shard_map/ppermute | solution.py:41
  26.0 0.7 %born.1 = (f32[48,8,256]{2,1,0:T(8,128)S(1)}, f32[48,8,256]{2,1,0:T(8,128)S(1)}, f32[48,8,256]{2,1,0:T(8,128)S(1)}, f32[48,8,256]{2,1,0:T(8,128)S(1)}, f32[24,8,...) custom-call(f32[24,8,128]{2,1,0:T(8,128)S(1)} %chunk.1.rest_0_.mine, ...), custom_call_target="tpu_custom_call" | custom-call | tf_op jit(solution)/shard_map/born/pallas_call | solution.py:24
  26.8 0.1 collective-permute-start.9
  26.9 3.2 %collective-permute-start.10 = (f32[24,8,256]{2,1,0:T(8,128)S(1)}, f32[24,8,256]{2,1,0:T(8,128)S(1)}, u32[]{:S(2)}, u32[]{:S(2)}) collective-permute-start(f32[24,8,256]{2,1,0:T(8,128)S(1)} %get-tuple-element.63), channel_id=1, source_target_pairs={{0,7},{1,0},{2,1},{3,2},{4,3},{5,4},{6,5},{7,6},{8,15},{9,8},{10,9... | collective-permute-start | bytes 589832 | tf_op jit(solution)/shard_map/ppermute | solution.py:37
  30.1 1.4 %collective-permute-start.12 = (f32[8,8,256]{2,1,0:T(8,128)S(1)}, f32[8,8,256]{2,1,0:T(8,128)S(1)}, u32[]{:S(2)}, u32[]{:S(2)}) collective-permute-start(f32[8,8,256]{2,1,0:T(8,128)S(1)} %get-tuple-element.65), channel_id=1, source_target_pairs={{0,24},{8,16},{16,8},{24,0},{1,25},{9,17},{17,9},{25,1},{2,26},{10... | collective-permute-start | bytes 196616 | tf_op jit(solution)/shard_map/ppermute | solution.py:454
  31.5 0.1 adjoint_y.1
  31.6 0.1 collective-permute-start.17
  31.7 3.2 %collective-permute-start.18 = (f32[24,8,256]{2,1,0:T(8,128)S(1)}, f32[24,8,256]{2,1,0:T(8,128)S(1)}, u32[]{:S(2)}, u32[]{:S(2)}) collective-permute-start(f32[24,8,256]{2,1,0:T(8,128)S(1)} %get-tuple-element.78), channel_id=1, source_target_pairs={{0,7},{1,0},{2,1},{3,2},{4,3},{5,4},{6,5},{7,6},{8,15},{9,8},{10,9... | collective-permute-start | bytes 589832 | tf_op jit(solution)/shard_map/ppermute | solution.py:37
  34.9 2.4 %second.1 = (f32[48,8,256]{2,1,0:T(8,128)S(1)}, f32[48,8,256]{2,1,0:T(8,128)S(1)}, f32[48,8,256]{2,1,0:T(8,128)S(1)}, f32[48,8,256]{2,1,0:T(8,128)S(1)}, f32[48,...) custom-call(f32[1,2]{1,0:T(1,128)S(1)} %copy-done.9, ...), custom_call_target="tpu_custom_call" | custom-call | tf_op jit(solution)/shard_map/second/pallas_call | solution.py:24
  37.3 0.1 collective-permute-start.13
  37.4 3.2 %collective-permute-start.14 = (f32[24,8,256]{2,1,0:T(8,128)S(1)}, f32[24,8,256]{2,1,0:T(8,128)S(1)}, u32[]{:S(2)}, u32[]{:S(2)}) collective-permute-start(f32[24,8,256]{2,1,0:T(8,128)S(1)} %get-tuple-element.69), channel_id=1, source_target_pairs={{0,7},{1,0},{2,1},{3,2},{4,3},{5,4},{6,5},{7,6},{8,15},{9,8},{10,9... | collective-permute-start | bytes 589832 | tf_op jit(solution)/shard_map/ppermute | solution.py:37
  40.6 0.9 %collective-permute-start.16 = (f32[4,8,256]{2,1,0:T(8,128)S(1)}, f32[4,8,256]{2,1,0:T(8,128)S(1)}, u32[]{:S(2)}, u32[]{:S(2)}) collective-permute-start(f32[4,8,256]{2,1,0:T(8,128)S(1)} %get-tuple-element.71), channel_id=1, source_target_pairs={{0,24},{8,16},{16,8},{24,0},{1,25},{9,17},{17,9},{25,1},{2,26},{10... | collective-permute-start | bytes 98312 | tf_op jit(solution)/shard_map/ppermute | solution.py:454
  41.5 2.2 %adjoint.1 = (f32[48,8,256]{2,1,0:T(8,128)S(1)}, f32[48,8,256]{2,1,0:T(8,128)S(1)}, f32[48,8,256]{2,1,0:T(8,128)S(1)}, f32[48,8,256]{2,1,0:T(8,128)S(1)}) custom-call(bf16[2,256,256]{2,1,0:T(8,128)(2,1)S(1)} %get-tuple-element.50.zmat, f32[1,48,8,256]{3,2,1,0:T(8,128)S(1)} %copy-done, f32[48,8,256]{2,1,0:T(8,128)S(1)} %get-tuple-element.54.l1.a, ...), custom_call_target="tpu_custom_call" | custom-call | tf_op jit(solution)/shard_map/adjoint/pallas_call | solution.py:24
  43.7 0.2 collective-permute-done.16.outer
  44.0 0.9 %collective-permute-done.13.ylo = f32[24,8,256]{2,1,0:T(8,128)S(1)} collective-permute-done((f32[24,8,256]{2,1,0:T(8,128)S(1)}, f32[24,8,256]{2,1,0:T(8,128)S(1)}, u32[]{:S(2)}, u32[]{:S(2)}) %collective-permute-start.13) | collective-permute-done | bytes 196640 | tf_op jit(solution)/shard_map/ppermute | solution.py:37
  44.8 0.9 %image.1 = (f32[2,24,8,128]{3,2,1,0:T(8,128)S(1)}, f32[2,24,8,128]{3,2,1,0:T(8,128)S(1)}, f32[2,24,8,128]{3,2,1,0:T(8,128)S(1)}, f32[2,24,8,128]{3,2,1,0:T(8,128)S(1)}) custom-call(f32[48,8,256]{2,1,0:T(8,128)S(1)} %get-tuple-element.66.u2, f32[48,8,256]{2,1,0:T(8,128)S(1)} %get-tuple-element.67.b2, f32[24,8,256]{2,1,0:T(8,128)S(1)} %collective-permute-done.13.ylo, ...), custom_call_target="tpu_custom_call" | custom-call | tf_op jit(solution)/shard_map/image/pallas_call | solution.py:24
  45.7 2.4 %collective-permute-start.19 = (f32[2,24,8,128]{3,2,1,0:T(8,128)S(1)}, f32[2,24,8,128]{3,2,1,0:T(8,128)S(1)}, u32[]{:S(2)}, u32[]{:S(2)}) collective-permute-start(f32[2,24,8,128]{3,2,1,0:T(8,128)S(1)} %get-tuple-element.84), channel_id=1, source_target_pairs={{0,128},{32,160},{64,192},{96,224},{128,0},{160,32},{192,64},{224,... | collective-permute-start | bytes 589832 | tf_op jit(solution)/shard_map/ppermute | solution.py:45
  48.1 2.3 %collective-permute-start.21 = (f32[2,24,8,128]{3,2,1,0:T(8,128)S(1)}, f32[2,24,8,128]{3,2,1,0:T(8,128)S(1)}, u32[]{:S(2)}, u32[]{:S(2)}) collective-permute-start(f32[2,24,8,128]{3,2,1,0:T(8,128)S(1)} %get-tuple-element.88), channel_id=1, source_target_pairs={{0,32},{32,0},{64,96},{96,64},{128,160},{160,128},{192,224},{224,1... | collective-permute-start | bytes 589832 | tf_op jit(solution)/shard_map/ppermute | solution.py:41
  50.4 3.6 %collective-permute-done.19.arrived = f32[2,24,8,128]{3,2,1,0:T(8,128)S(1)} collective-permute-done((f32[2,24,8,128]{3,2,1,0:T(8,128)S(1)}, f32[2,24,8,128]{3,2,1,0:T(8,128)S(1)}, u32[]{:S(2)}, u32[]{:S(2)}) %collective-permute-start.19) | collective-permute-done | bytes 196640 | tf_op jit(solution)/shard_map/ppermute | solution.py:45
  54.1 2.0 %collective-permute-start.20 = (f32[24,8,128]{2,1,0:T(8,128)S(1)}, f32[24,8,128]{2,1,0:T(8,128)S(1)}, u32[]{:S(2)}, u32[]{:S(2)}) collective-permute-start(f32[24,8,128]{2,1,0:T(8,128)S(1)} %get-tuple-element.86), channel_id=1, source_target_pairs={{0,32},{32,0},{64,96},{96,64},{128,160},{160,128},{192,224},{224,1... | collective-permute-start | bytes 294920 | tf_op jit(solution)/shard_map/ppermute | solution.py:41
  56.0 0.0 collective-permute-done.21.arrived
  56.1 2.2 %collective-permute-start.22 = (f32[24,8,128]{2,1,0:T(8,128)S(1)}, f32[24,8,128]{2,1,0:T(8,128)S(1)}, u32[]{:S(2)}, u32[]{:S(2)}) collective-permute-start(f32[24,8,128]{2,1,0:T(8,128)S(1)} %get-tuple-element.89), channel_id=1, source_target_pairs={{0,64},{32,96},{64,128},{96,160},{128,192},{160,224},{192,0},{224,... | collective-permute-start | bytes 294920 | tf_op jit(solution)/shard_map/ppermute | solution.py:45
  58.3 1.9 %collective-permute-done.20.other = f32[24,8,128]{2,1,0:T(8,128)S(1)} collective-permute-done((f32[24,8,128]{2,1,0:T(8,128)S(1)}, f32[24,8,128]{2,1,0:T(8,128)S(1)}, u32[]{:S(2)}, u32[]{:S(2)}) %collective-permute-start.20) | collective-permute-done | bytes 98336 | tf_op jit(solution)/shard_map/ppermute | solution.py:41
  60.3 0.5 collective-permute-done.22.up
  60.8 3.4 %collective-permute-done.23.down = f32[24,8,128]{2,1,0:T(8,128)S(1)} collective-permute-done((f32[24,8,128]{2,1,0:T(8,128)S(1)}, f32[24,8,128]{2,1,0:T(8,128)S(1)}, u32[]{:S(2)}, u32[]{:S(2)}) %collective-permute-start.23) | collective-permute-done | bytes 98336 | tf_op jit(solution)/shard_map/ppermute | solution.py:45
  64.1 0.3 sum.1
  64.5 1.0 %copy.14 = f32[3,48,8,32]{1,3,2,0:T(8,128)} copy(f32[3,48,8,32]{3,2,1,0:T(8,128)S(1)} %sum.1) | data formatting | bytes 294912 | tf_op jit(solution)/shard_map/sum/pallas_call | solution.py:24
  (37 shorter events, 0.2 us)
Async XLA Ops:
  0.0 1.3 %copy-start.4 = (f32[1,48,8,256]{3,2,1,0:T(8,128)S(1)}, f32[1,48,8,256]{3,2,1,0:T(8,128)}, u32[]{:S(2)}) copy-start(f32[1,48,8,256]{3,2,1,0:T(8,128)} %u.3) | copy-start | bytes 1179652
  0.0 1.3 %copy-start = (f32[1,48,8,256]{3,2,1,0:T(8,128)S(1)}, f32[1,48,8,256]{3,2,1,0:T(8,128)}, u32[]{:S(2)}) copy-start(f32[1,48,8,256]{3,2,1,0:T(8,128)} %l.3) | copy-start | bytes 1179652
  1.4 1.0 %copy-start.1 = (f32[48,8,256]{2,1,0:T(8,128)S(1)}, f32[48,8,256]{2,1,0:T(8,128)}, u32[]{:S(2)}) copy-start(f32[48,8,256]{2,1,0:T(8,128)} %speed.9) | copy-start | bytes 1179652
  1.4 1.1 %copy-start.2 = (f32[48,8,256]{2,1,0:T(8,128)S(1)}, f32[48,8,256]{2,1,0:T(8,128)}, u32[]{:S(2)}) copy-start(f32[48,8,256]{2,1,0:T(8,128)} %epsilon.9) | copy-start | bytes 1179652
  1.4 1.2 %copy-start.3 = (f32[48,8,256]{2,1,0:T(8,128)S(1)}, f32[48,8,256]{2,1,0:T(8,128)}, u32[]{:S(2)}) copy-start(f32[48,8,256]{2,1,0:T(8,128)} %delta.9) | copy-start | bytes 1179652
  3.7 12.8 %collective-permute-start.4 = (f32[24,8,128]{2,1,0:T(8,128)S(1)}, f32[24,8,128]{2,1,0:T(8,128)S(1)}, u32[]{:S(2)}, u32[]{:S(2)}) collective-permute-start(f32[24,8,128]{2,1,0:T(8,128)S(1)} %chunk.1.rest_0_.mine), channel_id=1, source_target_pairs={{0,32},{32,0},{64,96},{96,64},{128,160},{160,128},{192,224},{224,1... | collective-permute-start | bytes 294920 | tf_op jit(solution)/shard_map/ppermute | solution.py:41
  6.8 2.7 %collective-permute-start = (f32[4,8,256]{2,1,0:T(8,128)S(1)}, f32[4,8,256]{2,1,0:T(8,128)S(1)}, u32[]{:S(2)}, u32[]{:S(2)}) collective-permute-start(f32[4,8,256]{2,1,0:T(8,128)S(1)} %get-tuple-element.48.rest_0_), channel_id=1, source_target_pairs={{0,8},{8,0},{16,24},{24,16},{1,9},{9,1},{17,25},{25,17},{2,10},{10... | collective-permute-start | bytes 98312 | tf_op jit(solution)/shard_map/ppermute | solution.py:453
  6.8 3.5 %collective-permute-start.1 = (f32[4,8,256]{2,1,0:T(8,128)S(1)}, f32[4,8,256]{2,1,0:T(8,128)S(1)}, u32[]{:S(2)}, u32[]{:S(2)}) collective-permute-start(f32[4,8,256]{2,1,0:T(8,128)S(1)} %get-tuple-element.49.rest_1_), channel_id=1, source_target_pairs={{0,24},{8,16},{16,8},{24,0},{1,25},{9,17},{17,9},{25,1},{2,26},{10... | collective-permute-start | bytes 98312 | tf_op jit(solution)/shard_map/ppermute | solution.py:454
  7.5 10.4 %collective-permute-start.5 = (f32[24,8,128]{2,1,0:T(8,128)S(1)}, f32[24,8,128]{2,1,0:T(8,128)S(1)}, u32[]{:S(2)}, u32[]{:S(2)}) collective-permute-start(f32[24,8,128]{2,1,0:T(8,128)S(1)} %chunk.1.rest_0_.mine), channel_id=1, source_target_pairs={{0,64},{32,96},{64,128},{96,160},{128,192},{160,224},{192,0},{224,... | collective-permute-start | bytes 294920 | tf_op jit(solution)/shard_map/ppermute | solution.py:45
  7.7 10.1 %collective-permute-start.6 = (f32[24,8,128]{2,1,0:T(8,128)S(1)}, f32[24,8,128]{2,1,0:T(8,128)S(1)}, u32[]{:S(2)}, u32[]{:S(2)}) collective-permute-start(f32[24,8,128]{2,1,0:T(8,128)S(1)} %chunk.1.rest_0_.mine), channel_id=1, source_target_pairs={{0,192},{32,224},{64,0},{96,32},{128,64},{160,96},{192,128},{224,1... | collective-permute-start | bytes 294920 | tf_op jit(solution)/shard_map/ppermute | solution.py:45
  10.5 11.3 %collective-permute-start.2 = (f32[24,8,256]{2,1,0:T(8,128)S(1)}, f32[24,8,256]{2,1,0:T(8,128)S(1)}, u32[]{:S(2)}, u32[]{:S(2)}) collective-permute-start(f32[24,8,256]{2,1,0:T(8,128)S(1)} %get-tuple-element.51.rest_1_), channel_id=1, source_target_pairs={{0,1},{1,2},{2,3},{3,4},{4,5},{5,6},{6,7},{7,0},{8,9},{9,10},{10,1... | collective-permute-start | bytes 589832 | tf_op jit(solution)/shard_map/ppermute | solution.py:37
  12.5 9.3 %collective-permute-start.3 = (f32[24,8,256]{2,1,0:T(8,128)S(1)}, f32[24,8,256]{2,1,0:T(8,128)S(1)}, u32[]{:S(2)}, u32[]{:S(2)}) collective-permute-start(f32[24,8,256]{2,1,0:T(8,128)S(1)} %get-tuple-element.52.rest_2_), channel_id=1, source_target_pairs={{0,7},{1,0},{2,1},{3,2},{4,3},{5,4},{6,5},{7,6},{8,15},{9,8},{10,9... | collective-permute-start | bytes 589832 | tf_op jit(solution)/shard_map/ppermute | solution.py:37
  16.5 3.3 %copy-start.8 = (s32[1,1536]{1,0:T(1,128)S(1)}, s32[1,1536]{1,0:T(1,128)}, u32[]{:S(2)}) copy-start(s32[1,1536]{1,0:T(1,128)} %cells.1) | copy-start | bytes 18436
  16.5 8.4 %collective-permute-start.7 = (f32[48,8,128]{2,1,0:T(8,128)S(1)}, f32[48,8,128]{2,1,0:T(8,128)S(1)}, u32[]{:S(2)}, u32[]{:S(2)}) collective-permute-start(f32[48,8,128]{2,1,0:T(8,128)S(1)} %pad_maximum_fusion.rest_0_), channel_id=1, source_target_pairs={{0,128},{32,160},{64,192},{96,224},{128,0},{160,32},{192,64},{224,... | collective-permute-start | bytes 589832 | tf_op jit(solution)/shard_map/ppermute | solution.py:45
  17.8 4.0 %copy-start.7 = (f32[1,48,8,256]{3,2,1,0:T(8,128)S(1)}, f32[1,48,8,256]{3,2,1,0:T(8,128)}, u32[]{:S(2)}) copy-start(f32[1,48,8,256]{3,2,1,0:T(8,128)} %lm.1) | copy-start | bytes 1179652
  17.9 8.2 %collective-permute-start.8 = (f32[48,8,128]{2,1,0:T(8,128)S(1)}, f32[48,8,128]{2,1,0:T(8,128)S(1)}, u32[]{:S(2)}, u32[]{:S(2)}) collective-permute-start(f32[48,8,128]{2,1,0:T(8,128)S(1)} %pad_maximum_fusion.1), channel_id=1, source_target_pairs={{0,32},{32,0},{64,96},{96,64},{128,160},{160,128},{192,224},{224,1... | collective-permute-start | bytes 589832 | tf_op jit(solution)/shard_map/ppermute | solution.py:41
  19.8 2.0 %copy-start.5 = (f32[48,8,256]{2,1,0:T(8,128)S(1)}, f32[48,8,256]{2,1,0:T(8,128)}, u32[]{:S(2)}) copy-start(f32[48,8,256]{2,1,0:T(8,128)} %tilt.5) | copy-start | bytes 1179652
  19.9 2.0 %copy-start.6 = (f32[1,48,8,256]{3,2,1,0:T(8,128)S(1)}, f32[1,48,8,256]{3,2,1,0:T(8,128)}, u32[]{:S(2)}) copy-start(f32[1,48,8,256]{3,2,1,0:T(8,128)} %um.1) | copy-start | bytes 1179652
  20.4 1.4 %copy-start.9 = (f32[1,2]{1,0:T(1,128)S(1)}, f32[1,2]{1,0:T(1,128)}, u32[]{:S(2)}) copy-start(f32[1,2]{1,0:T(1,128)} %wavelet.3) | copy-start | bytes 28
  26.8 8.1 %collective-permute-start.9 = (f32[24,8,256]{2,1,0:T(8,128)S(1)}, f32[24,8,256]{2,1,0:T(8,128)S(1)}, u32[]{:S(2)}, u32[]{:S(2)}) collective-permute-start(f32[24,8,256]{2,1,0:T(8,128)S(1)} %get-tuple-element.62), channel_id=1, source_target_pairs={{0,1},{1,2},{2,3},{3,4},{4,5},{5,6},{6,7},{7,0},{8,9},{9,10},{10,1... | collective-permute-start | bytes 589832 | tf_op jit(solution)/shard_map/ppermute | solution.py:37
  26.9 8.0 %collective-permute-start.10 = (f32[24,8,256]{2,1,0:T(8,128)S(1)}, f32[24,8,256]{2,1,0:T(8,128)S(1)}, u32[]{:S(2)}, u32[]{:S(2)}) collective-permute-start(f32[24,8,256]{2,1,0:T(8,128)S(1)} %get-tuple-element.63), channel_id=1, source_target_pairs={{0,7},{1,0},{2,1},{3,2},{4,3},{5,4},{6,5},{7,6},{8,15},{9,8},{10,9... | collective-permute-start | bytes 589832 | tf_op jit(solution)/shard_map/ppermute | solution.py:37
  30.1 1.6 %collective-permute-start.11 = (f32[8,8,256]{2,1,0:T(8,128)S(1)}, f32[8,8,256]{2,1,0:T(8,128)S(1)}, u32[]{:S(2)}, u32[]{:S(2)}) collective-permute-start(f32[8,8,256]{2,1,0:T(8,128)S(1)} %get-tuple-element.64), channel_id=1, source_target_pairs={{0,8},{8,0},{16,24},{24,16},{1,9},{9,1},{17,25},{25,17},{2,10},{10... | collective-permute-start | bytes 196616 | tf_op jit(solution)/shard_map/ppermute | solution.py:453
  30.1 4.8 %collective-permute-start.12 = (f32[8,8,256]{2,1,0:T(8,128)S(1)}, f32[8,8,256]{2,1,0:T(8,128)S(1)}, u32[]{:S(2)}, u32[]{:S(2)}) collective-permute-start(f32[8,8,256]{2,1,0:T(8,128)S(1)} %get-tuple-element.65), channel_id=1, source_target_pairs={{0,24},{8,16},{16,8},{24,0},{1,25},{9,17},{17,9},{25,1},{2,26},{10... | collective-permute-start | bytes 196616 | tf_op jit(solution)/shard_map/ppermute | solution.py:454
  31.6 9.0 %collective-permute-start.17 = (f32[24,8,256]{2,1,0:T(8,128)S(1)}, f32[24,8,256]{2,1,0:T(8,128)S(1)}, u32[]{:S(2)}, u32[]{:S(2)}) collective-permute-start(f32[24,8,256]{2,1,0:T(8,128)S(1)} %get-tuple-element.77), channel_id=1, source_target_pairs={{0,1},{1,2},{2,3},{3,4},{4,5},{5,6},{6,7},{7,0},{8,9},{9,10},{10,1... | collective-permute-start | bytes 589832 | tf_op jit(solution)/shard_map/ppermute | solution.py:37
  31.7 9.8 %collective-permute-start.18 = (f32[24,8,256]{2,1,0:T(8,128)S(1)}, f32[24,8,256]{2,1,0:T(8,128)S(1)}, u32[]{:S(2)}, u32[]{:S(2)}) collective-permute-start(f32[24,8,256]{2,1,0:T(8,128)S(1)} %get-tuple-element.78), channel_id=1, source_target_pairs={{0,7},{1,0},{2,1},{3,2},{4,3},{5,4},{6,5},{7,6},{8,15},{9,8},{10,9... | collective-permute-start | bytes 589832 | tf_op jit(solution)/shard_map/ppermute | solution.py:37
  37.3 7.5 %collective-permute-start.13 = (f32[24,8,256]{2,1,0:T(8,128)S(1)}, f32[24,8,256]{2,1,0:T(8,128)S(1)}, u32[]{:S(2)}, u32[]{:S(2)}) collective-permute-start(f32[24,8,256]{2,1,0:T(8,128)S(1)} %get-tuple-element.68), channel_id=1, source_target_pairs={{0,1},{1,2},{2,3},{3,4},{4,5},{5,6},{6,7},{7,0},{8,9},{9,10},{10,1... | collective-permute-start | bytes 589832 | tf_op jit(solution)/shard_map/ppermute | solution.py:37
  37.4 7.4 %collective-permute-start.14 = (f32[24,8,256]{2,1,0:T(8,128)S(1)}, f32[24,8,256]{2,1,0:T(8,128)S(1)}, u32[]{:S(2)}, u32[]{:S(2)}) collective-permute-start(f32[24,8,256]{2,1,0:T(8,128)S(1)} %get-tuple-element.69), channel_id=1, source_target_pairs={{0,7},{1,0},{2,1},{3,2},{4,3},{5,4},{6,5},{7,6},{8,15},{9,8},{10,9... | collective-permute-start | bytes 589832 | tf_op jit(solution)/shard_map/ppermute | solution.py:37
  40.6 3.1 %collective-permute-start.15 = (f32[4,8,256]{2,1,0:T(8,128)S(1)}, f32[4,8,256]{2,1,0:T(8,128)S(1)}, u32[]{:S(2)}, u32[]{:S(2)}) collective-permute-start(f32[4,8,256]{2,1,0:T(8,128)S(1)} %get-tuple-element.70), channel_id=1, source_target_pairs={{0,8},{8,0},{16,24},{24,16},{1,9},{9,1},{17,25},{25,17},{2,10},{10... | collective-permute-start | bytes 98312 | tf_op jit(solution)/shard_map/ppermute | solution.py:453
  40.6 3.3 %collective-permute-start.16 = (f32[4,8,256]{2,1,0:T(8,128)S(1)}, f32[4,8,256]{2,1,0:T(8,128)S(1)}, u32[]{:S(2)}, u32[]{:S(2)}) collective-permute-start(f32[4,8,256]{2,1,0:T(8,128)S(1)} %get-tuple-element.71), channel_id=1, source_target_pairs={{0,24},{8,16},{16,8},{24,0},{1,25},{9,17},{17,9},{25,1},{2,26},{10... | collective-permute-start | bytes 98312 | tf_op jit(solution)/shard_map/ppermute | solution.py:454
  45.7 8.3 %collective-permute-start.19 = (f32[2,24,8,128]{3,2,1,0:T(8,128)S(1)}, f32[2,24,8,128]{3,2,1,0:T(8,128)S(1)}, u32[]{:S(2)}, u32[]{:S(2)}) collective-permute-start(f32[2,24,8,128]{3,2,1,0:T(8,128)S(1)} %get-tuple-element.84), channel_id=1, source_target_pairs={{0,128},{32,160},{64,192},{96,224},{128,0},{160,32},{192,64},{224,... | collective-permute-start | bytes 589832 | tf_op jit(solution)/shard_map/ppermute | solution.py:45
  48.1 8.0 %collective-permute-start.21 = (f32[2,24,8,128]{3,2,1,0:T(8,128)S(1)}, f32[2,24,8,128]{3,2,1,0:T(8,128)S(1)}, u32[]{:S(2)}, u32[]{:S(2)}) collective-permute-start(f32[2,24,8,128]{3,2,1,0:T(8,128)S(1)} %get-tuple-element.88), channel_id=1, source_target_pairs={{0,32},{32,0},{64,96},{96,64},{128,160},{160,128},{192,224},{224,1... | collective-permute-start | bytes 589832 | tf_op jit(solution)/shard_map/ppermute | solution.py:41
  54.1 6.2 %collective-permute-start.20 = (f32[24,8,128]{2,1,0:T(8,128)S(1)}, f32[24,8,128]{2,1,0:T(8,128)S(1)}, u32[]{:S(2)}, u32[]{:S(2)}) collective-permute-start(f32[24,8,128]{2,1,0:T(8,128)S(1)} %get-tuple-element.86), channel_id=1, source_target_pairs={{0,32},{32,0},{64,96},{96,64},{128,160},{160,128},{192,224},{224,1... | collective-permute-start | bytes 294920 | tf_op jit(solution)/shard_map/ppermute | solution.py:41
  56.1 4.7 %collective-permute-start.22 = (f32[24,8,128]{2,1,0:T(8,128)S(1)}, f32[24,8,128]{2,1,0:T(8,128)S(1)}, u32[]{:S(2)}, u32[]{:S(2)}) collective-permute-start(f32[24,8,128]{2,1,0:T(8,128)S(1)} %get-tuple-element.89), channel_id=1, source_target_pairs={{0,64},{32,96},{64,128},{96,160},{128,192},{160,224},{192,0},{224,... | collective-permute-start | bytes 294920 | tf_op jit(solution)/shard_map/ppermute | solution.py:45
  58.3 5.8 %collective-permute-start.23 = (f32[24,8,128]{2,1,0:T(8,128)S(1)}, f32[24,8,128]{2,1,0:T(8,128)S(1)}, u32[]{:S(2)}, u32[]{:S(2)}) collective-permute-start(f32[24,8,128]{2,1,0:T(8,128)S(1)} %get-tuple-element.90), channel_id=1, source_target_pairs={{0,192},{32,224},{64,0},{96,32},{128,64},{160,96},{192,128},{224,1... | collective-permute-start | bytes 294920 | tf_op jit(solution)/shard_map/ppermute | solution.py:45

commit v4 on v3

--- a/solution.py
+++ b/solution.py
@@ -16,33 +16,50 @@
 D1, D2 = 2.0 / 3.0, -1.0 / 12.0
 
 
-def call(kernel, outs, ins, scratch=(), smem=(), hbm=(), after=(), name=None):
-    place = {**dict.fromkeys(smem, pltpu.SMEM), **dict.fromkeys(hbm, pltpu.HBM)}
-    place |= {len(ins) + i: pl.ANY for i in range(len(after))}
-    ins = (*ins, *after)
+def call(kernel, outs, ins, scratch=(), after=(), name=None):
+    places = [pltpu.VMEM] * len(ins) + [pl.ANY] * len(after)
     typed = [out if out[-1] is BF16 else (out, F32) for out in outs]
     return pl.pallas_call(
         kernel,
         out_shape=[jax.ShapeDtypeStruct(*out) for out in typed],
-        in_specs=[pl.BlockSpec(memory_space=place.get(i, pltpu.VMEM)) for i in range(len(ins))],
+        in_specs=[pl.BlockSpec(memory_space=place) for place in places],
         out_specs=[pl.BlockSpec(memory_space=pltpu.VMEM)] * len(outs),
         scratch_shapes=list(scratch),
         compiler_params=pltpu.CompilerParams(vmem_limit_bytes=LIMIT),
         name=name,
-    )(*ins)
-
-
-def cycle(value, axis, step):
-    size = lax.axis_size(axis)
-    return lax.ppermute(value, axis, [(i, (i + step) % size) for i in range(size)])
+    )(*ins, *after)
+
+
+def pairs(value, axis, outer=False):
+    n = lax.axis_size(axis)
+    other = [i ^ 1 if not outer else (((i + 1) % n ^ 1) - 1) % n for i in range(n)]
+    return lax.ppermute(value, axis, list(enumerate(other)))
+
+
+def outer_y(value):
+    nx, ny = lax.axis_size("gx"), lax.axis_size("gy")
+    swaps = []
+    for x in range(nx):
+        for y in range(ny):
+            there = (x ^ 1, y) if y in (0, ny - 1) else (x, ((y + 1) ^ 1) - 1)
+            swaps.append((x * ny + y, there[0] * ny + there[1]))
+    return lax.ppermute(value, ("gx", "gy"), swaps)
 
 
 def across(value):
     return lax.ppermute(value, "shot", [(i, i ^ 1) for i in range(8)])
 
 
-def along(value, step):
-    return lax.ppermute(value, "shot", [(i, (i // 2 + step) % 4 * 2 + i % 2) for i in range(8)])
+def opposite_y(value):
+    return lax.ppermute(value, "shot", [(i, (i + 4) % 8) for i in range(8)])
+
+
+def beside_y(value, outer=False):
+    return lax.ppermute(value, "shot", [(i, neighbour(i // 2, outer) * 2 + i % 2) for i in range(8)])
+
+
+def neighbour(y, outer):
+    return (y ^ 1) if not outer else (((y + 1) & 3) ^ 1) + 3 & 3
 
 
 def rows():
@@ -53,31 +70,31 @@
     return lax.broadcasted_iota(jnp.int32, (8, 128), 1)
 
 
-def pack_y(fields, up, down):
+def even(axis):
+    return lax.rem(lax.axis_index(axis), 2) == 0
+
+
+def pack_y(fields, inner, outer):
     row = rows()
     nx = fields[0].shape[0]
-    for i in range(nx // 2):
-        for h in (0, 128):
-            tile = pl.ds(h, 128)
-            for out, base in ((up, 6), (down, 0)):
+    base = jnp.where(even("gy"), 6, 0)
+    for out, base in ((inner, base), (outer, 6 - base)):
+        for i in range(nx // 2):
+            for h in (0, 128):
+                tile = pl.ds(h, 128)
                 acc = None
                 for piece in (0, 1):
                     for f, field in enumerate(fields):
                         at = 4 * piece + 2 * f
-                        value = field[i + piece * (nx // 2), :, tile]
-                        value = pltpu.roll(value, (at - base) % 8, 0) if at != base else value
+                        value = pltpu.roll(field[i + piece * (nx // 2), :, tile], lax.rem(at + 8 - base, 8), 0)
                         acc = value if acc is None else jnp.where(row >= at, value, acc)
                 out[i, :, tile] = acc
 
 
-def even_x():
-    return lax.rem(lax.axis_index("gx"), 2) == 0
-
-
 def face_x(first, last, inner, outer, f):
-    even = even_x()
-    inner[2 * f : 2 * f + 2] = jnp.where(even, last, first)
-    outer[2 * f : 2 * f + 2] = jnp.where(even, first, last)
+    at_even = even("gx")
+    inner[2 * f : 2 * f + 2] = jnp.where(at_even, last, first)
+    outer[2 * f : 2 * f + 2] = jnp.where(at_even, first, last)
 
 
 def pack_x(fields, inner, outer):
@@ -88,25 +105,26 @@
 
 def fill(pad, field, inner, outer, f):
     n = field.shape[0]
-    gx, even = lax.axis_index("gx"), even_x()
+    gx, at_even = lax.axis_index("gx"), even("gx")
     inner, outer = inner[2 * f : 2 * f + 2], outer[2 * f : 2 * f + 2]
     pad[2 : n + 2] = field[...]
-    pad[0:2] = jnp.where(gx > 0, jnp.where(even, outer, inner), 0.0)
-    pad[n + 2 : n + 4] = jnp.where(gx < lax.axis_size("gx") - 1, jnp.where(even, inner, outer), 0.0)
-
-
-def edge_rows(before, after, x, f, half):
+    pad[0:2] = jnp.where(gx > 0, jnp.where(at_even, outer, inner), 0.0)
+    pad[n + 2 : n + 4] = jnp.where(gx < lax.axis_size("gx") - 1, jnp.where(at_even, inner, outer), 0.0)
+
+
+def edge_rows(inner, outer, x, f, half):
     row = rows()
-    gy = lax.axis_index("gy")
-    first, last = gy > 0, gy < lax.axis_size("gy") - 1
+    gy, n = lax.axis_index("gy"), lax.axis_size("gy")
+    low = jnp.where(even("gy"), 0, 6)
+    from_inner = (row >= low) & (row < low + 2)
+    from_outer = (row >= 6 - low) & (row < 8 - low) & (gy > 0) & (gy < n - 1)
     i, at = x % half, 4 * (x // half) + 2 * f
     out = []
     for t in (0, 1):
         tile = pl.ds(128 * t, 128)
-        lower, upper = before[i, :, tile], after[i, :, tile]
-        lower = pltpu.roll(lower, (6 - at) % 8, 0) if at != 6 else lower
-        upper = pltpu.roll(upper, (-at) % 8, 0) if at != 0 else upper
-        out.append(jnp.where((row >= 6) & first, lower, jnp.where((row <= 1) & last, upper, 0.0)))
+        near = pltpu.roll(inner[i, :, tile], lax.rem(low + 8 - at, 8), 0)
+        far = pltpu.roll(outer[i, :, tile], lax.rem(14 - low - at, 8), 0)
+        out.append(jnp.where(from_inner, near, jnp.where(from_outer, far, 0.0)))
     return out
 
 
@@ -183,25 +201,26 @@
     return tile, lax.rem(128 - 32 * lax.rem(shot, 4), 128)
 
 
-def chunk_kernel(p, speed, epsilon, delta, *rest):
-    chunk, pbuf = rest[-2:]
-    pbuf[:, :, :, 0:32] = p[...]
+def chunk_kernel(p, speed, other, *rest, which):
+    before, (chunk, first, second) = rest[:-3], rest[-3:]
+    first[:, :, 0:32] = p[0]
+    second[:, :, 0:32] = p[which]
     tile, shift = own_depth(lax.axis_index("shot"))
     lane = lanes()
-    group = p.shape[1] // 4
+    group = first.shape[0] // 4
+    start = 0
+    if before:
+        start = group
+        chunk[0:group] = before[0][...]
     for i in range(group):
-        parts = [[], []]
+        parts = []
         for g in range(4):
             x = g * group + i
-            p0, p1, p2 = (pbuf[k, x] for k in range(3))
-            s, e, d = (pltpu.roll(w[x, :, tile], shift, 1) for w in (speed, epsilon, delta))
-            for f, q in enumerate((p0 * e + s * p1, p0 * d + s * p2)):
-                parts[f].append(pltpu.roll(q, 32 * g, 1) if g else q)
-        for f in (0, 1):
-            a, b, c, d = parts[f]
-            chunk[f * group + i] = jnp.where(
-                lane < 32, a, jnp.where(lane < 64, b, jnp.where(lane < 96, c, d))
-            )
+            s, e = (pltpu.roll(w[x, :, tile], shift, 1) for w in (speed, other))
+            q = first[x] * e + s * second[x]
+            parts.append(pltpu.roll(q, 32 * g, 1) if g else q)
+        a, b, c, d = parts
+        chunk[start + i] = jnp.where(lane < 32, a, jnp.where(lane < 64, b, jnp.where(lane < 96, c, d)))
 
 
 def first_x_kernel(u_first, l_first, u_last, l_last, inner, outer):
@@ -220,12 +239,10 @@
 
 
 def first_kernel(
-    wavelet, source, zmat, u, um, l, lm, ylo, yhi, inner, outer, speed, epsilon, delta, tilt, _,
+    plane, zmat, u, um, l, lm, ylo, yhi, inner, outer, speed, epsilon, delta, tilt,
     u1, l1, hu, vu, hl, vl, padu, padl,
 ):
     model = (speed, epsilon, delta, tilt)
-    lane = lanes()
-    amount, depth = wavelet[0, 0], source[0]
     for f, (pad, w, prev, new, h_out, v_out) in enumerate(
         ((padu, u, um, u1, hu, vu), (padl, l, lm, l1, hl, vl))
     ):
@@ -237,28 +254,27 @@
             v_out[x, :, tile] = v
             value = 2.0 * c - prev[0, x, :, tile] + operate(model, x, tile, h, v, m)
             if f == 0:
-                value = value + jnp.where(lane + 128 * t == depth, amount, 0.0)
+                value = value + plane[0, :, tile]
             new[x, :, tile] = value
 
         derivs(pad, ylo, yhi, f, zmat, emit)
 
 
 def born_kernel(
-    mine, partner, before, behind, opposite, beside, u1, l1, hu, vu, hl, vl, q1, q2, b1, d1, yup, ydn, inner_out, outer_out, chunks,
+    mine, partner, inner, outer, opposite, beside, u1, l1, hu, vu, hl, vl, q1, q2, b1, d1, yup, ydn, inner_out, outer_out, chunks,
 ):
     shot = lax.axis_index("shot")
     y, xh = shot // 2, lax.rem(shot, 2)
     group = hu.shape[0] // 4
     n = 2 * group
-    for k, same, other in (
-        (0, mine[...], partner[...]),
-        (3, before[...], beside[0:n]),
-        (1, behind[...], beside[n : 2 * n]),
-        (2, opposite[0:n], opposite[n : 2 * n]),
+    for there, same, other in (
+        (y, mine[...], partner[...]),
+        (neighbour(y, False), inner[...], beside[0:n]),
+        (neighbour(y, True), outer[...], beside[n : 2 * n]),
+        (y ^ 2, opposite[0:n], opposite[n : 2 * n]),
     ):
-        there = lax.rem(y + k, 4) * 2
-        chunks[there + xh] = same
-        chunks[there + 1 - xh] = other
+        chunks[there * 2 + xh] = same
+        chunks[there * 2 + 1 - xh] = other
     lane = lanes()
     for x in range(4 * group):
         g, i = x // group, x % group
@@ -280,12 +296,10 @@
 
 
 def second_kernel(
-    wavelet, source, zmat, u, u1, b1, q1, q2, ylo, yhi, inner, outer, speed, epsilon, delta, tilt,
+    plane, zmat, u, u1, b1, q1, q2, ylo, yhi, inner, outer, speed, epsilon, delta, tilt,
     u2, b2, hu, vu, hb, vb, yup, ydn, inner_out, outer_out, padu, padb,
 ):
     model = (speed, epsilon, delta, tilt)
-    lane = lanes()
-    amount, depth = wavelet[0, 1], source[0]
     fill(padu, u1, inner, outer, 0)
     fill(padb, b1, inner, outer, 1)
 
@@ -295,7 +309,7 @@
         vu[x, :, tile] = v
         u2[x, :, tile] = (
             2.0 * c - u[0, x, :, tile] + operate(model, x, tile, h, v, m)
-            + jnp.where(lane + 128 * t == depth, amount, 0.0)
+            + plane[1, :, tile]
         )
 
     def emit_b(x, t, h, v, m, c):
@@ -314,8 +328,14 @@
     pack_x(fields, inner_out, outer_out)
 
 
-def counts_kernel(cells, *rest, size_y, depth):
-    out = rest[-1]
+def counts_kernel(cells, wavelet, source, *rest, size_y, depth):
+    out, plane, amounts, place, sems = rest[-5:]
+    copies = [
+        pltpu.make_async_copy(wavelet, amounts, sems.at[0]),
+        pltpu.make_async_copy(source, place, sems.at[1]),
+    ]
+    for copy in copies:
+        copy.start()
     nx, ny = out.shape[0], out.shape[1]
     gx, gy = lax.axis_index("gx"), lax.axis_index("gy")
     index = cells[...]
@@ -323,12 +343,17 @@
     cy = lax.rem(lax.div(index, depth), size_y) - gy * ny
     cz = lax.rem(index, depth)
     inside = (cx >= 0) & (cx < nx) & (cy >= 0) & (cy < ny)
-    place = jnp.where(inside, cx * ny + cy, -1)
+    at = jnp.where(inside, cx * ny + cy, -1)
     n = index.shape[1]
-    left = jnp.where(lax.broadcasted_iota(jnp.int32, (nx * ny, n), 0) == place, 1.0, 0.0).astype(BF16)
+    left = jnp.where(lax.broadcasted_iota(jnp.int32, (nx * ny, n), 0) == at, 1.0, 0.0).astype(BF16)
     right = jnp.where(lax.broadcasted_iota(jnp.int32, (depth, n), 0) == cz, 1.0, 0.0).astype(BF16)
     total = lax.dot_general(left, right, (((1,), (1,)), ((), ())), preferred_element_type=F32)
     out[...] = total.reshape(nx, ny, depth)
+    for copy in copies:
+        copy.wait()
+    cell = lax.broadcasted_iota(jnp.int32, (ny, depth), 1)
+    for step in range(plane.shape[0]):
+        plane[step] = jnp.where(cell == place[0], amounts[0, step], 0.0)
 
 
 def adjoint_kernel(
@@ -397,17 +422,19 @@
     shot = lax.axis_index("shot")
     y, xh = shot // 2, lax.rem(shot, 2)
 
-    def chunk_at(step, same):
-        return chunks[lax.rem(y + step, 4) * 2 + (xh if same else 1 - xh)]
+    def chunk_at(there, same):
+        return chunks[there * 2 + (xh if same else 1 - xh)]
+
+    inner_y, outer_y = neighbour(y, False), neighbour(y, True)
 
     for out, wanted in (
-        (near, ((0, True), (0, False))),
-        (far, ((1, True), (3, True))),
-        (opposite, ((2, True), (2, False))),
-        (beside, ((1, False), (3, False))),
+        (near, ((y, True), (y, False))),
+        (far, ((inner_y, True), (outer_y, True))),
+        (opposite, ((y ^ 2, True), (y ^ 2, False))),
+        (beside, ((inner_y, False), (outer_y, False))),
     ):
-        for i, (step, same) in enumerate(wanted):
-            out[i] = chunk_at(step, same)
+        for i, (there, same) in enumerate(wanted):
+            out[i] = chunk_at(there, same)
 
 
 def add_kernel(here, arrived, *outs):
@@ -444,17 +471,22 @@
     packed = (nx // 2, ny, 128)
     model = (speed, epsilon, delta, tilt)
 
-    def exchange_y(up, down):
-        return cycle(up, "gy", 1), cycle(down, "gy", -1)
+    def exchange_y(inner, outer):
+        outer = outer_y(outer)
+        return pairs(inner, "gy"), outer
 
     def exchange_x(inner, outer):
-        n = lax.axis_size("gx")
-        return (
-            lax.ppermute(inner, "gx", [(i, i ^ 1) for i in range(n)]),
-            lax.ppermute(outer, "gx", [(i, ((i + 1) ^ 1) - 1 if 0 < i < n - 1 else n - 1 - i) for i in range(n)]),
-        )
+        outer = pairs(outer, "gx", True)
+        return pairs(inner, "gx"), outer
 
     now = (forward_now[0], adjoint_now[0])
+    (half,) = call(
+        functools.partial(chunk_kernel, which=1),
+        [(nx // 4, ny, 128)],
+        (perturbation, speed, epsilon),
+        [pltpu.VMEM((nx, ny, 128), F32)] * 2,
+        name="half_chunk",
+    )
     sent = pl.pallas_call(
         first_x_kernel,
         out_shape=[jax.ShapeDtypeStruct((4, ny, nz), F32)] * 2,
@@ -466,41 +498,40 @@
     )(*now, *now)
     x0 = exchange_x(*sent)
     (mine,) = call(
-        chunk_kernel,
+        functools.partial(chunk_kernel, which=2),
         [packed],
-        (perturbation, speed, epsilon, delta),
-        [pltpu.VMEM((3, nx, ny, 128), F32)],
-        after=sent,
+        (perturbation, speed, delta, half),
+        [pltpu.VMEM((nx, ny, 128), F32)] * 2,
         name="chunk",
     )
-    partner, before, behind = across(mine), along(mine, 1), along(mine, -1)
+    partner, inner, outer = across(mine), beside_y(mine), beside_y(mine, True)
     *sent, zmat = call(
         first_y_kernel, layers[:2] + [((2, nz, nz), BF16)], now, after=(mine, *x0), name="layers_y"
     )
     y0 = exchange_y(*sent)
     pair = jnp.concatenate([mine, partner], axis=0)
-    opposite = along(pair, 2)
-    beside = across(jnp.concatenate([before, behind], axis=0))
-    (counts,) = call(
+    opposite = opposite_y(pair)
+    beside = across(jnp.concatenate([inner, outer], axis=0))
+    steps = wavelet.shape[1]
+    counts, plane = call(
         functools.partial(counts_kernel, size_y=ny * lax.axis_size("gy"), depth=nz),
-        [whole],
+        [whole, (steps, ny, nz)],
         (receiver_cells,),
-        after=(pair, *sent),
+        [pltpu.SMEM((1, steps), F32), pltpu.SMEM((1,), jnp.int32), pltpu.SemaphoreType.DMA((2,))],
+        after=(wavelet, source_cell, pair, *sent),
         name="counts",
     )
     u1, l1, hu0, vu0, hl0, vl0 = call(
         first_kernel,
         [whole] * 6,
-        (wavelet, source_cell, zmat, forward_now, forward_prev, adjoint_now, adjoint_prev) + y0 + x0 + model,
+        (plane, zmat, forward_now, forward_prev, adjoint_now, adjoint_prev) + y0 + x0 + model,
         [pad, pad],
-        (0, 1),
-        after=(counts,),
         name="first",
     )
     q1, q2, b1, d1, yup, ydn, inner_out, outer_out = call(
         born_kernel,
         [whole] * 4 + layers[:2] + [(8, ny, nz)] * 2,
-        (mine, partner, before, behind, opposite, beside, u1, l1, hu0, vu0, hl0, vl0),
+        (mine, partner, inner, outer, opposite, beside, u1, l1, hu0, vu0, hl0, vl0),
         [pltpu.VMEM((8, nx // 2, ny, 128), F32)],
         name="born",
     )
@@ -510,9 +541,8 @@
     u2, b2, hu1, vu1, hb1, vb1, yup, ydn, inner_out, outer_out = call(
         second_kernel,
         [whole] * 6 + layers,
-        (wavelet, source_cell, zmat, forward_now, u1, b1, q1, q2) + y_ub + x1 + model,
+        (plane, zmat, forward_now, u1, b1, q1, q2) + y_ub + x1 + model,
         [pad, pad],
-        (0, 1),
         name="second",
     )
     halo = exchange_y(yup, ydn) + exchange_x(inner_out, outer_out)
@@ -530,12 +560,12 @@
         [pad, pad, pltpu.VMEM(whole, F32), pltpu.VMEM((8,) + packed, F32)],
         name="image",
     )
-    own, other = call(add_kernel, [packed] * 2, (near, along(opposite, 2)), name="add_opposite")
-    up, down = call(add_kernel, [packed] * 2, (far, across(beside)), name="add_beside")
+    own, other = call(add_kernel, [packed] * 2, (near, opposite_y(opposite)), name="add_opposite")
+    inner, outer = call(add_kernel, [packed] * 2, (far, across(beside)), name="add_beside")
     (out,) = call(
         sum_kernel,
         [(3, nx, ny, nz // 8)],
-        model[:3] + (own, across(other), along(up, 1), along(down, -1)),
+        model[:3] + (own, across(other), beside_y(inner), beside_y(outer, True)),
         name="sum",
     )
     return out

time: 65.6 us -> 62.9 us (0.959)
  the two profiles are of different devices: /device:TPU:24 before, /device:TPU:32 now
where the time goes in v4:
time: 62.9 us; the launch traced here: 62.8 us
  starting transfers between devices  33.9 us (54%)
  waiting for transfers between devices  15.2 us (24%)
  Pallas kernels  9.65 us (15%)
  local copies, waits for them, and re-layouts  3.03 us (5%)
  between operations  0.94 us (1%)
    ppermute x4, starting transfers between devices, outer_y(): return lax.ppermute(value, ('gx', 'gy'), swaps)  13.1 us
    pallas_call x13, Pallas kernels, call(): pl.pallas_call(kernel, out_shape=[jax.ShapeDtypeStruct(*out) for out in t...  9.64 us
    ppermute x4, starting transfers between devices, across(): return lax.ppermute(value, 'shot', [(i, i ^ 1) for i in range(8)])  9.08 us
    ppermute x2, waiting for transfers between devices, opposite_y(): return lax.ppermute(value, 'shot', [(i, (i + 4) % 8) for i in range(8)])  5.82 us
    ppermute x4, waiting for transfers between devices, across(): return lax.ppermute(value, 'shot', [(i, i ^ 1) for i in range(8)])  5.22 us
    ppermute x4, starting transfers between devices, beside_y(): lax.ppermute(value, 'shot', [(i, neighbour(i // 2, outer) * 2 + i % 2) fo...  4.96 us
    ppermute x10, starting transfers between devices, pairs(): return lax.ppermute(value, axis, list(enumerate(other)))  3.84 us
    ppermute x4, waiting for transfers between devices, beside_y(): lax.ppermute(value, 'shot', [(i, neighbour(i // 2, outer) * 2 + i % 2) fo...  3.09 us
  transfers between devices with their start and end apart: 24, of which 9 were waited for; matrix products, arithmetic and copies ran while one was open for 0% of the time, Pallas kernels for 11%

profile of v4, /device:TPU:32, one launch (start us, length us, event | category | flops | bytes accessed | tf_op | source)
XLA Modules:
  0.0 62.8 jit_solution(1395272789834124946)
XLA Ops:
  0.0 1.3 %copy.14.p = f32[3,48,8,32]{3,2,1,0:T(8,128)S(1)} copy(f32[3,48,8,32]{1,3,2,0:T(8,128)} %param.16) | data formatting | bytes 294912 | tf_op args[4]
  1.4 0.0 copy-start.3
  1.4 0.3 half_chunk.1.rest_0_
  1.7 0.7 %copy-done.3 = f32[48,8,256]{2,1,0:T(8,128)S(1)} copy-done((f32[48,8,256]{2,1,0:T(8,128)S(1)}, f32[48,8,256]{2,1,0:T(8,128)}, u32[]{:S(2)}) %copy-start.3) | copy-done | bytes 393240
  2.4 0.3 chunk.1.rest_0_.mine
  2.6 3.1 %collective-permute-start = (f32[24,8,128]{2,1,0:T(8,128)S(1)}, f32[24,8,128]{2,1,0:T(8,128)S(1)}, u32[]{:S(2)}, u32[]{:S(2)}) collective-permute-start(f32[24,8,128]{2,1,0:T(8,128)S(1)} %chunk.1.rest_0_.mine), channel_id=1, source_target_pairs={{0,32},{32,0},{64,96},{96,64},{128,160},{160,128},{192,224},{224,1... | collective-permute-start | bytes 294920 | tf_op jit(solution)/shard_map/ppermute | solution.py:50
  5.8 0.1 collective-permute-start.1
  5.9 0.7 %collective-permute-start.2 = (f32[4,8,256]{2,1,0:T(8,128)S(1)}, f32[4,8,256]{2,1,0:T(8,128)S(1)}, u32[]{:S(2)}, u32[]{:S(2)}) collective-permute-start(f32[4,8,256]{2,1,0:T(8,128)S(1)} %get-tuple-element.51), channel_id=1, source_target_pairs={{0,24},{8,16},{16,8},{24,0},{1,25},{9,17},{17,9},{25,1},{2,26},{10... | collective-permute-start | bytes 98312 | tf_op jit(solution)/shard_map/ppermute | solution.py:36
  6.6 1.6 %collective-permute-start.5 = (f32[24,8,128]{2,1,0:T(8,128)S(1)}, f32[24,8,128]{2,1,0:T(8,128)S(1)}, u32[]{:S(2)}, u32[]{:S(2)}) collective-permute-start(f32[24,8,128]{2,1,0:T(8,128)S(1)} %chunk.1.rest_0_.mine), channel_id=1, source_target_pairs={{0,64},{32,96},{64,0},{96,32},{128,192},{160,224},{192,128},{224,1... | collective-permute-start | bytes 294920 | tf_op jit(solution)/shard_map/ppermute | solution.py:58
  8.2 2.2 %collective-permute-start.6 = (f32[24,8,128]{2,1,0:T(8,128)S(1)}, f32[24,8,128]{2,1,0:T(8,128)S(1)}, u32[]{:S(2)}, u32[]{:S(2)}) collective-permute-start(f32[24,8,128]{2,1,0:T(8,128)S(1)} %chunk.1.rest_0_.mine), channel_id=1, source_target_pairs={{0,192},{32,224},{64,128},{96,160},{128,64},{160,96},{192,0},{224,... | collective-permute-start | bytes 294920 | tf_op jit(solution)/shard_map/ppermute | solution.py:58
  10.4 0.0 collective-permute-done.1.rest_1_.inner
  10.4 0.2 layers_y.1
  10.6 0.2 collective-permute-start.3
  10.8 3.7 %collective-permute-start.4 = (f32[24,8,256]{2,1,0:T(8,128)S(1)}, f32[24,8,256]{2,1,0:T(8,128)S(1)}, u32[]{:S(2)}, u32[]{:S(2)}) collective-permute-start(f32[24,8,256]{2,1,0:T(8,128)S(1)} %get-tuple-element.53.rest_2_), channel_id=1, source_target_pairs={{0,8},{1,2},{2,1},{3,4},{4,3},{5,6},{6,5},{7,15},{8,0},{9,10},{10,... | collective-permute-start | bytes 589832 | tf_op jit(solution)/shard_map/ppermute | solution.py:46
  14.5 2.2 %collective-permute-start.7 = (f32[48,8,128]{2,1,0:T(8,128)S(1)}, f32[48,8,128]{2,1,0:T(8,128)S(1)}, u32[]{:S(2)}, u32[]{:S(2)}) collective-permute-start(f32[48,8,128]{2,1,0:T(8,128)S(1)} %pad_maximum_fusion.rest_0_), channel_id=1, source_target_pairs={{0,128},{32,160},{64,192},{96,224},{128,0},{160,32},{192,64},{224,... | collective-permute-start | bytes 589832 | tf_op jit(solution)/shard_map/ppermute | solution.py:54
  16.8 0.0 copy-start.5
  16.8 1.3 %collective-permute-start.8 = (f32[48,8,128]{2,1,0:T(8,128)S(1)}, f32[48,8,128]{2,1,0:T(8,128)S(1)}, u32[]{:S(2)}, u32[]{:S(2)}) collective-permute-start(f32[48,8,128]{2,1,0:T(8,128)S(1)} %pad_maximum_fusion.1), channel_id=1, source_target_pairs={{0,32},{32,0},{64,96},{96,64},{128,160},{160,128},{192,224},{224,1... | collective-permute-start | bytes 589832 | tf_op jit(solution)/shard_map/ppermute | solution.py:50
  18.7 1.0 %counts.1 = (f32[48,8,256]{2,1,0:T(8,128)S(1)}, f32[2,8,256]{2,1,0:T(8,128)S(1)}) custom-call(s32[1,1536]{1,0:T(1,128)S(1)} %copy-done.8, f32[1,2]{1,0:T(1,128)S(1)} %copy-done.9, s32[1]{0:T(128)S(6)} %copy.16.source, f32[48,8,128]{2,1,0:T(8,128)S(1)} %pad_maximum_fusion.rest_0_, f32[24,8,256]{2,1,0:T(8,128)S(1)} %get-tuple-element.52.rest_1_, ...), custom_call_target="tpu_custom_call" | custom-call | tf_op jit(solution)/shard_map/counts/pallas_call | solution.py:22
  19.8 1.7 %first.1 = (f32[48,8,256]{2,1,0:T(8,128)S(1)}, f32[48,8,256]{2,1,0:T(8,128)S(1)}, f32[48,8,256]{2,1,0:T(8,128)S(1)}, f32[48,8,256]{2,1,0:T(8,128)S(1)}, f32[48,8...) custom-call(f32[2,8,256]{2,1,0:T(8,128)S(1)} %get-tuple-element.54.plane, bf16[2,256,256]{2,1,0:T(8,128)(2,1)S(1)} %get-tuple-element.55.zmat, ...), custom_call_target="tpu_custom_call" | custom-call | tf_op jit(solution)/shard_map/first/pallas_call | solution.py:22
  21.5 0.4 collective-permute-done.7.opposite
  21.9 2.9 %collective-permute-done.8.beside = f32[48,8,128]{2,1,0:T(8,128)S(1)} collective-permute-done((f32[48,8,128]{2,1,0:T(8,128)S(1)}, f32[48,8,128]{2,1,0:T(8,128)S(1)}, u32[]{:S(2)}, u32[]{:S(2)}) %collective-permute-start.8) | collective-permute-done | bytes 196640 | tf_op jit(solution)/shard_map/ppermute | solution.py:50
  24.8 0.7 %born.1 = (f32[48,8,256]{2,1,0:T(8,128)S(1)}, f32[48,8,256]{2,1,0:T(8,128)S(1)}, f32[48,8,256]{2,1,0:T(8,128)S(1)}, f32[48,8,256]{2,1,0:T(8,128)S(1)}, f32[24,8,...) custom-call(f32[24,8,128]{2,1,0:T(8,128)S(1)} %chunk.1.rest_0_.mine, ...), custom_call_target="tpu_custom_call" | custom-call | tf_op jit(solution)/shard_map/born/pallas_call | solution.py:22
  25.5 0.1 collective-permute-start.9
  25.6 4.1 %collective-permute-start.10 = (f32[24,8,256]{2,1,0:T(8,128)S(1)}, f32[24,8,256]{2,1,0:T(8,128)S(1)}, u32[]{:S(2)}, u32[]{:S(2)}) collective-permute-start(f32[24,8,256]{2,1,0:T(8,128)S(1)} %get-tuple-element.66), channel_id=1, source_target_pairs={{0,8},{1,2},{2,1},{3,4},{4,3},{5,6},{6,5},{7,15},{8,0},{9,10},{10,... | collective-permute-start | bytes 589832 | tf_op jit(solution)/shard_map/ppermute | solution.py:46
  29.8 1.3 %collective-permute-start.12 = (f32[8,8,256]{2,1,0:T(8,128)S(1)}, f32[8,8,256]{2,1,0:T(8,128)S(1)}, u32[]{:S(2)}, u32[]{:S(2)}) collective-permute-start(f32[8,8,256]{2,1,0:T(8,128)S(1)} %get-tuple-element.68), channel_id=1, source_target_pairs={{0,24},{8,16},{16,8},{24,0},{1,25},{9,17},{17,9},{25,1},{2,26},{10... | collective-permute-start | bytes 196616 | tf_op jit(solution)/shard_map/ppermute | solution.py:36
  31.0 0.1 adjoint_y.1
  31.1 0.1 collective-permute-start.17
  31.2 2.0 %collective-permute-start.18 = (f32[24,8,256]{2,1,0:T(8,128)S(1)}, f32[24,8,256]{2,1,0:T(8,128)S(1)}, u32[]{:S(2)}, u32[]{:S(2)}) collective-permute-start(f32[24,8,256]{2,1,0:T(8,128)S(1)} %get-tuple-element.82), channel_id=1, source_target_pairs={{0,8},{1,2},{2,1},{3,4},{4,3},{5,6},{6,5},{7,15},{8,0},{9,10},{10,... | collective-permute-start | bytes 589832 | tf_op jit(solution)/shard_map/ppermute | solution.py:46
  33.3 0.3 collective-permute-done.12.outer
  33.5 1.9 %second.1 = (f32[48,8,256]{2,1,0:T(8,128)S(1)}, f32[48,8,256]{2,1,0:T(8,128)S(1)}, f32[48,8,256]{2,1,0:T(8,128)S(1)}, f32[48,8,256]{2,1,0:T(8,128)S(1)}, f32[48,...) custom-call(f32[2,8,256]{2,1,0:T(8,128)S(1)} %get-tuple-element.54.p, ...), custom_call_target="tpu_custom_call" | custom-call | tf_op jit(solution)/shard_map/second/pallas_call | solution.py:22
  35.4 0.1 collective-permute-start.13
  35.5 3.2 %collective-permute-start.14 = (f32[24,8,256]{2,1,0:T(8,128)S(1)}, f32[24,8,256]{2,1,0:T(8,128)S(1)}, u32[]{:S(2)}, u32[]{:S(2)}) collective-permute-start(f32[24,8,256]{2,1,0:T(8,128)S(1)} %get-tuple-element.72), channel_id=1, source_target_pairs={{0,8},{1,2},{2,1},{3,4},{4,3},{5,6},{6,5},{7,15},{8,0},{9,10},{10,... | collective-permute-start | bytes 589832 | tf_op jit(solution)/shard_map/ppermute | solution.py:46
  38.7 1.3 %collective-permute-start.16 = (f32[4,8,256]{2,1,0:T(8,128)S(1)}, f32[4,8,256]{2,1,0:T(8,128)S(1)}, u32[]{:S(2)}, u32[]{:S(2)}) collective-permute-start(f32[4,8,256]{2,1,0:T(8,128)S(1)} %get-tuple-element.74), channel_id=1, source_target_pairs={{0,24},{8,16},{16,8},{24,0},{1,25},{9,17},{17,9},{25,1},{2,26},{10... | collective-permute-start | bytes 98312 | tf_op jit(solution)/shard_map/ppermute | solution.py:36
  40.0 2.3 %adjoint.1 = (f32[48,8,256]{2,1,0:T(8,128)S(1)}, f32[48,8,256]{2,1,0:T(8,128)S(1)}, f32[48,8,256]{2,1,0:T(8,128)S(1)}, f32[48,8,256]{2,1,0:T(8,128)S(1)}) custom-call(bf16[2,256,256]{2,1,0:T(8,128)(2,1)S(1)} %get-tuple-element.55.zmat, f32[1,48,8,256]{3,2,1,0:T(8,128)S(1)} %copy-done.1, f32[48,8,256]{2,1,0:T(8,128)S(1)} %get-tuple-element.57.l1.a, ...), custom_call_target="tpu_custom_call" | custom-call | tf_op jit(solution)/shard_map/adjoint/pallas_call | solution.py:22
  42.3 0.5 collective-permute-done.13.ylo
  42.8 0.3 collective-permute-done.14.yhi
  43.1 0.9 %image.1 = (f32[2,24,8,128]{3,2,1,0:T(8,128)S(1)}, f32[2,24,8,128]{3,2,1,0:T(8,128)S(1)}, f32[2,24,8,128]{3,2,1,0:T(8,128)S(1)}, f32[2,24,8,128]{3,2,1,0:T(8,128)S(1)}) custom-call(f32[48,8,256]{2,1,0:T(8,128)S(1)} %get-tuple-element.69.u2, f32[48,8,256]{2,1,0:T(8,128)S(1)} %get-tuple-element.70.b2, f32[24,8,256]{2,1,0:T(8,128)S(1)} %collective-permute-done.13.ylo, ...), custom_call_target="tpu_custom_call" | custom-call | tf_op jit(solution)/shard_map/image/pallas_call | solution.py:22
  44.0 0.7 %collective-permute-start.19 = (f32[2,24,8,128]{3,2,1,0:T(8,128)S(1)}, f32[2,24,8,128]{3,2,1,0:T(8,128)S(1)}, u32[]{:S(2)}, u32[]{:S(2)}) collective-permute-start(f32[2,24,8,128]{3,2,1,0:T(8,128)S(1)} %get-tuple-element.88), channel_id=1, source_target_pairs={{0,128},{32,160},{64,192},{96,224},{128,0},{160,32},{192,64},{224,... | collective-permute-start | bytes 589832 | tf_op jit(solution)/shard_map/ppermute | solution.py:54
  44.7 2.0 %collective-permute-start.21 = (f32[2,24,8,128]{3,2,1,0:T(8,128)S(1)}, f32[2,24,8,128]{3,2,1,0:T(8,128)S(1)}, u32[]{:S(2)}, u32[]{:S(2)}) collective-permute-start(f32[2,24,8,128]{3,2,1,0:T(8,128)S(1)} %get-tuple-element.92), channel_id=1, source_target_pairs={{0,32},{32,0},{64,96},{96,64},{128,160},{160,128},{192,224},{224,1... | collective-permute-start | bytes 589832 | tf_op jit(solution)/shard_map/ppermute | solution.py:50
  46.7 5.4 %collective-permute-done.19.arrived = f32[2,24,8,128]{3,2,1,0:T(8,128)S(1)} collective-permute-done((f32[2,24,8,128]{3,2,1,0:T(8,128)S(1)}, f32[2,24,8,128]{3,2,1,0:T(8,128)S(1)}, u32[]{:S(2)}, u32[]{:S(2)}) %collective-permute-start.19) | collective-permute-done | bytes 196640 | tf_op jit(solution)/shard_map/ppermute | solution.py:54
  52.2 2.7 %collective-permute-start.20 = (f32[24,8,128]{2,1,0:T(8,128)S(1)}, f32[24,8,128]{2,1,0:T(8,128)S(1)}, u32[]{:S(2)}, u32[]{:S(2)}) collective-permute-start(f32[24,8,128]{2,1,0:T(8,128)S(1)} %get-tuple-element.90), channel_id=1, source_target_pairs={{0,32},{32,0},{64,96},{96,64},{128,160},{160,128},{192,224},{224,1... | collective-permute-start | bytes 294920 | tf_op jit(solution)/shard_map/ppermute | solution.py:50
  54.9 0.8 %collective-permute-start.22 = (f32[24,8,128]{2,1,0:T(8,128)S(1)}, f32[24,8,128]{2,1,0:T(8,128)S(1)}, u32[]{:S(2)}, u32[]{:S(2)}) collective-permute-start(f32[24,8,128]{2,1,0:T(8,128)S(1)} %get-tuple-element.93), channel_id=1, source_target_pairs={{0,64},{32,96},{64,0},{96,32},{128,192},{160,224},{192,128},{224,1... | collective-permute-start | bytes 294920 | tf_op jit(solution)/shard_map/ppermute | solution.py:58
  55.6 0.4 collective-permute-start.23
  56.1 2.3 %collective-permute-done.20.other = f32[24,8,128]{2,1,0:T(8,128)S(1)} collective-permute-done((f32[24,8,128]{2,1,0:T(8,128)S(1)}, f32[24,8,128]{2,1,0:T(8,128)S(1)}, u32[]{:S(2)}, u32[]{:S(2)}) %collective-permute-start.20) | collective-permute-done | bytes 98336 | tf_op jit(solution)/shard_map/ppermute | solution.py:50
  58.4 1.2 %collective-permute-done.22.up = f32[24,8,128]{2,1,0:T(8,128)S(1)} collective-permute-done((f32[24,8,128]{2,1,0:T(8,128)S(1)}, f32[24,8,128]{2,1,0:T(8,128)S(1)}, u32[]{:S(2)}, u32[]{:S(2)}) %collective-permute-start.22) | collective-permute-done | bytes 98336 | tf_op jit(solution)/shard_map/ppermute | solution.py:58
  59.6 1.9 %collective-permute-done.23.down = f32[24,8,128]{2,1,0:T(8,128)S(1)} collective-permute-done((f32[24,8,128]{2,1,0:T(8,128)S(1)}, f32[24,8,128]{2,1,0:T(8,128)S(1)}, u32[]{:S(2)}, u32[]{:S(2)}) %collective-permute-start.23) | collective-permute-done | bytes 98336 | tf_op jit(solution)/shard_map/ppermute | solution.py:58
  61.5 0.3 sum.1
  61.8 1.0 %copy.15 = f32[3,48,8,32]{1,3,2,0:T(8,128)} copy(f32[3,48,8,32]{3,2,1,0:T(8,128)S(1)} %sum.1) | data formatting | bytes 294912 | tf_op jit(solution)/shard_map/sum/pallas_call | solution.py:22
  (38 shorter events, 0.2 us)
Async XLA Ops:
  0.0 1.3 %copy-start = (f32[48,8,256]{2,1,0:T(8,128)S(1)}, f32[48,8,256]{2,1,0:T(8,128)}, u32[]{:S(2)}) copy-start(f32[48,8,256]{2,1,0:T(8,128)} %speed.11) | copy-start | bytes 1179652
  0.0 1.3 %copy-start.2 = (f32[48,8,256]{2,1,0:T(8,128)S(1)}, f32[48,8,256]{2,1,0:T(8,128)}, u32[]{:S(2)}) copy-start(f32[48,8,256]{2,1,0:T(8,128)} %epsilon.7) | copy-start | bytes 1179652
  1.4 1.0 %copy-start.3 = (f32[48,8,256]{2,1,0:T(8,128)S(1)}, f32[48,8,256]{2,1,0:T(8,128)}, u32[]{:S(2)}) copy-start(f32[48,8,256]{2,1,0:T(8,128)} %delta.7) | copy-start | bytes 1179652
  2.4 3.4 %copy-start.1 = (f32[1,48,8,256]{3,2,1,0:T(8,128)S(1)}, f32[1,48,8,256]{3,2,1,0:T(8,128)}, u32[]{:S(2)}) copy-start(f32[1,48,8,256]{3,2,1,0:T(8,128)} %l.3) | copy-start | bytes 1179652
  2.4 3.4 %copy-start.4 = (f32[1,48,8,256]{3,2,1,0:T(8,128)S(1)}, f32[1,48,8,256]{3,2,1,0:T(8,128)}, u32[]{:S(2)}) copy-start(f32[1,48,8,256]{3,2,1,0:T(8,128)} %u.3) | copy-start | bytes 1179652
  2.6 11.8 %collective-permute-start = (f32[24,8,128]{2,1,0:T(8,128)S(1)}, f32[24,8,128]{2,1,0:T(8,128)S(1)}, u32[]{:S(2)}, u32[]{:S(2)}) collective-permute-start(f32[24,8,128]{2,1,0:T(8,128)S(1)} %chunk.1.rest_0_.mine), channel_id=1, source_target_pairs={{0,32},{32,0},{64,96},{96,64},{128,160},{160,128},{192,224},{224,1... | collective-permute-start | bytes 294920 | tf_op jit(solution)/shard_map/ppermute | solution.py:50
  5.8 4.6 %collective-permute-start.1 = (f32[4,8,256]{2,1,0:T(8,128)S(1)}, f32[4,8,256]{2,1,0:T(8,128)S(1)}, u32[]{:S(2)}, u32[]{:S(2)}) collective-permute-start(f32[4,8,256]{2,1,0:T(8,128)S(1)} %get-tuple-element.50), channel_id=1, source_target_pairs={{0,8},{8,0},{16,24},{24,16},{1,9},{9,1},{17,25},{25,17},{2,10},{10... | collective-permute-start | bytes 98312 | tf_op jit(solution)/shard_map/ppermute | solution.py:36
  5.9 4.5 %collective-permute-start.2 = (f32[4,8,256]{2,1,0:T(8,128)S(1)}, f32[4,8,256]{2,1,0:T(8,128)S(1)}, u32[]{:S(2)}, u32[]{:S(2)}) collective-permute-start(f32[4,8,256]{2,1,0:T(8,128)S(1)} %get-tuple-element.51), channel_id=1, source_target_pairs={{0,24},{8,16},{16,8},{24,0},{1,25},{9,17},{17,9},{25,1},{2,26},{10... | collective-permute-start | bytes 98312 | tf_op jit(solution)/shard_map/ppermute | solution.py:36
  6.6 10.1 %collective-permute-start.5 = (f32[24,8,128]{2,1,0:T(8,128)S(1)}, f32[24,8,128]{2,1,0:T(8,128)S(1)}, u32[]{:S(2)}, u32[]{:S(2)}) collective-permute-start(f32[24,8,128]{2,1,0:T(8,128)S(1)} %chunk.1.rest_0_.mine), channel_id=1, source_target_pairs={{0,64},{32,96},{64,0},{96,32},{128,192},{160,224},{192,128},{224,1... | collective-permute-start | bytes 294920 | tf_op jit(solution)/shard_map/ppermute | solution.py:58
  8.2 8.6 %collective-permute-start.6 = (f32[24,8,128]{2,1,0:T(8,128)S(1)}, f32[24,8,128]{2,1,0:T(8,128)S(1)}, u32[]{:S(2)}, u32[]{:S(2)}) collective-permute-start(f32[24,8,128]{2,1,0:T(8,128)S(1)} %chunk.1.rest_0_.mine), channel_id=1, source_target_pairs={{0,192},{32,224},{64,128},{96,160},{128,64},{160,96},{192,0},{224,... | collective-permute-start | bytes 294920 | tf_op jit(solution)/shard_map/ppermute | solution.py:58
  10.6 9.2 %collective-permute-start.3 = (f32[24,8,256]{2,1,0:T(8,128)S(1)}, f32[24,8,256]{2,1,0:T(8,128)S(1)}, u32[]{:S(2)}, u32[]{:S(2)}) collective-permute-start(f32[24,8,256]{2,1,0:T(8,128)S(1)} %get-tuple-element.52.rest_1_), channel_id=1, source_target_pairs={{0,1},{1,0},{2,3},{3,2},{4,5},{5,4},{6,7},{7,6},{8,9},{9,8},{10,11... | collective-permute-start | bytes 589832 | tf_op jit(solution)/shard_map/ppermute | solution.py:36
  10.8 9.0 %collective-permute-start.4 = (f32[24,8,256]{2,1,0:T(8,128)S(1)}, f32[24,8,256]{2,1,0:T(8,128)S(1)}, u32[]{:S(2)}, u32[]{:S(2)}) collective-permute-start(f32[24,8,256]{2,1,0:T(8,128)S(1)} %get-tuple-element.53.rest_2_), channel_id=1, source_target_pairs={{0,8},{1,2},{2,1},{3,4},{4,3},{5,6},{6,5},{7,15},{8,0},{9,10},{10,... | collective-permute-start | bytes 589832 | tf_op jit(solution)/shard_map/ppermute | solution.py:46
  14.5 4.2 %copy-start.8 = (s32[1,1536]{1,0:T(1,128)S(1)}, s32[1,1536]{1,0:T(1,128)}, u32[]{:S(2)}) copy-start(s32[1,1536]{1,0:T(1,128)} %cells.1) | copy-start | bytes 18436
  14.5 4.2 %copy-start.9 = (f32[1,2]{1,0:T(1,128)S(1)}, f32[1,2]{1,0:T(1,128)}, u32[]{:S(2)}) copy-start(f32[1,2]{1,0:T(1,128)} %wavelet.1) | copy-start | bytes 28
  14.5 5.3 %copy-start.7 = (f32[1,48,8,256]{3,2,1,0:T(8,128)S(1)}, f32[1,48,8,256]{3,2,1,0:T(8,128)}, u32[]{:S(2)}) copy-start(f32[1,48,8,256]{3,2,1,0:T(8,128)} %lm.1) | copy-start | bytes 1179652
  14.5 7.4 %collective-permute-start.7 = (f32[48,8,128]{2,1,0:T(8,128)S(1)}, f32[48,8,128]{2,1,0:T(8,128)S(1)}, u32[]{:S(2)}, u32[]{:S(2)}) collective-permute-start(f32[48,8,128]{2,1,0:T(8,128)S(1)} %pad_maximum_fusion.rest_0_), channel_id=1, source_target_pairs={{0,128},{32,160},{64,192},{96,224},{128,0},{160,32},{192,64},{224,... | collective-permute-start | bytes 589832 | tf_op jit(solution)/shard_map/ppermute | solution.py:54
  16.7 3.0 %copy-start.6 = (f32[1,48,8,256]{3,2,1,0:T(8,128)S(1)}, f32[1,48,8,256]{3,2,1,0:T(8,128)}, u32[]{:S(2)}) copy-start(f32[1,48,8,256]{3,2,1,0:T(8,128)} %um.1) | copy-start | bytes 1179652
  16.8 3.0 %copy-start.5 = (f32[48,8,256]{2,1,0:T(8,128)S(1)}, f32[48,8,256]{2,1,0:T(8,128)}, u32[]{:S(2)}) copy-start(f32[48,8,256]{2,1,0:T(8,128)} %tilt.5) | copy-start | bytes 1179652
  16.8 8.0 %collective-permute-start.8 = (f32[48,8,128]{2,1,0:T(8,128)S(1)}, f32[48,8,128]{2,1,0:T(8,128)S(1)}, u32[]{:S(2)}, u32[]{:S(2)}) collective-permute-start(f32[48,8,128]{2,1,0:T(8,128)S(1)} %pad_maximum_fusion.1), channel_id=1, source_target_pairs={{0,32},{32,0},{64,96},{96,64},{128,160},{160,128},{192,224},{224,1... | collective-permute-start | bytes 589832 | tf_op jit(solution)/shard_map/ppermute | solution.py:50
  25.5 8.0 %collective-permute-start.9 = (f32[24,8,256]{2,1,0:T(8,128)S(1)}, f32[24,8,256]{2,1,0:T(8,128)S(1)}, u32[]{:S(2)}, u32[]{:S(2)}) collective-permute-start(f32[24,8,256]{2,1,0:T(8,128)S(1)} %get-tuple-element.65), channel_id=1, source_target_pairs={{0,1},{1,0},{2,3},{3,2},{4,5},{5,4},{6,7},{7,6},{8,9},{9,8},{10,11... | collective-permute-start | bytes 589832 | tf_op jit(solution)/shard_map/ppermute | solution.py:36
  25.6 7.9 %collective-permute-start.10 = (f32[24,8,256]{2,1,0:T(8,128)S(1)}, f32[24,8,256]{2,1,0:T(8,128)S(1)}, u32[]{:S(2)}, u32[]{:S(2)}) collective-permute-start(f32[24,8,256]{2,1,0:T(8,128)S(1)} %get-tuple-element.66), channel_id=1, source_target_pairs={{0,8},{1,2},{2,1},{3,4},{4,3},{5,6},{6,5},{7,15},{8,0},{9,10},{10,... | collective-permute-start | bytes 589832 | tf_op jit(solution)/shard_map/ppermute | solution.py:46
  29.8 1.5 %collective-permute-start.11 = (f32[8,8,256]{2,1,0:T(8,128)S(1)}, f32[8,8,256]{2,1,0:T(8,128)S(1)}, u32[]{:S(2)}, u32[]{:S(2)}) collective-permute-start(f32[8,8,256]{2,1,0:T(8,128)S(1)} %get-tuple-element.67), channel_id=1, source_target_pairs={{0,8},{8,0},{16,24},{24,16},{1,9},{9,1},{17,25},{25,17},{2,10},{10... | collective-permute-start | bytes 196616 | tf_op jit(solution)/shard_map/ppermute | solution.py:36
  29.8 3.7 %collective-permute-start.12 = (f32[8,8,256]{2,1,0:T(8,128)S(1)}, f32[8,8,256]{2,1,0:T(8,128)S(1)}, u32[]{:S(2)}, u32[]{:S(2)}) collective-permute-start(f32[8,8,256]{2,1,0:T(8,128)S(1)} %get-tuple-element.68), channel_id=1, source_target_pairs={{0,24},{8,16},{16,8},{24,0},{1,25},{9,17},{17,9},{25,1},{2,26},{10... | collective-permute-start | bytes 196616 | tf_op jit(solution)/shard_map/ppermute | solution.py:36
  31.1 7.6 %collective-permute-start.17 = (f32[24,8,256]{2,1,0:T(8,128)S(1)}, f32[24,8,256]{2,1,0:T(8,128)S(1)}, u32[]{:S(2)}, u32[]{:S(2)}) collective-permute-start(f32[24,8,256]{2,1,0:T(8,128)S(1)} %get-tuple-element.81), channel_id=1, source_target_pairs={{0,1},{1,0},{2,3},{3,2},{4,5},{5,4},{6,7},{7,6},{8,9},{9,8},{10,11... | collective-permute-start | bytes 589832 | tf_op jit(solution)/shard_map/ppermute | solution.py:36
  31.2 8.8 %collective-permute-start.18 = (f32[24,8,256]{2,1,0:T(8,128)S(1)}, f32[24,8,256]{2,1,0:T(8,128)S(1)}, u32[]{:S(2)}, u32[]{:S(2)}) collective-permute-start(f32[24,8,256]{2,1,0:T(8,128)S(1)} %get-tuple-element.82), channel_id=1, source_target_pairs={{0,8},{1,2},{2,1},{3,4},{4,3},{5,6},{6,5},{7,15},{8,0},{9,10},{10,... | collective-permute-start | bytes 589832 | tf_op jit(solution)/shard_map/ppermute | solution.py:46
  35.4 7.4 %collective-permute-start.13 = (f32[24,8,256]{2,1,0:T(8,128)S(1)}, f32[24,8,256]{2,1,0:T(8,128)S(1)}, u32[]{:S(2)}, u32[]{:S(2)}) collective-permute-start(f32[24,8,256]{2,1,0:T(8,128)S(1)} %get-tuple-element.71), channel_id=1, source_target_pairs={{0,1},{1,0},{2,3},{3,2},{4,5},{5,4},{6,7},{7,6},{8,9},{9,8},{10,11... | collective-permute-start | bytes 589832 | tf_op jit(solution)/shard_map/ppermute | solution.py:36
  35.5 7.6 %collective-permute-start.14 = (f32[24,8,256]{2,1,0:T(8,128)S(1)}, f32[24,8,256]{2,1,0:T(8,128)S(1)}, u32[]{:S(2)}, u32[]{:S(2)}) collective-permute-start(f32[24,8,256]{2,1,0:T(8,128)S(1)} %get-tuple-element.72), channel_id=1, source_target_pairs={{0,8},{1,2},{2,1},{3,4},{4,3},{5,6},{6,5},{7,15},{8,0},{9,10},{10,... | collective-permute-start | bytes 589832 | tf_op jit(solution)/shard_map/ppermute | solution.py:46
  38.7 3.6 %collective-permute-start.15 = (f32[4,8,256]{2,1,0:T(8,128)S(1)}, f32[4,8,256]{2,1,0:T(8,128)S(1)}, u32[]{:S(2)}, u32[]{:S(2)}) collective-permute-start(f32[4,8,256]{2,1,0:T(8,128)S(1)} %get-tuple-element.73), channel_id=1, source_target_pairs={{0,8},{8,0},{16,24},{24,16},{1,9},{9,1},{17,25},{25,17},{2,10},{10... | collective-permute-start | bytes 98312 | tf_op jit(solution)/shard_map/ppermute | solution.py:36
  38.7 3.6 %collective-permute-start.16 = (f32[4,8,256]{2,1,0:T(8,128)S(1)}, f32[4,8,256]{2,1,0:T(8,128)S(1)}, u32[]{:S(2)}, u32[]{:S(2)}) collective-permute-start(f32[4,8,256]{2,1,0:T(8,128)S(1)} %get-tuple-element.74), channel_id=1, source_target_pairs={{0,24},{8,16},{16,8},{24,0},{1,25},{9,17},{17,9},{25,1},{2,26},{10... | collective-permute-start | bytes 98312 | tf_op jit(solution)/shard_map/ppermute | solution.py:36
  44.0 8.2 %collective-permute-start.19 = (f32[2,24,8,128]{3,2,1,0:T(8,128)S(1)}, f32[2,24,8,128]{3,2,1,0:T(8,128)S(1)}, u32[]{:S(2)}, u32[]{:S(2)}) collective-permute-start(f32[2,24,8,128]{3,2,1,0:T(8,128)S(1)} %get-tuple-element.88), channel_id=1, source_target_pairs={{0,128},{32,160},{64,192},{96,224},{128,0},{160,32},{192,64},{224,... | collective-permute-start | bytes 589832 | tf_op jit(solution)/shard_map/ppermute | solution.py:54
  44.7 10.2 %collective-permute-start.21 = (f32[2,24,8,128]{3,2,1,0:T(8,128)S(1)}, f32[2,24,8,128]{3,2,1,0:T(8,128)S(1)}, u32[]{:S(2)}, u32[]{:S(2)}) collective-permute-start(f32[2,24,8,128]{3,2,1,0:T(8,128)S(1)} %get-tuple-element.92), channel_id=1, source_target_pairs={{0,32},{32,0},{64,96},{96,64},{128,160},{160,128},{192,224},{224,1... | collective-permute-start | bytes 589832 | tf_op jit(solution)/shard_map/ppermute | solution.py:50
  52.2 6.2 %collective-permute-start.20 = (f32[24,8,128]{2,1,0:T(8,128)S(1)}, f32[24,8,128]{2,1,0:T(8,128)S(1)}, u32[]{:S(2)}, u32[]{:S(2)}) collective-permute-start(f32[24,8,128]{2,1,0:T(8,128)S(1)} %get-tuple-element.90), channel_id=1, source_target_pairs={{0,32},{32,0},{64,96},{96,64},{128,160},{160,128},{192,224},{224,1... | collective-permute-start | bytes 294920 | tf_op jit(solution)/shard_map/ppermute | solution.py:50
  54.9 4.7 %collective-permute-start.22 = (f32[24,8,128]{2,1,0:T(8,128)S(1)}, f32[24,8,128]{2,1,0:T(8,128)S(1)}, u32[]{:S(2)}, u32[]{:S(2)}) collective-permute-start(f32[24,8,128]{2,1,0:T(8,128)S(1)} %get-tuple-element.93), channel_id=1, source_target_pairs={{0,64},{32,96},{64,0},{96,32},{128,192},{160,224},{192,128},{224,1... | collective-permute-start | bytes 294920 | tf_op jit(solution)/shard_map/ppermute | solution.py:58
  55.6 5.8 %collective-permute-start.23 = (f32[24,8,128]{2,1,0:T(8,128)S(1)}, f32[24,8,128]{2,1,0:T(8,128)S(1)}, u32[]{:S(2)}, u32[]{:S(2)}) collective-permute-start(f32[24,8,128]{2,1,0:T(8,128)S(1)} %get-tuple-element.94), channel_id=1, source_target_pairs={{0,192},{32,224},{64,128},{96,160},{128,64},{160,96},{192,0},{224,... | collective-permute-start | bytes 294920 | tf_op jit(solution)/shard_map/ppermute | solution.py:58

commit v5 on v4

--- a/solution.py
+++ b/solution.py
@@ -9,7 +9,7 @@
 
 F32 = jnp.float32
 BF16 = jnp.bfloat16
-GROUP = 16
+GROUP = 24
 LIMIT = 24 * 1024 * 1024
 
 S0, S1, S2 = -2.5, 4.0 / 3.0, -1.0 / 12.0
@@ -103,13 +103,19 @@
         face_x(field[0:2], field[n - 2 : n], inner, outer, f)
 
 
-def fill(pad, field, inner, outer, f):
+def extended(field, inner, outer, f):
     n = field.shape[0]
     gx, at_even = lax.axis_index("gx"), even("gx")
     inner, outer = inner[2 * f : 2 * f + 2], outer[2 * f : 2 * f + 2]
-    pad[2 : n + 2] = field[...]
-    pad[0:2] = jnp.where(gx > 0, jnp.where(at_even, outer, inner), 0.0)
-    pad[n + 2 : n + 4] = jnp.where(gx < lax.axis_size("gx") - 1, jnp.where(at_even, inner, outer), 0.0)
+    before = jnp.where(gx > 0, jnp.where(at_even, outer, inner), 0.0)
+    after = jnp.where(gx < lax.axis_size("gx") - 1, jnp.where(at_even, inner, outer), 0.0)
+
+    def slab(x, t):
+        if 0 <= x < n:
+            return field[x, :, pl.ds(128 * t, 128)]
+        return (before[x + 2] if x < 0 else after[x - n])[:, 128 * t : 128 * t + 128]
+
+    return slab
 
 
 def edge_rows(inner, outer, x, f, half):
@@ -135,16 +141,14 @@
         values = values - part.astype(F32)
         term = jnp.dot(part, matrix, preferred_element_type=F32)
         total = term if total is None else total + term
-    return total * (1.0 / 12.0)
-
-
-def lateral(pad, x, edge, slope=True):
+    return total
+
+
+def lateral(slab, x, edge, slope=True):
     row = rows()
     horizontal, slopes, centre = [], [], []
     for t in (0, 1):
-        tile = pl.ds(128 * t, 128)
-        c = pad[x + 2, :, tile]
-        xl, xh, xl2, xh2 = (pad[x + k, :, tile] for k in (1, 3, 0, 4))
+        c, xl, xh, xl2, xh2 = (slab(x + k, t) for k in (0, -1, 1, -2, 2))
         e = edge[t]
         yl = pltpu.roll(jnp.where(row == 7, e, c), 1, 0)
         yl2 = pltpu.roll(jnp.where(row >= 6, e, c), 2, 0)
@@ -152,7 +156,7 @@
         yh2 = pltpu.roll(jnp.where(row <= 1, e, c), 6, 0)
         horizontal.append(2.0 * S0 * c + S1 * ((xl + xh) + (yl + yh)) + S2 * ((xl2 + xh2) + (yl2 + yh2)))
         if slope:
-            slopes.append(D1 * ((xh - xl) + (yh - yl)) + D2 * ((xh2 - xl2) + (yh2 - yl2)))
+            slopes.append((D1 / 12.0) * ((xh - xl) + (yh - yl)) + (D2 / 12.0) * ((xh2 - xl2) + (yh2 - yl2)))
         centre.append(c)
     return horizontal, slopes, centre
 
@@ -161,11 +165,10 @@
     return jnp.concatenate([jnp.concatenate(pair, axis=1) for pair in lists], axis=0)
 
 
-def derivs(pad, before, after, f, zmat, emit):
-    nx = pad.shape[0] - 4
+def derivs(slab, nx, before, after, f, zmat, emit):
     for at in range(0, nx, GROUP):
-        found = [lateral(pad, x, edge_rows(before, after, x, f, nx // 2)) for x in range(at, at + GROUP)]
-        vertical = along_z(slabs([c for _, _, c in found]), zmat[0])
+        found = [lateral(slab, x, edge_rows(before, after, x, f, nx // 2)) for x in range(at, at + GROUP)]
+        vertical = along_z(slabs([c for _, _, c in found]), zmat[0]) * (1.0 / 12.0)
         mixed = along_z(slabs([s for _, s, _ in found]), zmat[1])
         for j, (horizontal, _, centre) in enumerate(found):
             for t in (0, 1):
@@ -175,7 +178,7 @@
 
 def second_z(field, zmat, emit):
     for at in range(0, field.shape[0], GROUP):
-        vertical = along_z(field[at : at + GROUP].reshape(GROUP * 8, field.shape[2]), zmat[0])
+        vertical = along_z(field[at : at + GROUP].reshape(GROUP * 8, field.shape[2]), zmat[0]) * (1.0 / 12.0)
         for j in range(GROUP):
             for t in (0, 1):
                 emit(at + j, t, vertical[8 * j : 8 * j + 8, 128 * t : 128 * t + 128])
@@ -240,13 +243,10 @@
 
 def first_kernel(
     plane, zmat, u, um, l, lm, ylo, yhi, inner, outer, speed, epsilon, delta, tilt,
-    u1, l1, hu, vu, hl, vl, padu, padl,
+    u1, l1, hu, vu, hl, vl,
 ):
     model = (speed, epsilon, delta, tilt)
-    for f, (pad, w, prev, new, h_out, v_out) in enumerate(
-        ((padu, u, um, u1, hu, vu), (padl, l, lm, l1, hl, vl))
-    ):
-        fill(pad, w.at[0], inner, outer, f)
+    for f, (w, prev, new, h_out, v_out) in enumerate(((u, um, u1, hu, vu), (l, lm, l1, hl, vl))):
 
         def emit(x, t, h, v, m, c, f=f, prev=prev, new=new, h_out=h_out, v_out=v_out):
             tile = pl.ds(128 * t, 128)
@@ -257,7 +257,8 @@
                 value = value + plane[0, :, tile]
             new[x, :, tile] = value
 
-        derivs(pad, ylo, yhi, f, zmat, emit)
+        slab = extended(w.at[0], inner, outer, f)
+        derivs(slab, w.shape[1], ylo, yhi, f, zmat, emit)
 
 
 def born_kernel(
@@ -297,11 +298,9 @@
 
 def second_kernel(
     plane, zmat, u, u1, b1, q1, q2, ylo, yhi, inner, outer, speed, epsilon, delta, tilt,
-    u2, b2, hu, vu, hb, vb, yup, ydn, inner_out, outer_out, padu, padb,
+    u2, b2, hu, vu, hb, vb, yup, ydn, inner_out, outer_out,
 ):
     model = (speed, epsilon, delta, tilt)
-    fill(padu, u1, inner, outer, 0)
-    fill(padb, b1, inner, outer, 1)
 
     def emit_u(x, t, h, v, m, c):
         tile = pl.ds(128 * t, 128)
@@ -321,8 +320,8 @@
             + (q1[x, :, tile] * hu[x, :, tile] + q2[x, :, tile] * vu[x, :, tile])
         )
 
-    derivs(padu, ylo, yhi, 0, zmat, emit_u)
-    derivs(padb, ylo, yhi, 1, zmat, emit_b)
+    derivs(extended(u1, inner, outer, 0), u1.shape[0], ylo, yhi, 0, zmat, emit_u)
+    derivs(extended(b1, inner, outer, 1), b1.shape[0], ylo, yhi, 1, zmat, emit_b)
     fields = [u2, b2]
     pack_y(fields, yup, ydn)
     pack_x(fields, inner_out, outer_out)
@@ -358,11 +357,9 @@
 
 def adjoint_kernel(
     zmat, l, l1, d1, b1, q1, q2, counts, hu, vu, hb, vb, u2, b2, ylo, yhi, inner, outer,
-    speed, epsilon, delta, tilt, l2, d2, a1, c1, padl, padd, hl, vl,
+    speed, epsilon, delta, tilt, l2, d2, a1, c1, hl, vl,
 ):
     model = (speed, epsilon, delta, tilt)
-    fill(padl, l1, inner, outer, 2)
-    fill(padd, d1, inner, outer, 3)
 
     def emit_l(x, t, h, v, m, c):
         tile = pl.ds(128 * t, 128)
@@ -380,8 +377,8 @@
         a1[x, :, tile] = hu[x, :, tile] * c + hb[x, :, tile] * l1[x, :, tile]
         c1[x, :, tile] = vu[x, :, tile] * c + vb[x, :, tile] * l1[x, :, tile]
 
-    derivs(padl, ylo, yhi, 0, zmat, emit_l)
-    derivs(padd, ylo, yhi, 1, zmat, emit_d)
+    derivs(extended(l1, inner, outer, 2), l1.shape[0], ylo, yhi, 0, zmat, emit_l)
+    derivs(extended(d1, inner, outer, 3), d1.shape[0], ylo, yhi, 1, zmat, emit_d)
 
     for field, other in ((u2, d2), (b2, l2)):
 
@@ -393,14 +390,13 @@
 
 
 def image_kernel(
-    u2, b2, ylo, yhi, inner, outer, l2, d2, a1, c1, near, far, opposite, beside, padu, padb, total, chunks,
+    u2, b2, ylo, yhi, inner, outer, l2, d2, a1, c1, near, far, opposite, beside, total, chunks,
 ):
-    for f, (pad, w) in enumerate(((padu, u2), (padb, b2))):
-        fill(pad, w, inner, outer, f)
+    fields = [extended(w, inner, outer, f) for f, w in enumerate((u2, b2))]
     nx = u2.shape[0]
     for x in range(nx):
         hu, hb = (
-            lateral(pad, x, edge_rows(ylo, yhi, x, f, nx // 2), False)[0] for f, pad in enumerate((padu, padb))
+            lateral(w, x, edge_rows(ylo, yhi, x, f, nx // 2), False)[0] for f, w in enumerate(fields)
         )
         for t in (0, 1):
             tile = pl.ds(128 * t, 128)
@@ -465,7 +461,6 @@
 ):
     nx, ny, nz = speed.shape
     whole = (nx, ny, nz)
-    pad = pltpu.VMEM((nx + 4, ny, nz), F32)
     half_rows = (nx // 2, ny, nz)
     layers = [half_rows] * 2 + [(4, ny, nz)] * 2
     packed = (nx // 2, ny, 128)
@@ -505,11 +500,11 @@
         name="chunk",
     )
     partner, inner, outer = across(mine), beside_y(mine), beside_y(mine, True)
+    pair = jnp.concatenate([mine, partner], axis=0)
     *sent, zmat = call(
-        first_y_kernel, layers[:2] + [((2, nz, nz), BF16)], now, after=(mine, *x0), name="layers_y"
+        first_y_kernel, layers[:2] + [((2, nz, nz), BF16)], now, after=(pair, *x0), name="layers_y"
     )
     y0 = exchange_y(*sent)
-    pair = jnp.concatenate([mine, partner], axis=0)
     opposite = opposite_y(pair)
     beside = across(jnp.concatenate([inner, outer], axis=0))
     steps = wavelet.shape[1]
@@ -525,7 +520,6 @@
         first_kernel,
         [whole] * 6,
         (plane, zmat, forward_now, forward_prev, adjoint_now, adjoint_prev) + y0 + x0 + model,
-        [pad, pad],
         name="first",
     )
     q1, q2, b1, d1, yup, ydn, inner_out, outer_out = call(
@@ -542,7 +536,6 @@
         second_kernel,
         [whole] * 6 + layers,
         (plane, zmat, forward_now, u1, b1, q1, q2) + y_ub + x1 + model,
-        [pad, pad],
         name="second",
     )
     halo = exchange_y(yup, ydn) + exchange_x(inner_out, outer_out)
@@ -550,14 +543,14 @@
         adjoint_kernel,
         [whole] * 4,
         (zmat, adjoint_now, l1, d1, b1, q1, q2, counts, hu1, vu1, hb1, vb1, u2, b2) + y_ld + x1 + model,
-        [pad, pad, pltpu.VMEM(whole, F32), pltpu.VMEM(whole, F32)],
+        [pltpu.VMEM(whole, F32), pltpu.VMEM(whole, F32)],
         name="adjoint",
     )
     near, far, opposite, beside = call(
         image_kernel,
         [(2,) + packed] * 4,
         (u2, b2) + halo + (l2, d2, a1, c1),
-        [pad, pad, pltpu.VMEM(whole, F32), pltpu.VMEM((8,) + packed, F32)],
+        [pltpu.VMEM(whole, F32), pltpu.VMEM((8,) + packed, F32)],
         name="image",
     )
     own, other = call(add_kernel, [packed] * 2, (near, opposite_y(opposite)), name="add_opposite")

time: 62.9 us -> 62.5 us (level)
  starting transfers between devices: 33.9 us -> 32.7 us
  waiting for transfers between devices: 15.2 us -> 16.1 us
    ppermute x10, waiting for transfers between devices: 0.75 us -> 3.04 us  [pairs(): return lax.ppermute(value, axis, list(enumerate(other)))]
    ppermute x4, starting transfers between devices: 4.96 us -> 6.59 us  [beside_y(): lax.ppermute(value, 'shot', [(i, neighbour(i // 2, outer) * 2 + i % 2) fo...]
    ppermute x4, waiting for transfers between devices: 5.22 us -> 3.73 us  [across(): return lax.ppermute(value, 'shot', [(i, i ^ 1) for i in range(8)])]
    ppermute x4, starting transfers between devices: 9.08 us -> 7.68 us  [across(): return lax.ppermute(value, 'shot', [(i, i ^ 1) for i in range(8)])]
    ppermute x4, waiting for transfers between devices: 3.09 us -> 1.79 us  [beside_y(): lax.ppermute(value, 'shot', [(i, neighbour(i // 2, outer) * 2 + i % 2) fo...]
    ppermute x4, waiting for transfers between devices: 0.31 us -> 1.6 us  [outer_y(): return lax.ppermute(value, ('gx', 'gy'), swaps)]
    ppermute x10, starting transfers between devices: 3.84 us -> 2.69 us  [pairs(): return lax.ppermute(value, axis, list(enumerate(other)))]
  transfers between devices with their start and end apart: 24 -> 24, of which waited for: 9 -> 11; matrix products, arithmetic and copies ran while one was open for 0% -> 0% of each run, Pallas kernels for 11% -> 11%
where the time goes in v5:
time: 62.5 us; the launch traced here: 62.4 us
  starting transfers between devices  32.7 us (52%)
  waiting for transfers between devices  16.1 us (26%)
  Pallas kernels  9.6 us (15%)
  local copies, waits for them, and re-layouts  3.03 us (5%)
  between operations  0.91 us (1%)
    ppermute x4, starting transfers between devices, outer_y(): return lax.ppermute(value, ('gx', 'gy'), swaps)  12.9 us
    pallas_call x13, Pallas kernels, call(): pl.pallas_call(kernel, out_shape=[jax.ShapeDtypeStruct(*out) for out in t...  9.58 us
    ppermute x4, starting transfers between devices, across(): return lax.ppermute(value, 'shot', [(i, i ^ 1) for i in range(8)])  7.68 us
    ppermute x4, starting transfers between devices, beside_y(): lax.ppermute(value, 'shot', [(i, neighbour(i // 2, outer) * 2 + i % 2) fo...  6.59 us
    ppermute x2, waiting for transfers between devices, opposite_y(): return lax.ppermute(value, 'shot', [(i, (i + 4) % 8) for i in range(8)])  5.94 us
    ppermute x4, waiting for transfers between devices, across(): return lax.ppermute(value, 'shot', [(i, i ^ 1) for i in range(8)])  3.73 us
    ppermute x10, waiting for transfers between devices, pairs(): return lax.ppermute(value, axis, list(enumerate(other)))  3.04 us
    ppermute x2, starting transfers between devices, opposite_y(): return lax.ppermute(value, 'shot', [(i, (i + 4) % 8) for i in range(8)])  2.88 us
  transfers between devices with their start and end apart: 24, of which 11 were waited for; matrix products, arithmetic and copies ran while one was open for 0% of the time, Pallas kernels for 11%

profile of v5, /device:TPU:32, one launch (start us, length us, event | category | flops | bytes accessed | tf_op | source)
XLA Modules:
  0.0 62.4 jit_solution(2562489304823129697)
XLA Ops:
  0.0 1.3 %copy.14.p = f32[3,48,8,32]{3,2,1,0:T(8,128)S(1)} copy(f32[3,48,8,32]{1,3,2,0:T(8,128)} %param.16) | data formatting | bytes 294912 | tf_op args[4]
  1.4 0.3 half_chunk.1.rest_0_
  1.7 0.7 %copy-done.3 = f32[48,8,256]{2,1,0:T(8,128)S(1)} copy-done((f32[48,8,256]{2,1,0:T(8,128)S(1)}, f32[48,8,256]{2,1,0:T(8,128)}, u32[]{:S(2)}) %copy-start.3) | copy-done | bytes 393240
  2.4 0.3 chunk.1.mine
  2.6 3.1 %collective-permute-start = (f32[24,8,128]{2,1,0:T(8,128)S(1)}, f32[24,8,128]{2,1,0:T(8,128)S(1)}, u32[]{:S(2)}, u32[]{:S(2)}) collective-permute-start(f32[24,8,128]{2,1,0:T(8,128)S(1)} %chunk.1.mine), channel_id=1, source_target_pairs={{0,32},{32,0},{64,96},{96,64},{128,160},{160,128},{192,224},{224,1... | collective-permute-start | bytes 294920 | tf_op jit(solution)/shard_map/ppermute | solution.py:50
  5.8 1.6 %collective-permute-start.5 = (f32[24,8,128]{2,1,0:T(8,128)S(1)}, f32[24,8,128]{2,1,0:T(8,128)S(1)}, u32[]{:S(2)}, u32[]{:S(2)}) collective-permute-start(f32[24,8,128]{2,1,0:T(8,128)S(1)} %chunk.1.mine), channel_id=1, source_target_pairs={{0,64},{32,96},{64,0},{96,32},{128,192},{160,224},{192,128},{224,1... | collective-permute-start | bytes 294920 | tf_op jit(solution)/shard_map/ppermute | solution.py:58
  7.3 2.2 %collective-permute-start.6 = (f32[24,8,128]{2,1,0:T(8,128)S(1)}, f32[24,8,128]{2,1,0:T(8,128)S(1)}, u32[]{:S(2)}, u32[]{:S(2)}) collective-permute-start(f32[24,8,128]{2,1,0:T(8,128)S(1)} %chunk.1.mine), channel_id=1, source_target_pairs={{0,192},{32,224},{64,128},{96,160},{128,64},{160,96},{192,0},{224,... | collective-permute-start | bytes 294920 | tf_op jit(solution)/shard_map/ppermute | solution.py:58
  9.6 0.1 collective-permute-start.1
  9.7 0.7 %collective-permute-start.2 = (f32[4,8,256]{2,1,0:T(8,128)S(1)}, f32[4,8,256]{2,1,0:T(8,128)S(1)}, u32[]{:S(2)}, u32[]{:S(2)}) collective-permute-start(f32[4,8,256]{2,1,0:T(8,128)S(1)} %get-tuple-element.51), channel_id=1, source_target_pairs={{0,24},{8,16},{16,8},{24,0},{1,25},{9,17},{17,9},{25,1},{2,26},{10... | collective-permute-start | bytes 98312 | tf_op jit(solution)/shard_map/ppermute | solution.py:36
  10.4 1.8 %collective-permute-start.7 = (f32[48,8,128]{2,1,0:T(8,128)S(1)}, f32[48,8,128]{2,1,0:T(8,128)S(1)}, u32[]{:S(2)}, u32[]{:S(2)}) collective-permute-start(f32[48,8,128]{2,1,0:T(8,128)S(1)} %pad_maximum_fusion.rest_0_), channel_id=1, source_target_pairs={{0,128},{32,160},{64,192},{96,224},{128,0},{160,32},{192,64},{224,... | collective-permute-start | bytes 589832 | tf_op jit(solution)/shard_map/ppermute | solution.py:54
  12.2 0.9 %collective-permute-done.2.rest_2_.outer = f32[4,8,256]{2,1,0:T(8,128)S(1)} collective-permute-done((f32[4,8,256]{2,1,0:T(8,128)S(1)}, f32[4,8,256]{2,1,0:T(8,128)S(1)}, u32[]{:S(2)}, u32[]{:S(2)}) %collective-permute-start.2) | collective-permute-done | bytes 32800 | tf_op jit(solution)/shard_map/ppermute | solution.py:36
  13.1 0.2 layers_y.1
  13.3 0.2 collective-permute-start.3
  13.5 3.7 %collective-permute-start.4 = (f32[24,8,256]{2,1,0:T(8,128)S(1)}, f32[24,8,256]{2,1,0:T(8,128)S(1)}, u32[]{:S(2)}, u32[]{:S(2)}) collective-permute-start(f32[24,8,256]{2,1,0:T(8,128)S(1)} %get-tuple-element.53.rest_2_), channel_id=1, source_target_pairs={{0,8},{1,2},{2,1},{3,4},{4,3},{5,6},{6,5},{7,15},{8,0},{9,10},{10,... | collective-permute-start | bytes 589832 | tf_op jit(solution)/shard_map/ppermute | solution.py:46
  17.3 2.2 %collective-permute-start.8 = (f32[48,8,128]{2,1,0:T(8,128)S(1)}, f32[48,8,128]{2,1,0:T(8,128)S(1)}, u32[]{:S(2)}, u32[]{:S(2)}) collective-permute-start(f32[48,8,128]{2,1,0:T(8,128)S(1)} %pad_maximum_fusion.1), channel_id=1, source_target_pairs={{0,32},{32,0},{64,96},{96,64},{128,160},{160,128},{192,224},{224,1... | collective-permute-start | bytes 589832 | tf_op jit(solution)/shard_map/ppermute | solution.py:50
  20.1 1.0 %counts.1 = (f32[48,8,256]{2,1,0:T(8,128)S(1)}, f32[2,8,256]{2,1,0:T(8,128)S(1)}) custom-call(s32[1,1536]{1,0:T(1,128)S(1)} %copy-done.8, f32[1,2]{1,0:T(1,128)S(1)} %copy-done.9, s32[1]{0:T(128)S(6)} %copy.16.source, f32[48,8,128]{2,1,0:T(8,128)S(1)} %pad_maximum_fusion.rest_0_, f32[24,8,256]{2,1,0:T(8,128)S(1)} %get-tuple-element.52.rest_1_, ...), custom_call_target="tpu_custom_call" | custom-call | tf_op jit(solution)/shard_map/counts/pallas_call | solution.py:22
  21.2 1.3 %collective-permute-done.4.yhi = f32[24,8,256]{2,1,0:T(8,128)S(1)} collective-permute-done((f32[24,8,256]{2,1,0:T(8,128)S(1)}, f32[24,8,256]{2,1,0:T(8,128)S(1)}, u32[]{:S(2)}, u32[]{:S(2)}) %collective-permute-start.4) | collective-permute-done | bytes 196640 | tf_op jit(solution)/shard_map/ppermute | solution.py:46
  22.4 1.7 %first.1 = (f32[48,8,256]{2,1,0:T(8,128)S(1)}, f32[48,8,256]{2,1,0:T(8,128)S(1)}, f32[48,8,256]{2,1,0:T(8,128)S(1)}, f32[48,8,256]{2,1,0:T(8,128)S(1)}, f32[48,8...) custom-call(f32[2,8,256]{2,1,0:T(8,128)S(1)} %get-tuple-element.54.plane, bf16[2,256,256]{2,1,0:T(8,128)(2,1)S(1)} %get-tuple-element.55.zmat, ...), custom_call_target="tpu_custom_call" | custom-call | tf_op jit(solution)/shard_map/first/pallas_call | solution.py:22
  24.1 1.4 %collective-permute-done.8.beside = f32[48,8,128]{2,1,0:T(8,128)S(1)} collective-permute-done((f32[48,8,128]{2,1,0:T(8,128)S(1)}, f32[48,8,128]{2,1,0:T(8,128)S(1)}, u32[]{:S(2)}, u32[]{:S(2)}) %collective-permute-start.8) | collective-permute-done | bytes 196640 | tf_op jit(solution)/shard_map/ppermute | solution.py:50
  25.5 0.7 %born.1 = (f32[48,8,256]{2,1,0:T(8,128)S(1)}, f32[48,8,256]{2,1,0:T(8,128)S(1)}, f32[48,8,256]{2,1,0:T(8,128)S(1)}, f32[48,8,256]{2,1,0:T(8,128)S(1)}, f32[24,8,...) custom-call(f32[24,8,128]{2,1,0:T(8,128)S(1)} %chunk.1.mine, ...), custom_call_target="tpu_custom_call" | custom-call | tf_op jit(solution)/shard_map/born/pallas_call | solution.py:22
  26.3 0.1 collective-permute-start.9
  26.4 4.1 %collective-permute-start.10 = (f32[24,8,256]{2,1,0:T(8,128)S(1)}, f32[24,8,256]{2,1,0:T(8,128)S(1)}, u32[]{:S(2)}, u32[]{:S(2)}) collective-permute-start(f32[24,8,256]{2,1,0:T(8,128)S(1)} %get-tuple-element.66), channel_id=1, source_target_pairs={{0,8},{1,2},{2,1},{3,4},{4,3},{5,6},{6,5},{7,15},{8,0},{9,10},{10,... | collective-permute-start | bytes 589832 | tf_op jit(solution)/shard_map/ppermute | solution.py:46
  30.5 0.7 %collective-permute-start.12 = (f32[8,8,256]{2,1,0:T(8,128)S(1)}, f32[8,8,256]{2,1,0:T(8,128)S(1)}, u32[]{:S(2)}, u32[]{:S(2)}) collective-permute-start(f32[8,8,256]{2,1,0:T(8,128)S(1)} %get-tuple-element.68), channel_id=1, source_target_pairs={{0,24},{8,16},{16,8},{24,0},{1,25},{9,17},{17,9},{25,1},{2,26},{10... | collective-permute-start | bytes 196616 | tf_op jit(solution)/shard_map/ppermute | solution.py:36
  31.2 0.1 adjoint_y.1
  31.3 0.1 collective-permute-start.17
  31.4 0.3 collective-permute-done.11.inner
  31.8 1.7 %collective-permute-start.18 = (f32[24,8,256]{2,1,0:T(8,128)S(1)}, f32[24,8,256]{2,1,0:T(8,128)S(1)}, u32[]{:S(2)}, u32[]{:S(2)}) collective-permute-start(f32[24,8,256]{2,1,0:T(8,128)S(1)} %get-tuple-element.82), channel_id=1, source_target_pairs={{0,8},{1,2},{2,1},{3,4},{4,3},{5,6},{6,5},{7,15},{8,0},{9,10},{10,... | collective-permute-start | bytes 589832 | tf_op jit(solution)/shard_map/ppermute | solution.py:46
  33.5 0.8 %collective-permute-done.12.outer = f32[8,8,256]{2,1,0:T(8,128)S(1)} collective-permute-done((f32[8,8,256]{2,1,0:T(8,128)S(1)}, f32[8,8,256]{2,1,0:T(8,128)S(1)}, u32[]{:S(2)}, u32[]{:S(2)}) %collective-permute-start.12) | collective-permute-done | bytes 65568 | tf_op jit(solution)/shard_map/ppermute | solution.py:36
  34.3 0.0 collective-permute-done.10.yhi
  34.3 1.9 %second.1 = (f32[48,8,256]{2,1,0:T(8,128)S(1)}, f32[48,8,256]{2,1,0:T(8,128)S(1)}, f32[48,8,256]{2,1,0:T(8,128)S(1)}, f32[48,8,256]{2,1,0:T(8,128)S(1)}, f32[48,...) custom-call(f32[2,8,256]{2,1,0:T(8,128)S(1)} %get-tuple-element.54.p, ...), custom_call_target="tpu_custom_call" | custom-call | tf_op jit(solution)/shard_map/second/pallas_call | solution.py:22
  36.2 0.1 collective-permute-start.13
  36.3 3.3 %collective-permute-start.14 = (f32[24,8,256]{2,1,0:T(8,128)S(1)}, f32[24,8,256]{2,1,0:T(8,128)S(1)}, u32[]{:S(2)}, u32[]{:S(2)}) collective-permute-start(f32[24,8,256]{2,1,0:T(8,128)S(1)} %get-tuple-element.72), channel_id=1, source_target_pairs={{0,8},{1,2},{2,1},{3,4},{4,3},{5,6},{6,5},{7,15},{8,0},{9,10},{10,... | collective-permute-start | bytes 589832 | tf_op jit(solution)/shard_map/ppermute | solution.py:46
  39.6 0.7 %collective-permute-start.16 = (f32[4,8,256]{2,1,0:T(8,128)S(1)}, f32[4,8,256]{2,1,0:T(8,128)S(1)}, u32[]{:S(2)}, u32[]{:S(2)}) collective-permute-start(f32[4,8,256]{2,1,0:T(8,128)S(1)} %get-tuple-element.74), channel_id=1, source_target_pairs={{0,24},{8,16},{16,8},{24,0},{1,25},{9,17},{17,9},{25,1},{2,26},{10... | collective-permute-start | bytes 98312 | tf_op jit(solution)/shard_map/ppermute | solution.py:36
  40.3 2.2 %adjoint.1 = (f32[48,8,256]{2,1,0:T(8,128)S(1)}, f32[48,8,256]{2,1,0:T(8,128)S(1)}, f32[48,8,256]{2,1,0:T(8,128)S(1)}, f32[48,8,256]{2,1,0:T(8,128)S(1)}) custom-call(bf16[2,256,256]{2,1,0:T(8,128)(2,1)S(1)} %get-tuple-element.55.zmat, f32[1,48,8,256]{3,2,1,0:T(8,128)S(1)} %copy-done.1, f32[48,8,256]{2,1,0:T(8,128)S(1)} %get-tuple-element.57.l1.a, ...), custom_call_target="tpu_custom_call" | custom-call | tf_op jit(solution)/shard_map/adjoint/pallas_call | solution.py:22
  42.6 0.4 collective-permute-done.16.outer
  43.0 0.6 collective-permute-done.13.ylo
  43.5 0.3 collective-permute-done.14.yhi
  43.8 0.9 %image.1 = (f32[2,24,8,128]{3,2,1,0:T(8,128)S(1)}, f32[2,24,8,128]{3,2,1,0:T(8,128)S(1)}, f32[2,24,8,128]{3,2,1,0:T(8,128)S(1)}, f32[2,24,8,128]{3,2,1,0:T(8,128)S(1)}) custom-call(f32[48,8,256]{2,1,0:T(8,128)S(1)} %get-tuple-element.69.u2, f32[48,8,256]{2,1,0:T(8,128)S(1)} %get-tuple-element.70.b2, f32[24,8,256]{2,1,0:T(8,128)S(1)} %collective-permute-done.13.ylo, ...), custom_call_target="tpu_custom_call" | custom-call | tf_op jit(solution)/shard_map/image/pallas_call | solution.py:22
  44.7 1.1 %collective-permute-start.19 = (f32[2,24,8,128]{3,2,1,0:T(8,128)S(1)}, f32[2,24,8,128]{3,2,1,0:T(8,128)S(1)}, u32[]{:S(2)}, u32[]{:S(2)}) collective-permute-start(f32[2,24,8,128]{3,2,1,0:T(8,128)S(1)} %get-tuple-element.88), channel_id=1, source_target_pairs={{0,128},{32,160},{64,192},{96,224},{128,0},{160,32},{192,64},{224,... | collective-permute-start | bytes 589832 | tf_op jit(solution)/shard_map/ppermute | solution.py:54
  45.8 1.3 %collective-permute-start.21 = (f32[2,24,8,128]{3,2,1,0:T(8,128)S(1)}, f32[2,24,8,128]{3,2,1,0:T(8,128)S(1)}, u32[]{:S(2)}, u32[]{:S(2)}) collective-permute-start(f32[2,24,8,128]{3,2,1,0:T(8,128)S(1)} %get-tuple-element.92), channel_id=1, source_target_pairs={{0,32},{32,0},{64,96},{96,64},{128,160},{160,128},{192,224},{224,1... | collective-permute-start | bytes 589832 | tf_op jit(solution)/shard_map/ppermute | solution.py:50
  47.1 5.9 %collective-permute-done.19.arrived = f32[2,24,8,128]{3,2,1,0:T(8,128)S(1)} collective-permute-done((f32[2,24,8,128]{3,2,1,0:T(8,128)S(1)}, f32[2,24,8,128]{3,2,1,0:T(8,128)S(1)}, u32[]{:S(2)}, u32[]{:S(2)}) %collective-permute-start.19) | collective-permute-done | bytes 196640 | tf_op jit(solution)/shard_map/ppermute | solution.py:54
  53.1 1.0 %collective-permute-start.20 = (f32[24,8,128]{2,1,0:T(8,128)S(1)}, f32[24,8,128]{2,1,0:T(8,128)S(1)}, u32[]{:S(2)}, u32[]{:S(2)}) collective-permute-start(f32[24,8,128]{2,1,0:T(8,128)S(1)} %get-tuple-element.90), channel_id=1, source_target_pairs={{0,32},{32,0},{64,96},{96,64},{128,160},{160,128},{192,224},{224,1... | collective-permute-start | bytes 294920 | tf_op jit(solution)/shard_map/ppermute | solution.py:50
  54.1 1.1 %collective-permute-start.22 = (f32[24,8,128]{2,1,0:T(8,128)S(1)}, f32[24,8,128]{2,1,0:T(8,128)S(1)}, u32[]{:S(2)}, u32[]{:S(2)}) collective-permute-start(f32[24,8,128]{2,1,0:T(8,128)S(1)} %get-tuple-element.93), channel_id=1, source_target_pairs={{0,64},{32,96},{64,0},{96,32},{128,192},{160,224},{192,128},{224,1... | collective-permute-start | bytes 294920 | tf_op jit(solution)/shard_map/ppermute | solution.py:58
  55.2 1.7 %collective-permute-start.23 = (f32[24,8,128]{2,1,0:T(8,128)S(1)}, f32[24,8,128]{2,1,0:T(8,128)S(1)}, u32[]{:S(2)}, u32[]{:S(2)}) collective-permute-start(f32[24,8,128]{2,1,0:T(8,128)S(1)} %get-tuple-element.94), channel_id=1, source_target_pairs={{0,192},{32,224},{64,128},{96,160},{128,64},{160,96},{192,0},{224,... | collective-permute-start | bytes 294920 | tf_op jit(solution)/shard_map/ppermute | solution.py:58
  57.0 2.3 %collective-permute-done.20.other = f32[24,8,128]{2,1,0:T(8,128)S(1)} collective-permute-done((f32[24,8,128]{2,1,0:T(8,128)S(1)}, f32[24,8,128]{2,1,0:T(8,128)S(1)}, u32[]{:S(2)}, u32[]{:S(2)}) %collective-permute-start.20) | collective-permute-done | bytes 98336 | tf_op jit(solution)/shard_map/ppermute | solution.py:50
  59.3 1.8 %collective-permute-done.23.down = f32[24,8,128]{2,1,0:T(8,128)S(1)} collective-permute-done((f32[24,8,128]{2,1,0:T(8,128)S(1)}, f32[24,8,128]{2,1,0:T(8,128)S(1)}, u32[]{:S(2)}, u32[]{:S(2)}) %collective-permute-start.23) | collective-permute-done | bytes 98336 | tf_op jit(solution)/shard_map/ppermute | solution.py:58
  61.1 0.3 sum.1
  61.4 1.0 %copy.15 = f32[3,48,8,32]{1,3,2,0:T(8,128)} copy(f32[3,48,8,32]{3,2,1,0:T(8,128)S(1)} %sum.1) | data formatting | bytes 294912 | tf_op jit(solution)/shard_map/sum/pallas_call | solution.py:22
  (38 shorter events, 0.2 us)
Async XLA Ops:
  0.0 1.3 %copy-start = (f32[48,8,256]{2,1,0:T(8,128)S(1)}, f32[48,8,256]{2,1,0:T(8,128)}, u32[]{:S(2)}) copy-start(f32[48,8,256]{2,1,0:T(8,128)} %speed.11) | copy-start | bytes 1179652
  0.0 1.3 %copy-start.2 = (f32[48,8,256]{2,1,0:T(8,128)S(1)}, f32[48,8,256]{2,1,0:T(8,128)}, u32[]{:S(2)}) copy-start(f32[48,8,256]{2,1,0:T(8,128)} %epsilon.7) | copy-start | bytes 1179652
  1.4 1.0 %copy-start.3 = (f32[48,8,256]{2,1,0:T(8,128)S(1)}, f32[48,8,256]{2,1,0:T(8,128)}, u32[]{:S(2)}) copy-start(f32[48,8,256]{2,1,0:T(8,128)} %delta.7) | copy-start | bytes 1179652
  2.4 7.2 %copy-start.1 = (f32[1,48,8,256]{3,2,1,0:T(8,128)S(1)}, f32[1,48,8,256]{3,2,1,0:T(8,128)}, u32[]{:S(2)}) copy-start(f32[1,48,8,256]{3,2,1,0:T(8,128)} %l.3) | copy-start | bytes 1179652
  2.4 7.2 %copy-start.4 = (f32[1,48,8,256]{3,2,1,0:T(8,128)S(1)}, f32[1,48,8,256]{3,2,1,0:T(8,128)}, u32[]{:S(2)}) copy-start(f32[1,48,8,256]{3,2,1,0:T(8,128)} %u.3) | copy-start | bytes 1179652
  2.6 7.7 %collective-permute-start = (f32[24,8,128]{2,1,0:T(8,128)S(1)}, f32[24,8,128]{2,1,0:T(8,128)S(1)}, u32[]{:S(2)}, u32[]{:S(2)}) collective-permute-start(f32[24,8,128]{2,1,0:T(8,128)S(1)} %chunk.1.mine), channel_id=1, source_target_pairs={{0,32},{32,0},{64,96},{96,64},{128,160},{160,128},{192,224},{224,1... | collective-permute-start | bytes 294920 | tf_op jit(solution)/shard_map/ppermute | solution.py:50
  5.8 11.4 %collective-permute-start.5 = (f32[24,8,128]{2,1,0:T(8,128)S(1)}, f32[24,8,128]{2,1,0:T(8,128)S(1)}, u32[]{:S(2)}, u32[]{:S(2)}) collective-permute-start(f32[24,8,128]{2,1,0:T(8,128)S(1)} %chunk.1.mine), channel_id=1, source_target_pairs={{0,64},{32,96},{64,0},{96,32},{128,192},{160,224},{192,128},{224,1... | collective-permute-start | bytes 294920 | tf_op jit(solution)/shard_map/ppermute | solution.py:58
  7.3 9.9 %collective-permute-start.6 = (f32[24,8,128]{2,1,0:T(8,128)S(1)}, f32[24,8,128]{2,1,0:T(8,128)S(1)}, u32[]{:S(2)}, u32[]{:S(2)}) collective-permute-start(f32[24,8,128]{2,1,0:T(8,128)S(1)} %chunk.1.mine), channel_id=1, source_target_pairs={{0,192},{32,224},{64,128},{96,160},{128,64},{160,96},{192,0},{224,... | collective-permute-start | bytes 294920 | tf_op jit(solution)/shard_map/ppermute | solution.py:58
  9.6 2.6 %collective-permute-start.1 = (f32[4,8,256]{2,1,0:T(8,128)S(1)}, f32[4,8,256]{2,1,0:T(8,128)S(1)}, u32[]{:S(2)}, u32[]{:S(2)}) collective-permute-start(f32[4,8,256]{2,1,0:T(8,128)S(1)} %get-tuple-element.50), channel_id=1, source_target_pairs={{0,8},{8,0},{16,24},{24,16},{1,9},{9,1},{17,25},{25,17},{2,10},{10... | collective-permute-start | bytes 98312 | tf_op jit(solution)/shard_map/ppermute | solution.py:36
  9.7 3.4 %collective-permute-start.2 = (f32[4,8,256]{2,1,0:T(8,128)S(1)}, f32[4,8,256]{2,1,0:T(8,128)S(1)}, u32[]{:S(2)}, u32[]{:S(2)}) collective-permute-start(f32[4,8,256]{2,1,0:T(8,128)S(1)} %get-tuple-element.51), channel_id=1, source_target_pairs={{0,24},{8,16},{16,8},{24,0},{1,25},{9,17},{17,9},{25,1},{2,26},{10... | collective-permute-start | bytes 98312 | tf_op jit(solution)/shard_map/ppermute | solution.py:36
  10.4 13.7 %collective-permute-start.7 = (f32[48,8,128]{2,1,0:T(8,128)S(1)}, f32[48,8,128]{2,1,0:T(8,128)S(1)}, u32[]{:S(2)}, u32[]{:S(2)}) collective-permute-start(f32[48,8,128]{2,1,0:T(8,128)S(1)} %pad_maximum_fusion.rest_0_), channel_id=1, source_target_pairs={{0,128},{32,160},{64,192},{96,224},{128,0},{160,32},{192,64},{224,... | collective-permute-start | bytes 589832 | tf_op jit(solution)/shard_map/ppermute | solution.py:54
  13.1 7.0 %copy-start.8 = (s32[1,1536]{1,0:T(1,128)S(1)}, s32[1,1536]{1,0:T(1,128)}, u32[]{:S(2)}) copy-start(s32[1,1536]{1,0:T(1,128)} %cells.1) | copy-start | bytes 18436
  13.1 9.3 %copy-start.7 = (f32[1,48,8,256]{3,2,1,0:T(8,128)S(1)}, f32[1,48,8,256]{3,2,1,0:T(8,128)}, u32[]{:S(2)}) copy-start(f32[1,48,8,256]{3,2,1,0:T(8,128)} %lm.1) | copy-start | bytes 1179652
  13.3 7.9 %collective-permute-start.3 = (f32[24,8,256]{2,1,0:T(8,128)S(1)}, f32[24,8,256]{2,1,0:T(8,128)S(1)}, u32[]{:S(2)}, u32[]{:S(2)}) collective-permute-start(f32[24,8,256]{2,1,0:T(8,128)S(1)} %get-tuple-element.52.rest_1_), channel_id=1, source_target_pairs={{0,1},{1,0},{2,3},{3,2},{4,5},{5,4},{6,7},{7,6},{8,9},{9,8},{10,11... | collective-permute-start | bytes 589832 | tf_op jit(solution)/shard_map/ppermute | solution.py:36
  13.5 9.0 %collective-permute-start.4 = (f32[24,8,256]{2,1,0:T(8,128)S(1)}, f32[24,8,256]{2,1,0:T(8,128)S(1)}, u32[]{:S(2)}, u32[]{:S(2)}) collective-permute-start(f32[24,8,256]{2,1,0:T(8,128)S(1)} %get-tuple-element.53.rest_2_), channel_id=1, source_target_pairs={{0,8},{1,2},{2,1},{3,4},{4,3},{5,6},{6,5},{7,15},{8,0},{9,10},{10,... | collective-permute-start | bytes 589832 | tf_op jit(solution)/shard_map/ppermute | solution.py:46
  17.2 2.9 %copy-start.9 = (f32[1,2]{1,0:T(1,128)S(1)}, f32[1,2]{1,0:T(1,128)}, u32[]{:S(2)}) copy-start(f32[1,2]{1,0:T(1,128)} %wavelet.1) | copy-start | bytes 28
  17.2 5.2 %copy-start.6 = (f32[1,48,8,256]{3,2,1,0:T(8,128)S(1)}, f32[1,48,8,256]{3,2,1,0:T(8,128)}, u32[]{:S(2)}) copy-start(f32[1,48,8,256]{3,2,1,0:T(8,128)} %um.1) | copy-start | bytes 1179652
  17.2 5.2 %copy-start.5 = (f32[48,8,256]{2,1,0:T(8,128)S(1)}, f32[48,8,256]{2,1,0:T(8,128)}, u32[]{:S(2)}) copy-start(f32[48,8,256]{2,1,0:T(8,128)} %tilt.5) | copy-start | bytes 1179652
  17.3 8.3 %collective-permute-start.8 = (f32[48,8,128]{2,1,0:T(8,128)S(1)}, f32[48,8,128]{2,1,0:T(8,128)S(1)}, u32[]{:S(2)}, u32[]{:S(2)}) collective-permute-start(f32[48,8,128]{2,1,0:T(8,128)S(1)} %pad_maximum_fusion.1), channel_id=1, source_target_pairs={{0,32},{32,0},{64,96},{96,64},{128,160},{160,128},{192,224},{224,1... | collective-permute-start | bytes 589832 | tf_op jit(solution)/shard_map/ppermute | solution.py:50
  26.3 8.0 %collective-permute-start.9 = (f32[24,8,256]{2,1,0:T(8,128)S(1)}, f32[24,8,256]{2,1,0:T(8,128)S(1)}, u32[]{:S(2)}, u32[]{:S(2)}) collective-permute-start(f32[24,8,256]{2,1,0:T(8,128)S(1)} %get-tuple-element.65), channel_id=1, source_target_pairs={{0,1},{1,0},{2,3},{3,2},{4,5},{5,4},{6,7},{7,6},{8,9},{9,8},{10,11... | collective-permute-start | bytes 589832 | tf_op jit(solution)/shard_map/ppermute | solution.py:36
  26.4 7.9 %collective-permute-start.10 = (f32[24,8,256]{2,1,0:T(8,128)S(1)}, f32[24,8,256]{2,1,0:T(8,128)S(1)}, u32[]{:S(2)}, u32[]{:S(2)}) collective-permute-start(f32[24,8,256]{2,1,0:T(8,128)S(1)} %get-tuple-element.66), channel_id=1, source_target_pairs={{0,8},{1,2},{2,1},{3,4},{4,3},{5,6},{6,5},{7,15},{8,0},{9,10},{10,... | collective-permute-start | bytes 589832 | tf_op jit(solution)/shard_map/ppermute | solution.py:46
  30.5 1.3 %collective-permute-start.11 = (f32[8,8,256]{2,1,0:T(8,128)S(1)}, f32[8,8,256]{2,1,0:T(8,128)S(1)}, u32[]{:S(2)}, u32[]{:S(2)}) collective-permute-start(f32[8,8,256]{2,1,0:T(8,128)S(1)} %get-tuple-element.67), channel_id=1, source_target_pairs={{0,8},{8,0},{16,24},{24,16},{1,9},{9,1},{17,25},{25,17},{2,10},{10... | collective-permute-start | bytes 196616 | tf_op jit(solution)/shard_map/ppermute | solution.py:36
  30.5 3.7 %collective-permute-start.12 = (f32[8,8,256]{2,1,0:T(8,128)S(1)}, f32[8,8,256]{2,1,0:T(8,128)S(1)}, u32[]{:S(2)}, u32[]{:S(2)}) collective-permute-start(f32[8,8,256]{2,1,0:T(8,128)S(1)} %get-tuple-element.68), channel_id=1, source_target_pairs={{0,24},{8,16},{16,8},{24,0},{1,25},{9,17},{17,9},{25,1},{2,26},{10... | collective-permute-start | bytes 196616 | tf_op jit(solution)/shard_map/ppermute | solution.py:36
  31.3 8.3 %collective-permute-start.17 = (f32[24,8,256]{2,1,0:T(8,128)S(1)}, f32[24,8,256]{2,1,0:T(8,128)S(1)}, u32[]{:S(2)}, u32[]{:S(2)}) collective-permute-start(f32[24,8,256]{2,1,0:T(8,128)S(1)} %get-tuple-element.81), channel_id=1, source_target_pairs={{0,1},{1,0},{2,3},{3,2},{4,5},{5,4},{6,7},{7,6},{8,9},{9,8},{10,11... | collective-permute-start | bytes 589832 | tf_op jit(solution)/shard_map/ppermute | solution.py:36
  31.8 8.5 %collective-permute-start.18 = (f32[24,8,256]{2,1,0:T(8,128)S(1)}, f32[24,8,256]{2,1,0:T(8,128)S(1)}, u32[]{:S(2)}, u32[]{:S(2)}) collective-permute-start(f32[24,8,256]{2,1,0:T(8,128)S(1)} %get-tuple-element.82), channel_id=1, source_target_pairs={{0,8},{1,2},{2,1},{3,4},{4,3},{5,6},{6,5},{7,15},{8,0},{9,10},{10,... | collective-permute-start | bytes 589832 | tf_op jit(solution)/shard_map/ppermute | solution.py:46
  36.2 7.3 %collective-permute-start.13 = (f32[24,8,256]{2,1,0:T(8,128)S(1)}, f32[24,8,256]{2,1,0:T(8,128)S(1)}, u32[]{:S(2)}, u32[]{:S(2)}) collective-permute-start(f32[24,8,256]{2,1,0:T(8,128)S(1)} %get-tuple-element.71), channel_id=1, source_target_pairs={{0,1},{1,0},{2,3},{3,2},{4,5},{5,4},{6,7},{7,6},{8,9},{9,8},{10,11... | collective-permute-start | bytes 589832 | tf_op jit(solution)/shard_map/ppermute | solution.py:36
  36.3 7.5 %collective-permute-start.14 = (f32[24,8,256]{2,1,0:T(8,128)S(1)}, f32[24,8,256]{2,1,0:T(8,128)S(1)}, u32[]{:S(2)}, u32[]{:S(2)}) collective-permute-start(f32[24,8,256]{2,1,0:T(8,128)S(1)} %get-tuple-element.72), channel_id=1, source_target_pairs={{0,8},{1,2},{2,1},{3,4},{4,3},{5,6},{6,5},{7,15},{8,0},{9,10},{10,... | collective-permute-start | bytes 589832 | tf_op jit(solution)/shard_map/ppermute | solution.py:46
  39.6 3.0 %collective-permute-start.15 = (f32[4,8,256]{2,1,0:T(8,128)S(1)}, f32[4,8,256]{2,1,0:T(8,128)S(1)}, u32[]{:S(2)}, u32[]{:S(2)}) collective-permute-start(f32[4,8,256]{2,1,0:T(8,128)S(1)} %get-tuple-element.73), channel_id=1, source_target_pairs={{0,8},{8,0},{16,24},{24,16},{1,9},{9,1},{17,25},{25,17},{2,10},{10... | collective-permute-start | bytes 98312 | tf_op jit(solution)/shard_map/ppermute | solution.py:36
  39.6 3.3 %collective-permute-start.16 = (f32[4,8,256]{2,1,0:T(8,128)S(1)}, f32[4,8,256]{2,1,0:T(8,128)S(1)}, u32[]{:S(2)}, u32[]{:S(2)}) collective-permute-start(f32[4,8,256]{2,1,0:T(8,128)S(1)} %get-tuple-element.74), channel_id=1, source_target_pairs={{0,24},{8,16},{16,8},{24,0},{1,25},{9,17},{17,9},{25,1},{2,26},{10... | collective-permute-start | bytes 98312 | tf_op jit(solution)/shard_map/ppermute | solution.py:36
  44.7 8.3 %collective-permute-start.19 = (f32[2,24,8,128]{3,2,1,0:T(8,128)S(1)}, f32[2,24,8,128]{3,2,1,0:T(8,128)S(1)}, u32[]{:S(2)}, u32[]{:S(2)}) collective-permute-start(f32[2,24,8,128]{3,2,1,0:T(8,128)S(1)} %get-tuple-element.88), channel_id=1, source_target_pairs={{0,128},{32,160},{64,192},{96,224},{128,0},{160,32},{192,64},{224,... | collective-permute-start | bytes 589832 | tf_op jit(solution)/shard_map/ppermute | solution.py:54
  45.8 8.3 %collective-permute-start.21 = (f32[2,24,8,128]{3,2,1,0:T(8,128)S(1)}, f32[2,24,8,128]{3,2,1,0:T(8,128)S(1)}, u32[]{:S(2)}, u32[]{:S(2)}) collective-permute-start(f32[2,24,8,128]{3,2,1,0:T(8,128)S(1)} %get-tuple-element.92), channel_id=1, source_target_pairs={{0,32},{32,0},{64,96},{96,64},{128,160},{160,128},{192,224},{224,1... | collective-permute-start | bytes 589832 | tf_op jit(solution)/shard_map/ppermute | solution.py:50
  53.1 6.2 %collective-permute-start.20 = (f32[24,8,128]{2,1,0:T(8,128)S(1)}, f32[24,8,128]{2,1,0:T(8,128)S(1)}, u32[]{:S(2)}, u32[]{:S(2)}) collective-permute-start(f32[24,8,128]{2,1,0:T(8,128)S(1)} %get-tuple-element.90), channel_id=1, source_target_pairs={{0,32},{32,0},{64,96},{96,64},{128,160},{160,128},{192,224},{224,1... | collective-permute-start | bytes 294920 | tf_op jit(solution)/shard_map/ppermute | solution.py:50
  54.1 5.1 %collective-permute-start.22 = (f32[24,8,128]{2,1,0:T(8,128)S(1)}, f32[24,8,128]{2,1,0:T(8,128)S(1)}, u32[]{:S(2)}, u32[]{:S(2)}) collective-permute-start(f32[24,8,128]{2,1,0:T(8,128)S(1)} %get-tuple-element.93), channel_id=1, source_target_pairs={{0,64},{32,96},{64,0},{96,32},{128,192},{160,224},{192,128},{224,1... | collective-permute-start | bytes 294920 | tf_op jit(solution)/shard_map/ppermute | solution.py:58
  55.2 5.8 %collective-permute-start.23 = (f32[24,8,128]{2,1,0:T(8,128)S(1)}, f32[24,8,128]{2,1,0:T(8,128)S(1)}, u32[]{:S(2)}, u32[]{:S(2)}) collective-permute-start(f32[24,8,128]{2,1,0:T(8,128)S(1)} %get-tuple-element.94), channel_id=1, source_target_pairs={{0,192},{32,224},{64,128},{96,160},{128,64},{160,96},{192,0},{224,... | collective-permute-start | bytes 294920 | tf_op jit(solution)/shard_map/ppermute | solution.py:58

commit v6 on v5

--- a/solution.py
+++ b/solution.py
@@ -438,8 +438,8 @@
         out[...] = here[i] + arrived[i]
 
 
-def sum_kernel(speed, epsilon, delta, own, other, up, down, out):
-    group = out.shape[1] // 4
+def sum_kernel(speed, epsilon, delta, own, other, up, down, out, values, turned, sems):
+    group = values.shape[1] // 4
     tile, shift = own_depth(lax.axis_index("shot"))
     for i in range(group):
         sums = []
@@ -450,9 +450,16 @@
             x = g * group + i
             a, c = (pltpu.roll(v, (128 - 32 * g) % 128, 1) if g else v for v in sums)
             s, e, d = (pltpu.roll(w[x, :, tile], shift, 1) for w in (speed, epsilon, delta))
-            out[0, x] = (e * a + d * c)[:, 0:32]
-            out[1, x] = (s * a)[:, 0:32]
-            out[2, x] = (s * c)[:, 0:32]
+            values[0, x] = e * a + d * c
+            values[1, x] = s * a
+            values[2, x] = s * c
+    copies = [pltpu.make_async_copy(turned.at[k], out.at[k], sems.at[k]) for k in range(3)]
+    for k, copy in enumerate(copies):
+        for y in range(turned.shape[1]):
+            turned[k, y] = values[k, :, y, 0:32].T
+        copy.start()
+    for copy in copies:
+        copy.wait()
 
 
 def per_device(
@@ -555,13 +562,21 @@
     )
     own, other = call(add_kernel, [packed] * 2, (near, opposite_y(opposite)), name="add_opposite")
     inner, outer = call(add_kernel, [packed] * 2, (far, across(beside)), name="add_beside")
-    (out,) = call(
+    turned = (3, ny, nz // 8, nx)
+    out = pl.pallas_call(
         sum_kernel,
-        [(3, nx, ny, nz // 8)],
-        model[:3] + (own, across(other), beside_y(inner), beside_y(outer, True)),
+        out_shape=jax.ShapeDtypeStruct(turned, F32),
+        in_specs=[pl.BlockSpec(memory_space=pltpu.VMEM)] * 7,
+        out_specs=pl.BlockSpec(memory_space=pl.ANY),
+        scratch_shapes=[
+            pltpu.VMEM((3, nx, ny, 128), F32),
+            pltpu.VMEM(turned, F32),
+            pltpu.SemaphoreType.DMA((3,)),
+        ],
+        compiler_params=pltpu.CompilerParams(vmem_limit_bytes=LIMIT),
         name="sum",
-    )
-    return out
+    )(*(model[:3] + (own, across(other), beside_y(inner), beside_y(outer, True))))
+    return jnp.transpose(out, (0, 3, 1, 2))
 
 
 def solution(mesh):

time: 62.5 us -> 62.6 us (level)
  Pallas kernels: 9.6 us -> 10.6 us
  local copies, waits for them, and re-layouts: 3.03 us -> 2.05 us
    pallas_call x0 -> x1, Pallas kernels: none -> 1.28 us  [per_device(): pl.pallas_call(sum_kernel, out_shape=jax.ShapeDtypeStruct(turned, F32), i...]
    pallas_call x1 -> x0, local copies, waits for them, and re-layouts: 0.98 us -> none  [call(): pl.pallas_call(kernel, out_shape=[jax.ShapeDtypeStruct(*out) for out in t...]
    pallas_call x13 -> x12, Pallas kernels: 9.58 us -> 9.28 us  [call(): pl.pallas_call(kernel, out_shape=[jax.ShapeDtypeStruct(*out) for out in t...]
where the time goes in v6:
time: 62.6 us; the launch traced here: 62.5 us
  starting transfers between devices  32.7 us (52%)
  waiting for transfers between devices  16.1 us (26%)
  Pallas kernels  10.6 us (17%)
  local copies, waits for them, and re-layouts  2.05 us (3%)
  between operations  1.06 us (2%)
    ppermute x4, starting transfers between devices, outer_y(): return lax.ppermute(value, ('gx', 'gy'), swaps)  12.9 us
    pallas_call x12, Pallas kernels, call(): pl.pallas_call(kernel, out_shape=[jax.ShapeDtypeStruct(*out) for out in t...  9.28 us
    ppermute x4, starting transfers between devices, across(): return lax.ppermute(value, 'shot', [(i, i ^ 1) for i in range(8)])  7.68 us
    ppermute x4, starting transfers between devices, beside_y(): lax.ppermute(value, 'shot', [(i, neighbour(i // 2, outer) * 2 + i % 2) fo...  6.59 us
    ppermute x2, waiting for transfers between devices, opposite_y(): return lax.ppermute(value, 'shot', [(i, (i + 4) % 8) for i in range(8)])  5.94 us
    ppermute x4, waiting for transfers between devices, across(): return lax.ppermute(value, 'shot', [(i, i ^ 1) for i in range(8)])  3.73 us
    ppermute x10, waiting for transfers between devices, pairs(): return lax.ppermute(value, axis, list(enumerate(other)))  3.04 us
    ppermute x2, starting transfers between devices, opposite_y(): return lax.ppermute(value, 'shot', [(i, (i + 4) % 8) for i in range(8)])  2.88 us
  transfers between devices with their start and end apart: 24, of which 11 were waited for; matrix products, arithmetic and copies ran while one was open for 0% of the time, Pallas kernels for 11%

profile of v6, /device:TPU:32, one launch (start us, length us, event | category | flops | bytes accessed | tf_op | source)
XLA Modules:
  0.0 62.5 jit_solution(15352546702417946690)
XLA Ops:
  0.0 1.3 %copy.14.p = f32[3,48,8,32]{3,2,1,0:T(8,128)S(1)} copy(f32[3,48,8,32]{1,3,2,0:T(8,128)} %param.16) | data formatting | bytes 294912 | tf_op args[4]
  1.4 0.0 copy-start.3
  1.4 0.3 half_chunk.1.rest_0_
  1.7 0.7 %copy-done.3 = f32[48,8,256]{2,1,0:T(8,128)S(1)} copy-done((f32[48,8,256]{2,1,0:T(8,128)S(1)}, f32[48,8,256]{2,1,0:T(8,128)}, u32[]{:S(2)}) %copy-start.3) | copy-done | bytes 393240
  2.4 0.3 chunk.1.mine
  2.6 3.1 %collective-permute-start = (f32[24,8,128]{2,1,0:T(8,128)S(1)}, f32[24,8,128]{2,1,0:T(8,128)S(1)}, u32[]{:S(2)}, u32[]{:S(2)}) collective-permute-start(f32[24,8,128]{2,1,0:T(8,128)S(1)} %chunk.1.mine), channel_id=1, source_target_pairs={{0,32},{32,0},{64,96},{96,64},{128,160},{160,128},{192,224},{224,1... | collective-permute-start | bytes 294920 | tf_op jit(solution)/shard_map/ppermute | solution.py:50
  5.8 1.6 %collective-permute-start.5 = (f32[24,8,128]{2,1,0:T(8,128)S(1)}, f32[24,8,128]{2,1,0:T(8,128)S(1)}, u32[]{:S(2)}, u32[]{:S(2)}) collective-permute-start(f32[24,8,128]{2,1,0:T(8,128)S(1)} %chunk.1.mine), channel_id=1, source_target_pairs={{0,64},{32,96},{64,0},{96,32},{128,192},{160,224},{192,128},{224,1... | collective-permute-start | bytes 294920 | tf_op jit(solution)/shard_map/ppermute | solution.py:58
  7.3 2.2 %collective-permute-start.6 = (f32[24,8,128]{2,1,0:T(8,128)S(1)}, f32[24,8,128]{2,1,0:T(8,128)S(1)}, u32[]{:S(2)}, u32[]{:S(2)}) collective-permute-start(f32[24,8,128]{2,1,0:T(8,128)S(1)} %chunk.1.mine), channel_id=1, source_target_pairs={{0,192},{32,224},{64,128},{96,160},{128,64},{160,96},{192,0},{224,... | collective-permute-start | bytes 294920 | tf_op jit(solution)/shard_map/ppermute | solution.py:58
  9.6 0.1 collective-permute-start.1
  9.7 0.7 %collective-permute-start.2 = (f32[4,8,256]{2,1,0:T(8,128)S(1)}, f32[4,8,256]{2,1,0:T(8,128)S(1)}, u32[]{:S(2)}, u32[]{:S(2)}) collective-permute-start(f32[4,8,256]{2,1,0:T(8,128)S(1)} %get-tuple-element.51), channel_id=1, source_target_pairs={{0,24},{8,16},{16,8},{24,0},{1,25},{9,17},{17,9},{25,1},{2,26},{10... | collective-permute-start | bytes 98312 | tf_op jit(solution)/shard_map/ppermute | solution.py:36
  10.4 1.8 %collective-permute-start.7 = (f32[48,8,128]{2,1,0:T(8,128)S(1)}, f32[48,8,128]{2,1,0:T(8,128)S(1)}, u32[]{:S(2)}, u32[]{:S(2)}) collective-permute-start(f32[48,8,128]{2,1,0:T(8,128)S(1)} %pad_maximum_fusion.rest_0_), channel_id=1, source_target_pairs={{0,128},{32,160},{64,192},{96,224},{128,0},{160,32},{192,64},{224,... | collective-permute-start | bytes 589832 | tf_op jit(solution)/shard_map/ppermute | solution.py:54
  12.2 0.9 %collective-permute-done.2.rest_2_.outer = f32[4,8,256]{2,1,0:T(8,128)S(1)} collective-permute-done((f32[4,8,256]{2,1,0:T(8,128)S(1)}, f32[4,8,256]{2,1,0:T(8,128)S(1)}, u32[]{:S(2)}, u32[]{:S(2)}) %collective-permute-start.2) | collective-permute-done | bytes 32800 | tf_op jit(solution)/shard_map/ppermute | solution.py:36
  13.1 0.2 layers_y.1
  13.3 0.2 collective-permute-start.3
  13.5 3.7 %collective-permute-start.4 = (f32[24,8,256]{2,1,0:T(8,128)S(1)}, f32[24,8,256]{2,1,0:T(8,128)S(1)}, u32[]{:S(2)}, u32[]{:S(2)}) collective-permute-start(f32[24,8,256]{2,1,0:T(8,128)S(1)} %get-tuple-element.53.rest_2_), channel_id=1, source_target_pairs={{0,8},{1,2},{2,1},{3,4},{4,3},{5,6},{6,5},{7,15},{8,0},{9,10},{10,... | collective-permute-start | bytes 589832 | tf_op jit(solution)/shard_map/ppermute | solution.py:46
  17.3 2.2 %collective-permute-start.8 = (f32[48,8,128]{2,1,0:T(8,128)S(1)}, f32[48,8,128]{2,1,0:T(8,128)S(1)}, u32[]{:S(2)}, u32[]{:S(2)}) collective-permute-start(f32[48,8,128]{2,1,0:T(8,128)S(1)} %pad_maximum_fusion.1), channel_id=1, source_target_pairs={{0,32},{32,0},{64,96},{96,64},{128,160},{160,128},{192,224},{224,1... | collective-permute-start | bytes 589832 | tf_op jit(solution)/shard_map/ppermute | solution.py:50
  20.1 1.0 %counts.1 = (f32[48,8,256]{2,1,0:T(8,128)S(1)}, f32[2,8,256]{2,1,0:T(8,128)S(1)}) custom-call(s32[1,1536]{1,0:T(1,128)S(1)} %copy-done.8, f32[1,2]{1,0:T(1,128)S(1)} %copy-done.9, s32[1]{0:T(128)S(6)} %copy.15.source, f32[48,8,128]{2,1,0:T(8,128)S(1)} %pad_maximum_fusion.rest_0_, f32[24,8,256]{2,1,0:T(8,128)S(1)} %get-tuple-element.52.rest_1_, ...), custom_call_target="tpu_custom_call" | custom-call | tf_op jit(solution)/shard_map/counts/pallas_call | solution.py:22
  21.2 1.3 %collective-permute-done.4.yhi = f32[24,8,256]{2,1,0:T(8,128)S(1)} collective-permute-done((f32[24,8,256]{2,1,0:T(8,128)S(1)}, f32[24,8,256]{2,1,0:T(8,128)S(1)}, u32[]{:S(2)}, u32[]{:S(2)}) %collective-permute-start.4) | collective-permute-done | bytes 196640 | tf_op jit(solution)/shard_map/ppermute | solution.py:46
  22.4 1.7 %first.1 = (f32[48,8,256]{2,1,0:T(8,128)S(1)}, f32[48,8,256]{2,1,0:T(8,128)S(1)}, f32[48,8,256]{2,1,0:T(8,128)S(1)}, f32[48,8,256]{2,1,0:T(8,128)S(1)}, f32[48,8...) custom-call(f32[2,8,256]{2,1,0:T(8,128)S(1)} %get-tuple-element.54.plane, bf16[2,256,256]{2,1,0:T(8,128)(2,1)S(1)} %get-tuple-element.55.zmat, ...), custom_call_target="tpu_custom_call" | custom-call | tf_op jit(solution)/shard_map/first/pallas_call | solution.py:22
  24.1 1.4 %collective-permute-done.8.beside = f32[48,8,128]{2,1,0:T(8,128)S(1)} collective-permute-done((f32[48,8,128]{2,1,0:T(8,128)S(1)}, f32[48,8,128]{2,1,0:T(8,128)S(1)}, u32[]{:S(2)}, u32[]{:S(2)}) %collective-permute-start.8) | collective-permute-done | bytes 196640 | tf_op jit(solution)/shard_map/ppermute | solution.py:50
  25.5 0.7 %born.1 = (f32[48,8,256]{2,1,0:T(8,128)S(1)}, f32[48,8,256]{2,1,0:T(8,128)S(1)}, f32[48,8,256]{2,1,0:T(8,128)S(1)}, f32[48,8,256]{2,1,0:T(8,128)S(1)}, f32[24,8,...) custom-call(f32[24,8,128]{2,1,0:T(8,128)S(1)} %chunk.1.mine, ...), custom_call_target="tpu_custom_call" | custom-call | tf_op jit(solution)/shard_map/born/pallas_call | solution.py:22
  26.3 0.1 collective-permute-start.9
  26.4 4.1 %collective-permute-start.10 = (f32[24,8,256]{2,1,0:T(8,128)S(1)}, f32[24,8,256]{2,1,0:T(8,128)S(1)}, u32[]{:S(2)}, u32[]{:S(2)}) collective-permute-start(f32[24,8,256]{2,1,0:T(8,128)S(1)} %get-tuple-element.66), channel_id=1, source_target_pairs={{0,8},{1,2},{2,1},{3,4},{4,3},{5,6},{6,5},{7,15},{8,0},{9,10},{10,... | collective-permute-start | bytes 589832 | tf_op jit(solution)/shard_map/ppermute | solution.py:46
  30.5 0.7 %collective-permute-start.12 = (f32[8,8,256]{2,1,0:T(8,128)S(1)}, f32[8,8,256]{2,1,0:T(8,128)S(1)}, u32[]{:S(2)}, u32[]{:S(2)}) collective-permute-start(f32[8,8,256]{2,1,0:T(8,128)S(1)} %get-tuple-element.68), channel_id=1, source_target_pairs={{0,24},{8,16},{16,8},{24,0},{1,25},{9,17},{17,9},{25,1},{2,26},{10... | collective-permute-start | bytes 196616 | tf_op jit(solution)/shard_map/ppermute | solution.py:36
  31.2 0.1 adjoint_y.1
  31.3 0.1 collective-permute-start.17
  31.4 0.3 collective-permute-done.11.inner
  31.8 1.7 %collective-permute-start.18 = (f32[24,8,256]{2,1,0:T(8,128)S(1)}, f32[24,8,256]{2,1,0:T(8,128)S(1)}, u32[]{:S(2)}, u32[]{:S(2)}) collective-permute-start(f32[24,8,256]{2,1,0:T(8,128)S(1)} %get-tuple-element.82), channel_id=1, source_target_pairs={{0,8},{1,2},{2,1},{3,4},{4,3},{5,6},{6,5},{7,15},{8,0},{9,10},{10,... | collective-permute-start | bytes 589832 | tf_op jit(solution)/shard_map/ppermute | solution.py:46
  33.5 0.8 %collective-permute-done.12.outer = f32[8,8,256]{2,1,0:T(8,128)S(1)} collective-permute-done((f32[8,8,256]{2,1,0:T(8,128)S(1)}, f32[8,8,256]{2,1,0:T(8,128)S(1)}, u32[]{:S(2)}, u32[]{:S(2)}) %collective-permute-start.12) | collective-permute-done | bytes 65568 | tf_op jit(solution)/shard_map/ppermute | solution.py:36
  34.3 0.0 collective-permute-done.10.yhi
  34.3 1.9 %second.1 = (f32[48,8,256]{2,1,0:T(8,128)S(1)}, f32[48,8,256]{2,1,0:T(8,128)S(1)}, f32[48,8,256]{2,1,0:T(8,128)S(1)}, f32[48,8,256]{2,1,0:T(8,128)S(1)}, f32[48,...) custom-call(f32[2,8,256]{2,1,0:T(8,128)S(1)} %get-tuple-element.54.p, ...), custom_call_target="tpu_custom_call" | custom-call | tf_op jit(solution)/shard_map/second/pallas_call | solution.py:22
  36.2 0.1 collective-permute-start.13
  36.3 3.3 %collective-permute-start.14 = (f32[24,8,256]{2,1,0:T(8,128)S(1)}, f32[24,8,256]{2,1,0:T(8,128)S(1)}, u32[]{:S(2)}, u32[]{:S(2)}) collective-permute-start(f32[24,8,256]{2,1,0:T(8,128)S(1)} %get-tuple-element.72), channel_id=1, source_target_pairs={{0,8},{1,2},{2,1},{3,4},{4,3},{5,6},{6,5},{7,15},{8,0},{9,10},{10,... | collective-permute-start | bytes 589832 | tf_op jit(solution)/shard_map/ppermute | solution.py:46
  39.6 0.7 %collective-permute-start.16 = (f32[4,8,256]{2,1,0:T(8,128)S(1)}, f32[4,8,256]{2,1,0:T(8,128)S(1)}, u32[]{:S(2)}, u32[]{:S(2)}) collective-permute-start(f32[4,8,256]{2,1,0:T(8,128)S(1)} %get-tuple-element.74), channel_id=1, source_target_pairs={{0,24},{8,16},{16,8},{24,0},{1,25},{9,17},{17,9},{25,1},{2,26},{10... | collective-permute-start | bytes 98312 | tf_op jit(solution)/shard_map/ppermute | solution.py:36
  40.3 2.2 %adjoint.1 = (f32[48,8,256]{2,1,0:T(8,128)S(1)}, f32[48,8,256]{2,1,0:T(8,128)S(1)}, f32[48,8,256]{2,1,0:T(8,128)S(1)}, f32[48,8,256]{2,1,0:T(8,128)S(1)}) custom-call(bf16[2,256,256]{2,1,0:T(8,128)(2,1)S(1)} %get-tuple-element.55.zmat, f32[1,48,8,256]{3,2,1,0:T(8,128)S(1)} %copy-done.1, f32[48,8,256]{2,1,0:T(8,128)S(1)} %get-tuple-element.57.l1.a, ...), custom_call_target="tpu_custom_call" | custom-call | tf_op jit(solution)/shard_map/adjoint/pallas_call | solution.py:22
  42.6 0.4 collective-permute-done.16.outer
  43.0 0.6 collective-permute-done.13.ylo
  43.5 0.3 collective-permute-done.14.yhi
  43.8 0.9 %image.1 = (f32[2,24,8,128]{3,2,1,0:T(8,128)S(1)}, f32[2,24,8,128]{3,2,1,0:T(8,128)S(1)}, f32[2,24,8,128]{3,2,1,0:T(8,128)S(1)}, f32[2,24,8,128]{3,2,1,0:T(8,128)S(1)}) custom-call(f32[48,8,256]{2,1,0:T(8,128)S(1)} %get-tuple-element.69.u2, f32[48,8,256]{2,1,0:T(8,128)S(1)} %get-tuple-element.70.b2, f32[24,8,256]{2,1,0:T(8,128)S(1)} %collective-permute-done.13.ylo, ...), custom_call_target="tpu_custom_call" | custom-call | tf_op jit(solution)/shard_map/image/pallas_call | solution.py:22
  44.7 1.1 %collective-permute-start.19 = (f32[2,24,8,128]{3,2,1,0:T(8,128)S(1)}, f32[2,24,8,128]{3,2,1,0:T(8,128)S(1)}, u32[]{:S(2)}, u32[]{:S(2)}) collective-permute-start(f32[2,24,8,128]{3,2,1,0:T(8,128)S(1)} %get-tuple-element.88), channel_id=1, source_target_pairs={{0,128},{32,160},{64,192},{96,224},{128,0},{160,32},{192,64},{224,... | collective-permute-start | bytes 589832 | tf_op jit(solution)/shard_map/ppermute | solution.py:54
  45.8 1.3 %collective-permute-start.21 = (f32[2,24,8,128]{3,2,1,0:T(8,128)S(1)}, f32[2,24,8,128]{3,2,1,0:T(8,128)S(1)}, u32[]{:S(2)}, u32[]{:S(2)}) collective-permute-start(f32[2,24,8,128]{3,2,1,0:T(8,128)S(1)} %get-tuple-element.92), channel_id=1, source_target_pairs={{0,32},{32,0},{64,96},{96,64},{128,160},{160,128},{192,224},{224,1... | collective-permute-start | bytes 589832 | tf_op jit(solution)/shard_map/ppermute | solution.py:50
  47.1 5.9 %collective-permute-done.19.arrived = f32[2,24,8,128]{3,2,1,0:T(8,128)S(1)} collective-permute-done((f32[2,24,8,128]{3,2,1,0:T(8,128)S(1)}, f32[2,24,8,128]{3,2,1,0:T(8,128)S(1)}, u32[]{:S(2)}, u32[]{:S(2)}) %collective-permute-start.19) | collective-permute-done | bytes 196640 | tf_op jit(solution)/shard_map/ppermute | solution.py:54
  53.1 1.0 %collective-permute-start.20 = (f32[24,8,128]{2,1,0:T(8,128)S(1)}, f32[24,8,128]{2,1,0:T(8,128)S(1)}, u32[]{:S(2)}, u32[]{:S(2)}) collective-permute-start(f32[24,8,128]{2,1,0:T(8,128)S(1)} %get-tuple-element.90), channel_id=1, source_target_pairs={{0,32},{32,0},{64,96},{96,64},{128,160},{160,128},{192,224},{224,1... | collective-permute-start | bytes 294920 | tf_op jit(solution)/shard_map/ppermute | solution.py:50
  54.1 1.1 %collective-permute-start.22 = (f32[24,8,128]{2,1,0:T(8,128)S(1)}, f32[24,8,128]{2,1,0:T(8,128)S(1)}, u32[]{:S(2)}, u32[]{:S(2)}) collective-permute-start(f32[24,8,128]{2,1,0:T(8,128)S(1)} %get-tuple-element.93), channel_id=1, source_target_pairs={{0,64},{32,96},{64,0},{96,32},{128,192},{160,224},{192,128},{224,1... | collective-permute-start | bytes 294920 | tf_op jit(solution)/shard_map/ppermute | solution.py:58
  55.2 1.7 %collective-permute-start.23 = (f32[24,8,128]{2,1,0:T(8,128)S(1)}, f32[24,8,128]{2,1,0:T(8,128)S(1)}, u32[]{:S(2)}, u32[]{:S(2)}) collective-permute-start(f32[24,8,128]{2,1,0:T(8,128)S(1)} %get-tuple-element.94), channel_id=1, source_target_pairs={{0,192},{32,224},{64,128},{96,160},{128,64},{160,96},{192,0},{224,... | collective-permute-start | bytes 294920 | tf_op jit(solution)/shard_map/ppermute | solution.py:58
  57.0 2.3 %collective-permute-done.20.other = f32[24,8,128]{2,1,0:T(8,128)S(1)} collective-permute-done((f32[24,8,128]{2,1,0:T(8,128)S(1)}, f32[24,8,128]{2,1,0:T(8,128)S(1)}, u32[]{:S(2)}, u32[]{:S(2)}) %collective-permute-start.20) | collective-permute-done | bytes 98336 | tf_op jit(solution)/shard_map/ppermute | solution.py:50
  59.3 1.8 %collective-permute-done.23.down = f32[24,8,128]{2,1,0:T(8,128)S(1)} collective-permute-done((f32[24,8,128]{2,1,0:T(8,128)S(1)}, f32[24,8,128]{2,1,0:T(8,128)S(1)}, u32[]{:S(2)}, u32[]{:S(2)}) %collective-permute-start.23) | collective-permute-done | bytes 98336 | tf_op jit(solution)/shard_map/ppermute | solution.py:58
  61.1 1.3 %sum.1 = f32[3,8,32,48]{3,2,1,0:T(8,128)} custom-call(f32[48,8,256]{2,1,0:T(8,128)S(1)} %copy-done, f32[48,8,256]{2,1,0:T(8,128)S(1)} %copy-done.2, f32[48,8,256]{2,1,0:T(8,128)S(1)} %copy-done.3, f32[24,8,128]{2,1,0:T(8,128)S(1)} %get-tuple-element.89.own, f32[24,8,128]{2,1,0:T(8,128)S(1)} %collective-permute-done.20.other, ...), custom_call_target="tpu_custom_call" | custom-call | tf_op jit(solution)/shard_map/sum/pallas_call | solution.py:566
  (37 shorter events, 0.2 us)
Async XLA Ops:
  0.0 1.3 %copy-start = (f32[48,8,256]{2,1,0:T(8,128)S(1)}, f32[48,8,256]{2,1,0:T(8,128)}, u32[]{:S(2)}) copy-start(f32[48,8,256]{2,1,0:T(8,128)} %speed.11) | copy-start | bytes 1179652
  0.0 1.3 %copy-start.2 = (f32[48,8,256]{2,1,0:T(8,128)S(1)}, f32[48,8,256]{2,1,0:T(8,128)}, u32[]{:S(2)}) copy-start(f32[48,8,256]{2,1,0:T(8,128)} %epsilon.7) | copy-start | bytes 1179652
  1.4 1.0 %copy-start.3 = (f32[48,8,256]{2,1,0:T(8,128)S(1)}, f32[48,8,256]{2,1,0:T(8,128)}, u32[]{:S(2)}) copy-start(f32[48,8,256]{2,1,0:T(8,128)} %delta.7) | copy-start | bytes 1179652
  2.4 7.2 %copy-start.1 = (f32[1,48,8,256]{3,2,1,0:T(8,128)S(1)}, f32[1,48,8,256]{3,2,1,0:T(8,128)}, u32[]{:S(2)}) copy-start(f32[1,48,8,256]{3,2,1,0:T(8,128)} %l.3) | copy-start | bytes 1179652
  2.4 7.2 %copy-start.4 = (f32[1,48,8,256]{3,2,1,0:T(8,128)S(1)}, f32[1,48,8,256]{3,2,1,0:T(8,128)}, u32[]{:S(2)}) copy-start(f32[1,48,8,256]{3,2,1,0:T(8,128)} %u.3) | copy-start | bytes 1179652
  2.6 7.7 %collective-permute-start = (f32[24,8,128]{2,1,0:T(8,128)S(1)}, f32[24,8,128]{2,1,0:T(8,128)S(1)}, u32[]{:S(2)}, u32[]{:S(2)}) collective-permute-start(f32[24,8,128]{2,1,0:T(8,128)S(1)} %chunk.1.mine), channel_id=1, source_target_pairs={{0,32},{32,0},{64,96},{96,64},{128,160},{160,128},{192,224},{224,1... | collective-permute-start | bytes 294920 | tf_op jit(solution)/shard_map/ppermute | solution.py:50
  5.8 11.4 %collective-permute-start.5 = (f32[24,8,128]{2,1,0:T(8,128)S(1)}, f32[24,8,128]{2,1,0:T(8,128)S(1)}, u32[]{:S(2)}, u32[]{:S(2)}) collective-permute-start(f32[24,8,128]{2,1,0:T(8,128)S(1)} %chunk.1.mine), channel_id=1, source_target_pairs={{0,64},{32,96},{64,0},{96,32},{128,192},{160,224},{192,128},{224,1... | collective-permute-start | bytes 294920 | tf_op jit(solution)/shard_map/ppermute | solution.py:58
  7.3 9.9 %collective-permute-start.6 = (f32[24,8,128]{2,1,0:T(8,128)S(1)}, f32[24,8,128]{2,1,0:T(8,128)S(1)}, u32[]{:S(2)}, u32[]{:S(2)}) collective-permute-start(f32[24,8,128]{2,1,0:T(8,128)S(1)} %chunk.1.mine), channel_id=1, source_target_pairs={{0,192},{32,224},{64,128},{96,160},{128,64},{160,96},{192,0},{224,... | collective-permute-start | bytes 294920 | tf_op jit(solution)/shard_map/ppermute | solution.py:58
  9.6 2.6 %collective-permute-start.1 = (f32[4,8,256]{2,1,0:T(8,128)S(1)}, f32[4,8,256]{2,1,0:T(8,128)S(1)}, u32[]{:S(2)}, u32[]{:S(2)}) collective-permute-start(f32[4,8,256]{2,1,0:T(8,128)S(1)} %get-tuple-element.50), channel_id=1, source_target_pairs={{0,8},{8,0},{16,24},{24,16},{1,9},{9,1},{17,25},{25,17},{2,10},{10... | collective-permute-start | bytes 98312 | tf_op jit(solution)/shard_map/ppermute | solution.py:36
  9.7 3.4 %collective-permute-start.2 = (f32[4,8,256]{2,1,0:T(8,128)S(1)}, f32[4,8,256]{2,1,0:T(8,128)S(1)}, u32[]{:S(2)}, u32[]{:S(2)}) collective-permute-start(f32[4,8,256]{2,1,0:T(8,128)S(1)} %get-tuple-element.51), channel_id=1, source_target_pairs={{0,24},{8,16},{16,8},{24,0},{1,25},{9,17},{17,9},{25,1},{2,26},{10... | collective-permute-start | bytes 98312 | tf_op jit(solution)/shard_map/ppermute | solution.py:36
  10.4 13.7 %collective-permute-start.7 = (f32[48,8,128]{2,1,0:T(8,128)S(1)}, f32[48,8,128]{2,1,0:T(8,128)S(1)}, u32[]{:S(2)}, u32[]{:S(2)}) collective-permute-start(f32[48,8,128]{2,1,0:T(8,128)S(1)} %pad_maximum_fusion.rest_0_), channel_id=1, source_target_pairs={{0,128},{32,160},{64,192},{96,224},{128,0},{160,32},{192,64},{224,... | collective-permute-start | bytes 589832 | tf_op jit(solution)/shard_map/ppermute | solution.py:54
  13.1 7.0 %copy-start.8 = (s32[1,1536]{1,0:T(1,128)S(1)}, s32[1,1536]{1,0:T(1,128)}, u32[]{:S(2)}) copy-start(s32[1,1536]{1,0:T(1,128)} %cells.1) | copy-start | bytes 18436
  13.1 9.3 %copy-start.7 = (f32[1,48,8,256]{3,2,1,0:T(8,128)S(1)}, f32[1,48,8,256]{3,2,1,0:T(8,128)}, u32[]{:S(2)}) copy-start(f32[1,48,8,256]{3,2,1,0:T(8,128)} %lm.1) | copy-start | bytes 1179652
  13.3 7.9 %collective-permute-start.3 = (f32[24,8,256]{2,1,0:T(8,128)S(1)}, f32[24,8,256]{2,1,0:T(8,128)S(1)}, u32[]{:S(2)}, u32[]{:S(2)}) collective-permute-start(f32[24,8,256]{2,1,0:T(8,128)S(1)} %get-tuple-element.52.rest_1_), channel_id=1, source_target_pairs={{0,1},{1,0},{2,3},{3,2},{4,5},{5,4},{6,7},{7,6},{8,9},{9,8},{10,11... | collective-permute-start | bytes 589832 | tf_op jit(solution)/shard_map/ppermute | solution.py:36
  13.5 9.0 %collective-permute-start.4 = (f32[24,8,256]{2,1,0:T(8,128)S(1)}, f32[24,8,256]{2,1,0:T(8,128)S(1)}, u32[]{:S(2)}, u32[]{:S(2)}) collective-permute-start(f32[24,8,256]{2,1,0:T(8,128)S(1)} %get-tuple-element.53.rest_2_), channel_id=1, source_target_pairs={{0,8},{1,2},{2,1},{3,4},{4,3},{5,6},{6,5},{7,15},{8,0},{9,10},{10,... | collective-permute-start | bytes 589832 | tf_op jit(solution)/shard_map/ppermute | solution.py:46
  17.2 2.9 %copy-start.9 = (f32[1,2]{1,0:T(1,128)S(1)}, f32[1,2]{1,0:T(1,128)}, u32[]{:S(2)}) copy-start(f32[1,2]{1,0:T(1,128)} %wavelet.1) | copy-start | bytes 28
  17.2 5.2 %copy-start.6 = (f32[1,48,8,256]{3,2,1,0:T(8,128)S(1)}, f32[1,48,8,256]{3,2,1,0:T(8,128)}, u32[]{:S(2)}) copy-start(f32[1,48,8,256]{3,2,1,0:T(8,128)} %um.1) | copy-start | bytes 1179652
  17.2 5.2 %copy-start.5 = (f32[48,8,256]{2,1,0:T(8,128)S(1)}, f32[48,8,256]{2,1,0:T(8,128)}, u32[]{:S(2)}) copy-start(f32[48,8,256]{2,1,0:T(8,128)} %tilt.5) | copy-start | bytes 1179652
  17.3 8.3 %collective-permute-start.8 = (f32[48,8,128]{2,1,0:T(8,128)S(1)}, f32[48,8,128]{2,1,0:T(8,128)S(1)}, u32[]{:S(2)}, u32[]{:S(2)}) collective-permute-start(f32[48,8,128]{2,1,0:T(8,128)S(1)} %pad_maximum_fusion.1), channel_id=1, source_target_pairs={{0,32},{32,0},{64,96},{96,64},{128,160},{160,128},{192,224},{224,1... | collective-permute-start | bytes 589832 | tf_op jit(solution)/shard_map/ppermute | solution.py:50
  26.3 8.0 %collective-permute-start.9 = (f32[24,8,256]{2,1,0:T(8,128)S(1)}, f32[24,8,256]{2,1,0:T(8,128)S(1)}, u32[]{:S(2)}, u32[]{:S(2)}) collective-permute-start(f32[24,8,256]{2,1,0:T(8,128)S(1)} %get-tuple-element.65), channel_id=1, source_target_pairs={{0,1},{1,0},{2,3},{3,2},{4,5},{5,4},{6,7},{7,6},{8,9},{9,8},{10,11... | collective-permute-start | bytes 589832 | tf_op jit(solution)/shard_map/ppermute | solution.py:36
  26.4 7.9 %collective-permute-start.10 = (f32[24,8,256]{2,1,0:T(8,128)S(1)}, f32[24,8,256]{2,1,0:T(8,128)S(1)}, u32[]{:S(2)}, u32[]{:S(2)}) collective-permute-start(f32[24,8,256]{2,1,0:T(8,128)S(1)} %get-tuple-element.66), channel_id=1, source_target_pairs={{0,8},{1,2},{2,1},{3,4},{4,3},{5,6},{6,5},{7,15},{8,0},{9,10},{10,... | collective-permute-start | bytes 589832 | tf_op jit(solution)/shard_map/ppermute | solution.py:46
  30.5 1.3 %collective-permute-start.11 = (f32[8,8,256]{2,1,0:T(8,128)S(1)}, f32[8,8,256]{2,1,0:T(8,128)S(1)}, u32[]{:S(2)}, u32[]{:S(2)}) collective-permute-start(f32[8,8,256]{2,1,0:T(8,128)S(1)} %get-tuple-element.67), channel_id=1, source_target_pairs={{0,8},{8,0},{16,24},{24,16},{1,9},{9,1},{17,25},{25,17},{2,10},{10... | collective-permute-start | bytes 196616 | tf_op jit(solution)/shard_map/ppermute | solution.py:36
  30.5 3.7 %collective-permute-start.12 = (f32[8,8,256]{2,1,0:T(8,128)S(1)}, f32[8,8,256]{2,1,0:T(8,128)S(1)}, u32[]{:S(2)}, u32[]{:S(2)}) collective-permute-start(f32[8,8,256]{2,1,0:T(8,128)S(1)} %get-tuple-element.68), channel_id=1, source_target_pairs={{0,24},{8,16},{16,8},{24,0},{1,25},{9,17},{17,9},{25,1},{2,26},{10... | collective-permute-start | bytes 196616 | tf_op jit(solution)/shard_map/ppermute | solution.py:36
  31.3 8.3 %collective-permute-start.17 = (f32[24,8,256]{2,1,0:T(8,128)S(1)}, f32[24,8,256]{2,1,0:T(8,128)S(1)}, u32[]{:S(2)}, u32[]{:S(2)}) collective-permute-start(f32[24,8,256]{2,1,0:T(8,128)S(1)} %get-tuple-element.81), channel_id=1, source_target_pairs={{0,1},{1,0},{2,3},{3,2},{4,5},{5,4},{6,7},{7,6},{8,9},{9,8},{10,11... | collective-permute-start | bytes 589832 | tf_op jit(solution)/shard_map/ppermute | solution.py:36
  31.8 8.5 %collective-permute-start.18 = (f32[24,8,256]{2,1,0:T(8,128)S(1)}, f32[24,8,256]{2,1,0:T(8,128)S(1)}, u32[]{:S(2)}, u32[]{:S(2)}) collective-permute-start(f32[24,8,256]{2,1,0:T(8,128)S(1)} %get-tuple-element.82), channel_id=1, source_target_pairs={{0,8},{1,2},{2,1},{3,4},{4,3},{5,6},{6,5},{7,15},{8,0},{9,10},{10,... | collective-permute-start | bytes 589832 | tf_op jit(solution)/shard_map/ppermute | solution.py:46
  36.2 7.3 %collective-permute-start.13 = (f32[24,8,256]{2,1,0:T(8,128)S(1)}, f32[24,8,256]{2,1,0:T(8,128)S(1)}, u32[]{:S(2)}, u32[]{:S(2)}) collective-permute-start(f32[24,8,256]{2,1,0:T(8,128)S(1)} %get-tuple-element.71), channel_id=1, source_target_pairs={{0,1},{1,0},{2,3},{3,2},{4,5},{5,4},{6,7},{7,6},{8,9},{9,8},{10,11... | collective-permute-start | bytes 589832 | tf_op jit(solution)/shard_map/ppermute | solution.py:36
  36.3 7.5 %collective-permute-start.14 = (f32[24,8,256]{2,1,0:T(8,128)S(1)}, f32[24,8,256]{2,1,0:T(8,128)S(1)}, u32[]{:S(2)}, u32[]{:S(2)}) collective-permute-start(f32[24,8,256]{2,1,0:T(8,128)S(1)} %get-tuple-element.72), channel_id=1, source_target_pairs={{0,8},{1,2},{2,1},{3,4},{4,3},{5,6},{6,5},{7,15},{8,0},{9,10},{10,... | collective-permute-start | bytes 589832 | tf_op jit(solution)/shard_map/ppermute | solution.py:46
  39.6 3.0 %collective-permute-start.15 = (f32[4,8,256]{2,1,0:T(8,128)S(1)}, f32[4,8,256]{2,1,0:T(8,128)S(1)}, u32[]{:S(2)}, u32[]{:S(2)}) collective-permute-start(f32[4,8,256]{2,1,0:T(8,128)S(1)} %get-tuple-element.73), channel_id=1, source_target_pairs={{0,8},{8,0},{16,24},{24,16},{1,9},{9,1},{17,25},{25,17},{2,10},{10... | collective-permute-start | bytes 98312 | tf_op jit(solution)/shard_map/ppermute | solution.py:36
  39.6 3.3 %collective-permute-start.16 = (f32[4,8,256]{2,1,0:T(8,128)S(1)}, f32[4,8,256]{2,1,0:T(8,128)S(1)}, u32[]{:S(2)}, u32[]{:S(2)}) collective-permute-start(f32[4,8,256]{2,1,0:T(8,128)S(1)} %get-tuple-element.74), channel_id=1, source_target_pairs={{0,24},{8,16},{16,8},{24,0},{1,25},{9,17},{17,9},{25,1},{2,26},{10... | collective-permute-start | bytes 98312 | tf_op jit(solution)/shard_map/ppermute | solution.py:36
  44.7 8.3 %collective-permute-start.19 = (f32[2,24,8,128]{3,2,1,0:T(8,128)S(1)}, f32[2,24,8,128]{3,2,1,0:T(8,128)S(1)}, u32[]{:S(2)}, u32[]{:S(2)}) collective-permute-start(f32[2,24,8,128]{3,2,1,0:T(8,128)S(1)} %get-tuple-element.88), channel_id=1, source_target_pairs={{0,128},{32,160},{64,192},{96,224},{128,0},{160,32},{192,64},{224,... | collective-permute-start | bytes 589832 | tf_op jit(solution)/shard_map/ppermute | solution.py:54
  45.8 8.3 %collective-permute-start.21 = (f32[2,24,8,128]{3,2,1,0:T(8,128)S(1)}, f32[2,24,8,128]{3,2,1,0:T(8,128)S(1)}, u32[]{:S(2)}, u32[]{:S(2)}) collective-permute-start(f32[2,24,8,128]{3,2,1,0:T(8,128)S(1)} %get-tuple-element.92), channel_id=1, source_target_pairs={{0,32},{32,0},{64,96},{96,64},{128,160},{160,128},{192,224},{224,1... | collective-permute-start | bytes 589832 | tf_op jit(solution)/shard_map/ppermute | solution.py:50
  53.1 6.2 %collective-permute-start.20 = (f32[24,8,128]{2,1,0:T(8,128)S(1)}, f32[24,8,128]{2,1,0:T(8,128)S(1)}, u32[]{:S(2)}, u32[]{:S(2)}) collective-permute-start(f32[24,8,128]{2,1,0:T(8,128)S(1)} %get-tuple-element.90), channel_id=1, source_target_pairs={{0,32},{32,0},{64,96},{96,64},{128,160},{160,128},{192,224},{224,1... | collective-permute-start | bytes 294920 | tf_op jit(solution)/shard_map/ppermute | solution.py:50
  54.1 5.1 %collective-permute-start.22 = (f32[24,8,128]{2,1,0:T(8,128)S(1)}, f32[24,8,128]{2,1,0:T(8,128)S(1)}, u32[]{:S(2)}, u32[]{:S(2)}) collective-permute-start(f32[24,8,128]{2,1,0:T(8,128)S(1)} %get-tuple-element.93), channel_id=1, source_target_pairs={{0,64},{32,96},{64,0},{96,32},{128,192},{160,224},{192,128},{224,1... | collective-permute-start | bytes 294920 | tf_op jit(solution)/shard_map/ppermute | solution.py:58
  55.2 5.8 %collective-permute-start.23 = (f32[24,8,128]{2,1,0:T(8,128)S(1)}, f32[24,8,128]{2,1,0:T(8,128)S(1)}, u32[]{:S(2)}, u32[]{:S(2)}) collective-permute-start(f32[24,8,128]{2,1,0:T(8,128)S(1)} %get-tuple-element.94), channel_id=1, source_target_pairs={{0,192},{32,224},{64,128},{96,160},{128,64},{160,96},{192,0},{224,... | collective-permute-start | bytes 294920 | tf_op jit(solution)/shard_map/ppermute | solution.py:58
